TPU v7x, 256 devices: a whole 4x4x8 slice. The times are simulated.
256 devices in a mesh: row: 8 (over y, z_lo), col: 32 (over z_hi, x, core).
Axes of the slice: x: 4, y: 4, z: 8 (z_hi: 4, z_lo: 2; z = z_hi * 2 + z_lo), core: 2. Of those that a mesh axis runs over, the one named last changes fastest.
Arguments:
- blocks: float32 [8192, 128, 128], P(('row', 'col')), may hold values from -0.21875 to 0.21875
- block_row: int32 [8192], P(('row', 'col')), may hold values from 0 to 511, as said below
- block_col: int32 [8192], P(('row', 'col')), may hold values from 0 to 511, as said below
- counts: int32 [256], P(('row', 'col')), may hold values from 1 to 32, as said below
- diagonal: float32 [65536], P(('row', 'col')), may hold values from 0.25 to 4
- vector: float32 [65536, 256], P(('row', 'col')), may hold values from -8 to 8
Outputs:
- next_basis: float32 [65536, 256], P(('row', 'col'))
- second_image: float32 [65536, 256], P(('row', 'col'))
- arnoldi_column: float32 [2, 256], replicated
Inputs may be any that keep to these rules, and one draw needn't show every extreme that they name: The slots of device d = r * 32 + c are rows d * 32 to (d + 1) * 32 - 1. Its slot d * 32 + k * 32 + o (k below 1) has block_row // 2 equal to r * 32 + o, and (block_col // 2) % 32 equals c. No pair (block_row, block_col) occurs twice among all slots. `block_col`: paired with block_row as stated there. Only the first counts[d] slots of device d hold blocks; later slots are ignored. Some device has exactly 32.
All inputs are finite; a program needn't handle non-finite values.
Results may differ from a plain program's by a relative error of at most 0.0001.
Values sent between devices are 32-bit elements; how exact they have to be, the bound alone decides.
No kernel may reach another device: no remote copies, remote signals or barrier semaphores. Data moves between devices by JAX's collectives and lax.ppermute only.
A program may use at most 64 MiB of HBM per device.

v0:
```python
import math

import jax
import jax.numpy as jnp
from jax import lax
from jax.sharding import PartitionSpec as P


def collect_tiles(products, local_col, live_slot, n_local):
    slot_count = products.shape[0]
    targets = jnp.arange(n_local, dtype=jnp.int32)
    selector = jnp.where(
        (local_col[:, None] == targets[None, :]) & live_slot[:, None], 1.0, 0.0
    ).astype(jnp.float32)
    return jnp.dot(
        selector.T,
        products.reshape(slot_count, -1),
        precision=lax.Precision.HIGHEST,
        preferred_element_type=jnp.float32,
    )


def local_terms(gathered, blocks, local_row, local_col, live_slot, n_local):
    tile_size = blocks.shape[1]
    rhs_count = gathered.shape[1]
    slot_count = blocks.shape[0]
    group_size = math.gcd(slot_count, 32)
    turn_count = slot_count // group_size
    stacked = gathered.reshape(gathered.shape[0] // tile_size, tile_size, rhs_count)

    def advance(turn_id, totals):
        picked = jnp.take(stacked, local_row, axis=0)
        products = jnp.einsum(
            "gab,gak->gbk",
            blocks,
            picked,
            precision=lax.Precision.HIGHEST,
            preferred_element_type=jnp.float32,
        )
        return totals + collect_tiles(products, local_col, live_slot, n_local)

    start_sum = jnp.zeros((n_local, tile_size * rhs_count), jnp.float32)
    return lax.fori_loop(0, turn_count, advance, start_sum)


def per_device(blocks, block_row, block_col, counts, diagonal, vector):
    n_rows = lax.axis_size("row")
    n_cols = lax.axis_size("col")
    tile_size = blocks.shape[1]
    rhs_count = vector.shape[1]
    per_piece = vector.shape[0] // tile_size
    total_rows = vector.shape[0] * n_rows * n_cols
    grid_row = lax.axis_index("row")
    piece_id = block_col // per_piece
    local_col = piece_id // n_cols * per_piece + block_col % per_piece
    live_slot = jnp.arange(blocks.shape[0], dtype=jnp.int32) < counts[0]
    n_local = n_rows * per_piece
    local_row = block_row - grid_row * (n_cols * per_piece)

    def partial_terms(source):
        gathered = lax.all_gather(source, "col", axis=0, tiled=True)
        return local_terms(gathered, blocks, local_row, local_col, live_slot, n_local)

    def apply_transpose(source):
        partial_sums = partial_terms(source).reshape(n_local * tile_size, rhs_count)
        reduced = lax.psum_scatter(partial_sums, "row", scatter_dimension=0, tiled=True)
        return diagonal[:, None] * source + reduced

    squares = lax.psum(jnp.sum(vector * vector, axis=0), ("row", "col"))
    magnitude = jnp.sqrt(squares / total_rows + 1e-06)
    unit_basis = vector / magnitude
    first_image = apply_transpose(unit_basis)
    projection = lax.psum(jnp.sum(first_image * unit_basis, axis=0), ("row", "col")) / total_rows
    remainder = first_image - projection * unit_basis
    remainder_power = lax.psum(jnp.sum(remainder * remainder, axis=0), ("row", "col")) / total_rows
    norm_new = jnp.sqrt(remainder_power + 1e-06)
    next_basis = remainder / norm_new
    second_image = apply_transpose(next_basis)
    return (next_basis, second_image, jnp.stack([projection, norm_new]))


def solution(mesh):
    return jax.shard_map(
        per_device,
        mesh=mesh,
        in_specs=(
            P(("row", "col"), None, None),
            P(("row", "col")),
            P(("row", "col")),
            P(("row", "col")),
            P(("row", "col")),
            P(("row", "col"), None),
        ),
        out_specs=(P(("row", "col"), None), P(("row", "col"), None), P()),
        check_vma=False,
    )
```

profile of v0, /device:TPU:1, one launch (start us, length us, event | category | flops | bytes accessed | tf_op | source)
XLA Modules:
  0.0 568.8 jit_solution(9993740631379046708)
XLA Ops:
  7.2 0.0 copy-start
  7.2 0.0 all-gather.3.cloned.1.call-start
  7.2 1.1 multiply_reduce_fusion.2
  8.4 81.4 %psum.21 = f32[256]{0:T(256)S(1)} all-reduce(f32[256]{0:T(256)S(1)} %multiply_reduce_fusion.2), channel_id=1, replica_groups=mesh['row'=8,'col'=32] {'row','col'}, use_global_device_ids=true, to_apply=%region_1.2 | all-reduce | flops 256 | bytes 2048 | tf_op jit(solution)/shard_map/psum | solution.py:69
  89.8 1.7 broadcast_divide_fusion.1
  91.5 0.0 all-gather.3.cloned.1.call-update
  91.5 0.0 reduce-scatter.3.cloned.1.call-start
  92.2 0.7 compare_and_fusion
  92.9 0.7 fusion.29
  93.6 69.8 %all-gather.3.cloned.1.call-done = f32[8192,256]{1,0:T(8,128)} async-done(((f32[256,256]{1,0:T(8,128)}), f32[8192,256]{1,0:T(8,128)}) %all-gather.3.cloned.1.call-update) | async-done | bytes 8388624 | tf_op jit(solution)/shard_map/all_gather | solution.py:61
  163.4 6.2 %gather_fusion = f32[32,128,256]{2,1,0:T(8,128)} fusion(f32[64,128,256]{2,1,0:T(8,128)} %bitcast.24, s32[1024]{0:T(1024)S(1)} %pad_clamp_fusion), kind=kCustom, calls=%fused_computation.clone | custom fusion | bytes 8388736 | tf_op jit(solution)/shard_map/while/body/eval_jaxpr/jit(_take)/gather | solution.py:32
  169.5 0.0 copy-done
  169.5 10.5 %fusion.4 = f32[32,128,256]{1,2,0:T(8,128)} fusion(f32[32,128,128]{2,1,0:T(8,128)S(1)} %copy-done, f32[32,128,256]{2,1,0:T(8,128)} %gather_fusion, pred[32]{0:T(512)(128)(4,1)S(1)} %get-tuple-element.32), kind=kOutput, calls=%fused_computation.6 | convolution fusion | flops 1611661312 | bytes 10485792 | tf_op jit(solution)/shard_map/while/body/eval_jaxpr/gab,gak->gbk/dot_general | solution.py:33
  180.1 5.4 copy.15
  185.5 5.0 fusion.16
  190.5 0.0 copy-start.1
  190.5 0.0 copy-start.3
  190.5 2.7 reshape.42
  193.2 0.0 reduce-scatter.3.cloned.1.call-update
  193.2 0.0 all-gather.5.cloned.1.call-start
  193.3 55.5 %reduce-scatter.3.cloned.1.call-done = f32[256,256]{1,0:T(8,128)} async-done(((f32[2048,256]{1,0:T(8,128)}), f32[256,256]{1,0:T(8,128)}) %reduce-scatter.3.cloned.1.call-update) | async-done | bytes 262160 | tf_op jit(solution)/shard_map/reduce_scatter | solution.py:66
  248.8 0.0 copy-done.1
  248.8 0.0 copy-done.3
  248.8 1.1 multiply_reduce_fusion.1
  249.9 76.0 %psum.22 = f32[256]{0:T(256)S(1)} all-reduce(f32[256]{0:T(256)S(1)} %multiply_reduce_fusion.1), channel_id=1, replica_groups=mesh['row'=8,'col'=32] {'row','col'}, use_global_device_ids=true, to_apply=%region_4.6 | all-reduce | flops 256 | bytes 2048 | tf_op jit(solution)/shard_map/psum | solution.py:73
  325.9 1.1 multiply_reduce_fusion
  326.9 73.5 %psum.23 = f32[256]{0:T(256)S(1)} all-reduce(f32[256]{0:T(256)S(1)} %multiply_reduce_fusion), channel_id=1, replica_groups=mesh['row'=8,'col'=32] {'row','col'}, use_global_device_ids=true, to_apply=%region_6.8 | all-reduce | flops 256 | bytes 2048 | tf_op jit(solution)/shard_map/psum | solution.py:75
  400.5 1.8 broadcast_divide_fusion
  402.2 0.0 all-gather.5.cloned.1.call-update
  402.3 0.2 reduce-scatter.5.cloned.1.call-start
  402.5 72.6 %all-gather.5.cloned.1.call-done = f32[8192,256]{1,0:T(8,128)} async-done(((f32[256,256]{1,0:T(8,128)}), f32[8192,256]{1,0:T(8,128)}) %all-gather.5.cloned.1.call-update) | async-done | bytes 8388624 | tf_op jit(solution)/shard_map/all_gather | solution.py:61
  475.1 6.2 %gather_fusion.1 = f32[32,128,256]{2,1,0:T(8,128)} fusion(f32[64,128,256]{2,1,0:T(8,128)} %bitcast.25, s32[1024]{0:T(1024)S(1)} %pad_clamp_fusion), kind=kCustom, calls=%fused_computation.1.clone | custom fusion | bytes 8388736 | tf_op jit(solution)/shard_map/while/body/eval_jaxpr/jit(_take)/gather | solution.py:32
  481.2 10.5 %fusion.7 = f32[32,128,256]{1,2,0:T(8,128)} fusion(f32[32,128,128]{2,1,0:T(8,128)S(1)} %copy-done, f32[32,128,256]{2,1,0:T(8,128)} %gather_fusion.1, pred[32]{0:T(512)(128)(4,1)S(1)} %get-tuple-element.32), kind=kOutput, calls=%fused_computation.7 | convolution fusion | flops 1611661312 | bytes 10485792 | tf_op jit(solution)/shard_map/while/body/eval_jaxpr/gab,gak->gbk/dot_general | solution.py:33
  491.7 5.4 copy.16
  497.2 5.0 fusion.14
  502.2 0.0 copy-start.2
  502.2 2.7 reshape.45
  504.9 0.0 reduce-scatter.5.cloned.1.call-update
  504.9 0.6 pad_maximum_fusion
  505.5 55.0 %reduce-scatter.5.cloned.1.call-done = f32[256,256]{1,0:T(8,128)} async-done(((f32[2048,256]{1,0:T(8,128)}), f32[256,256]{1,0:T(8,128)}) %reduce-scatter.5.cloned.1.call-update) | async-done | bytes 262160 | tf_op jit(solution)/shard_map/reduce_scatter | solution.py:66
  560.5 0.0 copy-done.2
  560.5 1.8 multiply_add_fusion
  (5 shorter events, 0.0 us)
Async XLA Ops:
  7.2 162.4 %copy-start = (f32[32,128,128]{2,1,0:T(8,128)S(1)}, f32[32,128,128]{2,1,0:T(8,128)}, u32[]{:S(2)}) copy-start(f32[32,128,128]{2,1,0:T(8,128)} %param.8) | copy-start | bytes 6291460
  7.2 156.2 %all-gather.3.cloned.1.call-start = ((), (), s32[]{:S(2)}) async-start(), calls=%async_computation.2 | async-start | bytes 8650752 | tf_op jit(solution)/shard_map/all_gather | solution.py:61
  91.5 157.3 %reduce-scatter.3.cloned.1.call-start = ((), (), s32[]{:S(2)}) async-start(), calls=%async_computation.3 | async-start | bytes 2359296 | tf_op jit(solution)/shard_map/reduce_scatter | solution.py:66
  190.5 58.3 %copy-start.1 = (f32[256,256]{1,0:T(8,128)S(1)}, f32[256,256]{1,0:T(8,128)}, u32[]{:S(2)}) copy-start(f32[256,256]{1,0:T(8,128)} %param.13) | copy-start | bytes 786436
  190.5 58.3 %copy-start.3 = (f32[256]{0:T(256)S(1)}, f32[256]{0:T(256)}, u32[]{:S(2)}) copy-start(f32[256]{0:T(256)} %param.12) | copy-start | bytes 3076
  193.2 281.8 %all-gather.5.cloned.1.call-start = ((), (), s32[]{:S(2)}) async-start(), calls=%async_computation.4 | async-start | bytes 8650752 | tf_op jit(solution)/shard_map/all_gather | solution.py:61
  402.3 158.2 %reduce-scatter.5.cloned.1.call-start = ((), (), s32[]{:S(2)}) async-start(), calls=%async_computation.5 | async-start | bytes 2359296 | tf_op jit(solution)/shard_map/reduce_scatter | solution.py:66
  502.2 58.3 %copy-start.2 = (f32[256,256]{1,0:T(8,128)S(1)}, f32[256,256]{1,0:T(8,128)}, u32[]{:S(2)}) copy-start(f32[256,256]{1,0:T(8,128)} %broadcast_divide_fusion) | copy-start | bytes 786436
Sparse Core Ops, SparseCore 0:
  91.6 71.7 all-gather.2
  193.4 55.4 reduce-scatter.2
  402.4 72.6 all-gather.4
  505.0 55.4 reduce-scatter.4
where the time goes:
time: 570 us; the launch traced here: 569 us
  waiting for transfers between devices  253 us (44%)
  blocking collectives  231 us (41%)
  matrix products  31 us (5%)
  local copies, waits for them, and re-layouts  28.7 us (5%)
  between operations  14.4 us (3%)
  other arithmetic  10.4 us (2%)
    all_gather x2, waiting for transfers between devices, partial_terms(): gathered = lax.all_gather(source, 'col', axis=0, tiled=True)  142 us
    reduce_scatter x2, waiting for transfers between devices, apply_transpose(): lax.psum_scatter(partial_sums, 'row', scatter_dimension=0, tiled=True)  111 us
    psum x1, blocking collectives, per_device(): squares = lax.psum(jnp.sum(vector * vector, axis=0), ('row', 'col'))  81.4 us
    psum x1, blocking collectives, per_device(): lax.psum(jnp.sum(first_image * unit_basis, axis=0), ('row', 'col'))  76 us
    psum x1, blocking collectives, per_device(): lax.psum(jnp.sum(remainder * remainder, axis=0), ('row', 'col'))  73.5 us
    dot_general x2, matrix products, advance(): jnp.einsum('gab,gak->gbk', blocks, picked, precision=lax.Precision.HIGHES...  21 us
    gather x2, local copies, waits for them, and re-layouts, advance(): picked = jnp.take(stacked, local_row, axis=0)  12.3 us
  transfers between devices with their start and end apart: 4, of which 4 were waited for; matrix products, arithmetic and copies ran while one was open for 0% of the time, Pallas kernels for 0%

commit v1 on v0

v1 whole, which is shorter than its diff:
```python
import functools

import jax
import jax.numpy as jnp
from jax import lax
from jax.experimental import pallas as pl
from jax.experimental.pallas import tpu as pltpu
from jax.sharding import PartitionSpec as P

TILE = 128
HALF = 128
STAT = 8
LIMIT = 48 * 1024 * 1024
OFFSETS = (0, 3, 1, 2)


def col_index(z, x, core):
    return (z % 4) * 8 + (x % 4) * 2 + core


def col_pairs(dz, dx):
    return [
        (col_index(z, x, k), col_index(z + dz, x + dx, k))
        for z in range(4)
        for x in range(4)
        for k in range(2)
    ]


def smem():
    return pl.BlockSpec(memory_space=pltpu.SMEM)


def vmem():
    return pl.BlockSpec(memory_space=pltpu.VMEM)


def params():
    return pltpu.CompilerParams(vmem_limit_bytes=LIMIT)


def split_blocks_kernel(counts, blocks, out):
    base = pl.program_id(0) * blocks.shape[0]
    for i in range(blocks.shape[0]):
        block = jnp.where(base + i < counts[0], blocks[i], 0.0).T
        high = block.astype(jnp.bfloat16)
        low = (block - high.astype(jnp.float32)).astype(jnp.bfloat16)
        out[i, :, :TILE] = high
        out[i, :, TILE:] = low


def split_blocks(counts, blocks):
    n, step = blocks.shape[0], 8
    return pl.pallas_call(
        split_blocks_kernel,
        grid=(n // step,),
        out_shape=jax.ShapeDtypeStruct((n, TILE, 2 * TILE), jnp.bfloat16),
        in_specs=[smem(), pl.BlockSpec((step, TILE, TILE), lambda i: (i, 0, 0))],
        out_specs=pl.BlockSpec((step, TILE, 2 * TILE), lambda i: (i, 0, 0)),
        compiler_params=params(),
        name="split_blocks",
    )(counts, blocks)


def pieces_of(near, left, right, far_top, far_bottom):
    listed = []
    for dx, ref in ((0, near), (3, left), (1, right)):
        listed += [(dx, dz, ref, i) for i, dz in enumerate(OFFSETS)]
    listed += [(2, dz, far_top, i) for i, dz in enumerate(OFFSETS[:2])]
    listed += [(2, dz, far_bottom, i) for i, dz in enumerate(OFFSETS[2:])]
    return listed


def slot_of(place, dx, dz, core):
    return ((place[0] + dz) & 3) * 8 + ((place[1] + dx) & 3) * 2 + core


def pick_kernel(place, rows, near, left, right, far_top, far_bottom, out):
    for n, (dx, dz, ref, i) in enumerate(pieces_of(near, left, right, far_top, far_bottom)):
        slot = slot_of(place, dx, dz, place[2])
        start = pl.multiple_of((rows[slot] & 1) * TILE, TILE)
        out[n, :TILE] = ref[i, pl.ds(start, TILE)]
        if out.shape[1] > TILE:
            out[n, TILE:] = ref[i, 2 * TILE :]


def pick_for_partner(place, partner_rows, gathered):
    extra = gathered[0].shape[1] - 2 * TILE
    return pl.pallas_call(
        pick_kernel,
        out_shape=jax.ShapeDtypeStruct((16, TILE + extra, HALF), jnp.float32),
        in_specs=[smem(), smem()] + [vmem()] * 5,
        out_specs=vmem(),
        compiler_params=params(),
        name="pick_for_partner",
    )(place, partner_rows, *gathered)


def merge(stats):
    squares, inner, rest = stats
    ratio = jnp.where(squares > 0, inner / jnp.where(squares > 0, squares, 1.0), 0.0)
    total, inner_total = jnp.sum(squares, axis=0), jnp.sum(inner, axis=0)
    safe = jnp.where(total > 0, total, 1.0)
    mean_ratio = jnp.where(total > 0, inner_total / safe, 0.0)
    away = ratio - mean_ratio[None]
    return total, inner_total, jnp.sum(rest + squares * away * away, axis=0), mean_ratio


def multiply_kernel(place, rows, cols, split, near, left, right, far_top, far_bottom, other, out, *stats):
    out[...] = jnp.zeros_like(out)
    with_stats = out.shape[1] > 2 * TILE
    core = place[2]

    def add(slot, source):
        high = source.astype(jnp.bfloat16)
        low = (source - high.astype(jnp.float32)).astype(jnp.bfloat16)
        row = jnp.concatenate([high, low], axis=1)
        wide = jnp.dot(
            split[slot],
            jnp.concatenate([row, row], axis=0),
            preferred_element_type=jnp.float32,
        )
        target = cols[slot]
        owner = lax.shift_right_logical(target, 6)
        start = pl.multiple_of((target & 1) * TILE, TILE)
        out[owner, pl.ds(start, TILE)] += wide[:, :HALF] + wide[:, HALF:]

    for n, (dx, dz, ref, i) in enumerate(pieces_of(near, left, right, far_top, far_bottom)):
        slot = slot_of(place, dx, dz, core)
        start = pl.multiple_of((rows[slot] & 1) * TILE, TILE)
        add(slot, ref[i, pl.ds(start, TILE)])
        slot_other = slot_of(place, dx, dz, 1 - core)
        add(slot_other, other[n, :TILE])
        if with_stats:
            stats[0][slot] = ref[i, 2 * TILE :]
            stats[0][slot_other] = other[n, TILE:]
    if with_stats:
        total, inner, rest, _ = merge([stats[0][:, k : k + 1, :] for k in range(3)])
        joined = jnp.concatenate([total, inner, rest, jnp.zeros((STAT - 3, HALF), jnp.float32)], axis=0)
        for owner in range(out.shape[0]):
            out[owner, 2 * TILE :] = joined


def multiply(place, rows, cols, split, gathered, other):
    height = gathered[0].shape[1]
    return pl.pallas_call(
        multiply_kernel,
        out_shape=jax.ShapeDtypeStruct((8, height, HALF), jnp.float32),
        in_specs=[smem()] * 3 + [vmem()] * 7,
        out_specs=vmem(),
        scratch_shapes=[pltpu.VMEM((32, STAT, HALF), jnp.float32)] if height > 2 * TILE else [],
        compiler_params=params(),
        name="multiply",
    )(place, rows, cols, split, *gathered, other)


def sum_terms(terms, diagonal, source):
    total = terms[0, : 2 * TILE]
    for k in range(1, terms.shape[0]):
        total = total + terms[k, : 2 * TILE]
    return diagonal[...] * source + total


def first_image_kernel(terms, diagonal, vector, out):
    v = vector[...]
    w = sum_terms(terms, diagonal, v)
    out[: 2 * TILE] = w
    squares = jnp.sum(v * v, axis=0, keepdims=True)
    inner = jnp.sum(w * v, axis=0, keepdims=True)
    ratio = jnp.where(squares > 0, inner / jnp.where(squares > 0, squares, 1.0), 0.0)
    away = w - ratio * v
    rest = jnp.sum(away * away, axis=0, keepdims=True)
    out[2 * TILE :] = jnp.concatenate(
        [squares, inner, rest, jnp.zeros((STAT - 3, HALF), jnp.float32)], axis=0
    )


def first_image(terms, diagonal, vector):
    return pl.pallas_call(
        first_image_kernel,
        out_shape=jax.ShapeDtypeStruct((2 * TILE + STAT, HALF), jnp.float32),
        in_specs=[vmem()] * 3,
        out_specs=vmem(),
        compiler_params=params(),
        name="first_image",
    )(terms, diagonal, vector)


def finish_kernel(count, diagonal, *refs):
    (terms_a, image_a, vector_a, terms_b, image_b, vector_b, basis, second, column) = refs
    for half, (terms, image, vector) in enumerate(
        ((terms_a, image_a, vector_a), (terms_b, image_b, vector_b))
    ):
        span = slice(half * HALF, (half + 1) * HALF)
        stats = [terms[:, 2 * TILE + k : 2 * TILE + k + 1, :] for k in range(3)]
        squares, inner, rest, ratio = merge(stats)
        mean = squares / count + 1e-06
        magnitude = jnp.sqrt(mean)
        projection = inner / count / mean
        gap = projection - ratio
        left_over = rest + squares * gap * gap
        norm = jnp.sqrt(left_over / count / mean + 1e-06)
        column[0:1, span] = projection
        column[1:2, span] = norm
        w = image[: 2 * TILE]
        scale = 1.0 / (magnitude * norm)
        basis[:, span] = (w - projection * vector[...]) * scale
        second[:, span] = (sum_terms(terms, diagonal, w) - projection * w) * scale


def finish(count, diagonal, halves):
    flat = [part for half in halves for part in half]
    return pl.pallas_call(
        functools.partial(finish_kernel, count),
        out_shape=(
            jax.ShapeDtypeStruct((2 * TILE, 2 * HALF), jnp.float32),
            jax.ShapeDtypeStruct((2 * TILE, 2 * HALF), jnp.float32),
            jax.ShapeDtypeStruct((2, 2 * HALF), jnp.float32),
        ),
        in_specs=[vmem()] * 7,
        out_specs=(vmem(),) * 3,
        compiler_params=params(),
        name="finish",
    )(diagonal, *flat)


def ring_gather(own, pairs):
    send = lambda part, step: lax.ppermute(part, "col", pairs(step))
    n = own.shape[0]
    back, ahead = send(own, 1), send(own, 3)
    if n == 1:
        cut = TILE
        far = jnp.concatenate(
            [send(back[:, :cut], 1), send(ahead[:, cut:], 3)], axis=1
        )
        return own, back, ahead, far
    return own, back, ahead, send(back[: n // 2], 1), send(ahead[n // 2 :], 3)


def gather_z(own):
    return jnp.concatenate(ring_gather(own[None], lambda step: col_pairs(step, 0)), axis=0)


def gather_x(stack):
    return ring_gather(stack, lambda step: col_pairs(0, step))


def swap_cores(part):
    return lax.ppermute(part, "col", [(i, i ^ 1) for i in range(32)])


def per_device(blocks, block_row, block_col, counts, diagonal, vector):
    count = vector.shape[0] * lax.axis_size("row") * lax.axis_size("col")
    index = lax.axis_index("col")
    place = jnp.stack([index // 8, index // 2 % 4, index % 2]).astype(jnp.int32)
    partner_rows = swap_cores(block_row)
    vectors = [vector[:, :HALF], vector[:, HALF:]]
    diagonal = jnp.broadcast_to(diagonal[:, None], (2 * TILE, HALF))

    def product(sources):
        stacks = [gather_z(source) for source in sources]
        gathered = [gather_x(stack) for stack in stacks]
        terms = []
        for each in gathered:
            other = swap_cores(pick_for_partner(place, partner_rows, each))
            partial = multiply(place, block_row, block_col, split, each, other)
            terms.append(lax.all_to_all(partial, "row", 0, 0, tiled=True))
        return terms

    split = split_blocks(counts, blocks)
    terms = product(vectors)
    images = [first_image(t, diagonal, v) for t, v in zip(terms, vectors)]
    terms = product(images)
    return finish(count, diagonal, list(zip(terms, images, vectors)))


def solution(mesh):
    return jax.shard_map(
        per_device,
        mesh=mesh,
        in_specs=(
            P(("row", "col"), None, None),
            P(("row", "col")),
            P(("row", "col")),
            P(("row", "col")),
            P(("row", "col")),
            P(("row", "col"), None),
        ),
        out_specs=(P(("row", "col"), None), P(("row", "col"), None), P()),
        check_vma=False,
    )
```

time: 570 us -> 223 us (0.39)
  blocking collectives: 231 us -> 22.6 us
  waiting for transfers between devices: 253 us -> 81.5 us
  starting transfers between devices: 0.34 us -> 87.9 us
  matrix products: 31 us -> 0 us
  local copies, waits for them, and re-layouts: 28.7 us -> 5.62 us
  Pallas kernels: 0 us -> 20.5 us
  between operations: 14.4 us -> 1.68 us
  other arithmetic: 10.4 us -> 1.13 us
    psum x3 -> x0, blocking collectives: 231 us -> none  [the longest x1 81.4 us: per_device(): squares = lax.psum(jnp.sum(vector * vector, axis=0), ('row', 'col'))]
    all_gather x2 -> x0, waiting for transfers between devices: 142 us -> none  [partial_terms(): gathered = lax.all_gather(source, 'col', axis=0, tiled=True)]
    reduce_scatter x2 -> x0, waiting for transfers between devices: 111 us -> none  [apply_transpose(): lax.psum_scatter(partial_sums, 'row', scatter_dimension=0, tiled=True)]
    ppermute x0 -> x37, waiting for transfers between devices: none -> 81.5 us  [the longest x32 78.4 us: ring_gather(): send = lambda part, step: lax.ppermute(part, 'col', pairs(step))]
    ppermute x0 -> x37, starting transfers between devices: none -> 71.7 us  [the longest x32 54.5 us: ring_gather(): send = lambda part, step: lax.ppermute(part, 'col', pairs(step))]
    dot_general x4 -> x0, matrix products: 31 us -> none  [the longest x2 21 us: advance(): jnp.einsum('gab,gak->gbk', blocks, picked, precision=lax.Precision.HIGHES...]
    all_to_all x0 -> x1, blocking collectives: none -> 22.6 us  [product(): terms.append(lax.all_to_all(partial, 'row', 0, 0, tiled=True))]
    pallas_call x0 -> x12, Pallas kernels: none -> 20.5 us  [the longest x4 13.3 us: multiply(): pl.pallas_call(multiply_kernel, out_shape=jax.ShapeDtypeStruct((8, height...]
  transfers between devices with their start and end apart: 4 -> 40, of which waited for: 4 -> 17; matrix products, arithmetic and copies ran while one was open for 0% -> 1% of each run, Pallas kernels for 0% -> 9%
where the time goes in v1:
time: 223 us; the launch traced here: 221 us
  starting transfers between devices  87.9 us (39%)
  waiting for transfers between devices  81.5 us (37%)
  blocking collectives  22.6 us (10%)
  Pallas kernels  20.5 us (9%)
  local copies, waits for them, and re-layouts  5.62 us (3%)
    ppermute x32, waiting for transfers between devices, ring_gather(): send = lambda part, step: lax.ppermute(part, 'col', pairs(step))  78.4 us
    ppermute x32, starting transfers between devices, ring_gather(): send = lambda part, step: lax.ppermute(part, 'col', pairs(step))  54.5 us
    all_to_all x1, blocking collectives, product(): terms.append(lax.all_to_all(partial, 'row', 0, 0, tiled=True))  22.6 us
    ppermute x5, starting transfers between devices, swap_cores(): return lax.ppermute(part, 'col', [(i, i ^ 1) for i in range(32)])  17.2 us
    all_to_all x3, starting transfers between devices, product(): terms.append(lax.all_to_all(partial, 'row', 0, 0, tiled=True))  16.2 us
    pallas_call x4, Pallas kernels, multiply(): pl.pallas_call(multiply_kernel, out_shape=jax.ShapeDtypeStruct((8, height...  13.3 us
    pallas_call x4, Pallas kernels, pick_for_partner(): pl.pallas_call(pick_kernel, out_shape=jax.ShapeDtypeStruct((16, TILE + ex...  4.98 us
  transfers between devices with their start and end apart: 40, of which 17 were waited for; matrix products, arithmetic and copies ran while one was open for 1% of the time, Pallas kernels for 9%

profile of v1, /device:TPU:1, one launch (start us, length us, event | category | flops | bytes accessed | tf_op | source)
XLA Modules:
  0.0 220.9 jit_solution(2112340427563352785)
XLA Ops:
  1.7 3.9 %collective-permute-start.19 = (f32[1,256,128]{2,1,0:T(8,128)S(1)}, f32[1,256,128]{2,1,0:T(8,128)S(1)}, u32[]{:S(2)}, u32[]{:S(2)}) collective-permute-start(f32[1,256,128]{2,1,0:T(8,128)S(1)} %get-tuple-element.5), channel_id=1, source_target_pairs={{0,8},{1,9},{2,10},{3,11},{4,12},{5,13},{6,14},{7,15},{8,16},{9,17... | collective-permute-start | bytes 393224 | tf_op jit(solution)/shard_map/ppermute | solution.py:228
  5.6 3.1 %collective-permute-start.20 = (f32[1,256,128]{2,1,0:T(8,128)S(1)}, f32[1,256,128]{2,1,0:T(8,128)S(1)}, u32[]{:S(2)}, u32[]{:S(2)}) collective-permute-start(f32[1,256,128]{2,1,0:T(8,128)S(1)} %get-tuple-element.5), channel_id=1, source_target_pairs={{0,24},{1,25},{2,26},{3,27},{4,28},{5,29},{6,30},{7,31},{8,0},{9,1... | collective-permute-start | bytes 393224 | tf_op jit(solution)/shard_map/ppermute | solution.py:228
  8.7 3.7 %collective-permute-done.19 = f32[1,256,128]{2,1,0:T(8,128)S(1)} collective-permute-done((f32[1,256,128]{2,1,0:T(8,128)S(1)}, f32[1,256,128]{2,1,0:T(8,128)S(1)}, u32[]{:S(2)}, u32[]{:S(2)}) %collective-permute-start.19) | collective-permute-done | bytes 131104 | tf_op jit(solution)/shard_map/ppermute | solution.py:228
  12.4 2.8 %collective-permute-start.21 = (f32[1,128,128]{2,1,0:T(8,128)S(1)}, f32[1,128,128]{2,1,0:T(8,128)S(1)}, u32[]{:S(2)}, u32[]{:S(2)}) collective-permute-start(f32[1,128,128]{2,1,0:T(8,128)S(1)} %slice.80), channel_id=1, source_target_pairs={{0,8},{1,9},{2,10},{3,11},{4,12},{5,13},{6,14},{7,15},{8,16},{9,17... | collective-permute-start | bytes 196616 | tf_op jit(solution)/shard_map/ppermute | solution.py:228
  16.1 2.4 %collective-permute-start.22 = (f32[1,128,128]{2,1,0:T(8,128)S(1)}, f32[1,128,128]{2,1,0:T(8,128)S(1)}, u32[]{:S(2)}, u32[]{:S(2)}) collective-permute-start(f32[1,128,128]{2,1,0:T(8,128)S(1)} %slice.81), channel_id=1, source_target_pairs={{0,24},{1,25},{2,26},{3,27},{4,28},{5,29},{6,30},{7,31},{8,0},{9,1... | collective-permute-start | bytes 196616 | tf_op jit(solution)/shard_map/ppermute | solution.py:228
  18.4 3.0 %collective-permute-done.22 = f32[1,128,128]{2,1,0:T(8,128)S(1)} collective-permute-done((f32[1,128,128]{2,1,0:T(8,128)S(1)}, f32[1,128,128]{2,1,0:T(8,128)S(1)}, u32[]{:S(2)}, u32[]{:S(2)}) %collective-permute-start.22) | collective-permute-done | bytes 65568 | tf_op jit(solution)/shard_map/ppermute | solution.py:228
  22.8 1.5 collective-permute-start.24
  24.3 9.5 %collective-permute-done.23.left = f32[4,256,128]{2,1,0:T(8,128)S(1)} collective-permute-done((f32[4,256,128]{2,1,0:T(8,128)S(1)}, f32[4,256,128]{2,1,0:T(8,128)S(1)}, u32[]{:S(2)}, u32[]{:S(2)}) %collective-permute-start.23) | collective-permute-done | bytes 524320 | tf_op jit(solution)/shard_map/ppermute | solution.py:228
  33.9 2.7 %collective-permute-start.26 = (f32[2,256,128]{2,1,0:T(8,128)S(1)}, f32[2,256,128]{2,1,0:T(8,128)S(1)}, u32[]{:S(2)}, u32[]{:S(2)}) collective-permute-start(f32[2,256,128]{2,1,0:T(8,128)S(1)} %slice.83), channel_id=1, source_target_pairs={{0,6},{1,7},{2,0},{3,1},{4,2},{5,3},{6,4},{7,5},{8,14},{9,15},{10,... | collective-permute-start | bytes 786440 | tf_op jit(solution)/shard_map/ppermute | solution.py:228
  36.6 3.9 %collective-permute-start.8 = (s32[32]{0:T(128)S(1)}, s32[32]{0:T(128)S(1)}, u32[]{:S(2)}, u32[]{:S(2)}) collective-permute-start(s32[32]{0:T(128)S(1)} %copy-done.16), channel_id=1, source_target_pairs={{0,1},{1,0},{2,3},{3,2},{4,5},{5,4},{6,7},{7,6},{8,9},{9,8},{10,11... | collective-permute-start | bytes 392 | tf_op jit(solution)/shard_map/ppermute | solution.py:249
  42.0 3.5 %collective-permute-start.27 = (f32[16,128,128]{2,1,0:T(8,128)S(1)}, f32[16,128,128]{2,1,0:T(8,128)S(1)}, u32[]{:S(2)}, u32[]{:S(2)}) collective-permute-start(f32[16,128,128]{2,1,0:T(8,128)S(1)} %pick_for_partner.6), channel_id=1, source_target_pairs={{0,1},{1,0},{2,3},{3,2},{4,5},{5,4},{6,7},{7,6},{8,9},{9,8},{10,11... | collective-permute-start | bytes 3145736 | tf_op jit(solution)/shard_map/ppermute | solution.py:249
  45.5 3.5 %collective-permute-start = (f32[1,256,128]{2,1,0:T(8,128)S(1)}, f32[1,256,128]{2,1,0:T(8,128)S(1)}, u32[]{:S(2)}, u32[]{:S(2)}) collective-permute-start(f32[1,256,128]{2,1,0:T(8,128)S(1)} %get-tuple-element.4), channel_id=1, source_target_pairs={{0,8},{1,9},{2,10},{3,11},{4,12},{5,13},{6,14},{7,15},{8,16},{9,17... | collective-permute-start | bytes 393224 | tf_op jit(solution)/shard_map/ppermute | solution.py:228
  49.1 6.3 %collective-permute-done = f32[1,256,128]{2,1,0:T(8,128)S(1)} collective-permute-done((f32[1,256,128]{2,1,0:T(8,128)S(1)}, f32[1,256,128]{2,1,0:T(8,128)S(1)}, u32[]{:S(2)}, u32[]{:S(2)}) %collective-permute-start) | collective-permute-done | bytes 131104 | tf_op jit(solution)/shard_map/ppermute | solution.py:228
  55.4 1.5 collective-permute-start.2
  57.1 2.3 %collective-permute-start.3 = (f32[1,128,128]{2,1,0:T(8,128)S(1)}, f32[1,128,128]{2,1,0:T(8,128)S(1)}, u32[]{:S(2)}, u32[]{:S(2)}) collective-permute-start(f32[1,128,128]{2,1,0:T(8,128)S(1)} %slice.73), channel_id=1, source_target_pairs={{0,24},{1,25},{2,26},{3,27},{4,28},{5,29},{6,30},{7,31},{8,0},{9,1... | collective-permute-start | bytes 196616 | tf_op jit(solution)/shard_map/ppermute | solution.py:228
  60.9 1.3 copy-done
  62.3 3.4 %multiply.6 = f32[8,256,128]{2,1,0:T(8,128)} custom-call(s32[3]{0:T(128)S(1)} %pad_add_fusion.place, s32[32]{0:T(128)S(1)} %copy-done.16, s32[32]{0:T(128)S(1)} %copy-done.17, bf16[32,128,256]{2,1,0:T(8,128)(2,1)} %copy-done, f32[4,256,128]{2,1,0:T(8,128)S(1)} %maximum_maximum_fusion.3.near, f32[4,256,128]{2,1,0:T(8,128)S(1)} %collective-permute-done.23.left, ...), custom_call_target="tpu_custom_call" | custom-call | tf_op jit(solution)/shard_map/multiply/pallas_call | solution.py:146
  65.7 4.2 %all-to-all-start.2 = ((f32[8,256,128]{2,1,0:T(8,128)}), f32[8,256,128]{2,1,0:T(8,128)S(1)}, u32[]{:S(2)}, u32[]{:S(2)}) async-start(f32[8,256,128]{2,1,0:T(8,128)} %multiply.6), calls=%async_computation.2 | async-start | bytes 2097152 | tf_op jit(solution)/shard_map/all_to_all | solution.py:267
  70.8 2.5 %collective-permute-start.5 = (f32[4,256,128]{2,1,0:T(8,128)S(1)}, f32[4,256,128]{2,1,0:T(8,128)S(1)}, u32[]{:S(2)}, u32[]{:S(2)}) collective-permute-start(f32[4,256,128]{2,1,0:T(8,128)S(1)} %maximum_maximum_fusion.2.near), channel_id=1, source_target_pairs={{0,6},{1,7},{2,0},{3,1},{4,2},{5,3},{6,4},{7,5},{8,14},{9,15},{10,... | collective-permute-start | bytes 1572872 | tf_op jit(solution)/shard_map/ppermute | solution.py:228
  73.3 10.7 %collective-permute-done.4.left = f32[4,256,128]{2,1,0:T(8,128)S(1)} collective-permute-done((f32[4,256,128]{2,1,0:T(8,128)S(1)}, f32[4,256,128]{2,1,0:T(8,128)S(1)}, u32[]{:S(2)}, u32[]{:S(2)}) %collective-permute-start.4) | collective-permute-done | bytes 524320 | tf_op jit(solution)/shard_map/ppermute | solution.py:228
  84.2 2.7 %collective-permute-start.7 = (f32[2,256,128]{2,1,0:T(8,128)S(1)}, f32[2,256,128]{2,1,0:T(8,128)S(1)}, u32[]{:S(2)}, u32[]{:S(2)}) collective-permute-start(f32[2,256,128]{2,1,0:T(8,128)S(1)} %slice.75), channel_id=1, source_target_pairs={{0,6},{1,7},{2,0},{3,1},{4,2},{5,3},{6,4},{7,5},{8,14},{9,15},{10,... | collective-permute-start | bytes 786440 | tf_op jit(solution)/shard_map/ppermute | solution.py:228
  86.9 4.1 %collective-permute-done.6.far_top = f32[2,256,128]{2,1,0:T(8,128)S(1)} collective-permute-done((f32[2,256,128]{2,1,0:T(8,128)S(1)}, f32[2,256,128]{2,1,0:T(8,128)S(1)}, u32[]{:S(2)}, u32[]{:S(2)}) %collective-permute-start.6) | collective-permute-done | bytes 262176 | tf_op jit(solution)/shard_map/ppermute | solution.py:228
  91.1 1.6 pick_for_partner.4
  92.7 3.0 %collective-permute-start.9 = (f32[16,128,128]{2,1,0:T(8,128)}, f32[16,128,128]{2,1,0:T(8,128)}, u32[]{:S(2)}, u32[]{:S(2)}) collective-permute-start(f32[16,128,128]{2,1,0:T(8,128)} %pick_for_partner.4), channel_id=1, source_target_pairs={{0,1},{1,0},{2,3},{3,2},{4,5},{5,4},{6,7},{7,6},{8,9},{9,8},{10,11... | collective-permute-start | bytes 3145736 | tf_op jit(solution)/shard_map/ppermute | solution.py:249
  96.0 2.4 %collective-permute-start.28 = (f32[1,264,128]{2,1,0:T(8,128)S(1)}, f32[1,264,128]{2,1,0:T(8,128)}, u32[]{:S(2)}, u32[]{:S(2)}) collective-permute-start(f32[1,264,128]{2,1,0:T(8,128)S(1)} %bitcast.10), channel_id=1, source_target_pairs={{0,8},{1,9},{2,10},{3,11},{4,12},{5,13},{6,14},{7,15},{8,16},{9,17... | collective-permute-start | bytes 405512 | tf_op jit(solution)/shard_map/ppermute | solution.py:228
  98.4 3.7 %multiply.4 = f32[8,256,128]{2,1,0:T(8,128)} custom-call(s32[3]{0:T(128)S(1)} %pad_add_fusion.place, s32[32]{0:T(128)S(1)} %copy-done.16, s32[32]{0:T(128)S(1)} %copy-done.17, bf16[32,128,256]{2,1,0:T(8,128)(2,1)} %copy-done, f32[4,256,128]{2,1,0:T(8,128)S(1)} %maximum_maximum_fusion.2.near, f32[4,256,128]{2,1,0:T(8,128)S(1)} %collective-permute-done.4.left, ...), custom_call_target="tpu_custom_call" | custom-call | tf_op jit(solution)/shard_map/multiply/pallas_call | solution.py:146
  102.1 4.9 %all-to-all-start = ((f32[8,256,128]{2,1,0:T(8,128)}), f32[8,256,128]{2,1,0:T(8,128)S(1)}, u32[]{:S(2)}, u32[]{:S(2)}) async-start(f32[8,256,128]{2,1,0:T(8,128)} %multiply.4), calls=%async_computation | async-start | bytes 2097152 | tf_op jit(solution)/shard_map/all_to_all | solution.py:267
  107.0 1.4 collective-permute-start.31
  110.3 12.4 %collective-permute-done.30 = f32[1,128,128]{2,1,0:T(8,128)S(1)} collective-permute-done((f32[1,128,128]{2,1,0:T(8,128)S(1)}, f32[1,128,128]{2,1,0:T(8,128)S(1)}, u32[]{:S(2)}, u32[]{:S(2)}) %collective-permute-start.30) | collective-permute-done | bytes 65568 | tf_op jit(solution)/shard_map/ppermute | solution.py:228
  124.0 2.9 %collective-permute-start.33 = (f32[4,264,128]{2,1,0:T(8,128)S(1)}, f32[4,264,128]{2,1,0:T(8,128)S(1)}, u32[]{:S(2)}, u32[]{:S(2)}) collective-permute-start(f32[4,264,128]{2,1,0:T(8,128)S(1)} %maximum_maximum_fusion.1.near), channel_id=1, source_target_pairs={{0,6},{1,7},{2,0},{3,1},{4,2},{5,3},{6,4},{7,5},{8,14},{9,15},{10,... | collective-permute-start | bytes 1622024 | tf_op jit(solution)/shard_map/ppermute | solution.py:228
  126.8 10.9 %collective-permute-done.32.left = f32[4,264,128]{2,1,0:T(8,128)S(1)} collective-permute-done((f32[4,264,128]{2,1,0:T(8,128)S(1)}, f32[4,264,128]{2,1,0:T(8,128)S(1)}, u32[]{:S(2)}, u32[]{:S(2)}) %collective-permute-start.32) | collective-permute-done | bytes 540704 | tf_op jit(solution)/shard_map/ppermute | solution.py:228
  137.8 2.7 %collective-permute-start.35 = (f32[2,264,128]{2,1,0:T(8,128)S(1)}, f32[2,264,128]{2,1,0:T(8,128)S(1)}, u32[]{:S(2)}, u32[]{:S(2)}) collective-permute-start(f32[2,264,128]{2,1,0:T(8,128)S(1)} %slice.87), channel_id=1, source_target_pairs={{0,6},{1,7},{2,0},{3,1},{4,2},{5,3},{6,4},{7,5},{8,14},{9,15},{10,... | collective-permute-start | bytes 811016 | tf_op jit(solution)/shard_map/ppermute | solution.py:228
  140.6 4.1 %collective-permute-done.34.far_top = f32[2,264,128]{2,1,0:T(8,128)S(1)} collective-permute-done((f32[2,264,128]{2,1,0:T(8,128)S(1)}, f32[2,264,128]{2,1,0:T(8,128)S(1)}, u32[]{:S(2)}, u32[]{:S(2)}) %collective-permute-start.34) | collective-permute-done | bytes 270368 | tf_op jit(solution)/shard_map/ppermute | solution.py:228
  144.7 1.6 pick_for_partner.7
  146.3 3.2 %collective-permute-start.36 = (f32[16,136,128]{2,1,0:T(8,128)}, f32[16,136,128]{2,1,0:T(8,128)}, u32[]{:S(2)}, u32[]{:S(2)}) collective-permute-start(f32[16,136,128]{2,1,0:T(8,128)} %pick_for_partner.7), channel_id=1, source_target_pairs={{0,1},{1,0},{2,3},{3,2},{4,5},{5,4},{6,7},{7,6},{8,9},{9,8},{10,11... | collective-permute-start | bytes 3342344 | tf_op jit(solution)/shard_map/ppermute | solution.py:249
  149.7 2.8 %collective-permute-start.11 = (f32[1,264,128]{2,1,0:T(8,128)S(1)}, f32[1,264,128]{2,1,0:T(8,128)S(1)}, u32[]{:S(2)}, u32[]{:S(2)}) collective-permute-start(f32[1,264,128]{2,1,0:T(8,128)S(1)} %bitcast.12), channel_id=1, source_target_pairs={{0,24},{1,25},{2,26},{3,27},{4,28},{5,29},{6,30},{7,31},{8,0},{9,1... | collective-permute-start | bytes 405512 | tf_op jit(solution)/shard_map/ppermute | solution.py:228
  152.5 4.1 %collective-permute-done.11 = f32[1,264,128]{2,1,0:T(8,128)S(1)} collective-permute-done((f32[1,264,128]{2,1,0:T(8,128)S(1)}, f32[1,264,128]{2,1,0:T(8,128)S(1)}, u32[]{:S(2)}, u32[]{:S(2)}) %collective-permute-start.11) | collective-permute-done | bytes 135200 | tf_op jit(solution)/shard_map/ppermute | solution.py:228
  156.6 3.5 %collective-permute-start.13 = (f32[1,136,128]{2,1,0:T(8,128)S(1)}, f32[1,136,128]{2,1,0:T(8,128)S(1)}, u32[]{:S(2)}, u32[]{:S(2)}) collective-permute-start(f32[1,136,128]{2,1,0:T(8,128)S(1)} %slice.77), channel_id=1, source_target_pairs={{0,24},{1,25},{2,26},{3,27},{4,28},{5,29},{6,30},{7,31},{8,0},{9,1... | collective-permute-start | bytes 208904 | tf_op jit(solution)/shard_map/ppermute | solution.py:228
  160.2 5.2 %collective-permute-done.12 = f32[1,128,128]{2,1,0:T(8,128)S(1)} collective-permute-done((f32[1,128,128]{2,1,0:T(8,128)S(1)}, f32[1,128,128]{2,1,0:T(8,128)S(1)}, u32[]{:S(2)}, u32[]{:S(2)}) %collective-permute-start.12) | collective-permute-done | bytes 65568 | tf_op jit(solution)/shard_map/ppermute | solution.py:228
  165.6 3.0 %collective-permute-start.15 = (f32[4,264,128]{2,1,0:T(8,128)S(1)}, f32[4,264,128]{2,1,0:T(8,128)}, u32[]{:S(2)}, u32[]{:S(2)}) collective-permute-start(f32[4,264,128]{2,1,0:T(8,128)S(1)} %maximum_maximum_fusion.near), channel_id=1, source_target_pairs={{0,6},{1,7},{2,0},{3,1},{4,2},{5,3},{6,4},{7,5},{8,14},{9,15},{10,... | collective-permute-start | bytes 1622024 | tf_op jit(solution)/shard_map/ppermute | solution.py:228
  168.6 3.7 %multiply.7 = f32[8,264,128]{2,1,0:T(8,128)} custom-call(s32[3]{0:T(128)S(1)} %pad_add_fusion.place, s32[32]{0:T(128)S(1)} %copy-done.16, s32[32]{0:T(128)S(1)} %copy-done.17, bf16[32,128,256]{2,1,0:T(8,128)(2,1)} %copy-done, f32[4,264,128]{2,1,0:T(8,128)S(1)} %maximum_maximum_fusion.1.near, f32[4,264,128]{2,1,0:T(8,128)S(1)} %collective-permute-done.32.left, ...), custom_call_target="tpu_custom_call" | custom-call | tf_op jit(solution)/shard_map/multiply/pallas_call | solution.py:146
  172.3 7.1 %all-to-all-start.3 = ((f32[8,264,128]{2,1,0:T(8,128)}), f32[8,264,128]{2,1,0:T(8,128)S(1)}, u32[]{:S(2)}, u32[]{:S(2)}) async-start(f32[8,264,128]{2,1,0:T(8,128)} %multiply.7), calls=%async_computation.3 | async-start | bytes 2162688 | tf_op jit(solution)/shard_map/all_to_all | solution.py:267
  180.6 2.7 %collective-permute-start.17 = (f32[2,264,128]{2,1,0:T(8,128)S(1)}, f32[2,264,128]{2,1,0:T(8,128)S(1)}, u32[]{:S(2)}, u32[]{:S(2)}) collective-permute-start(f32[2,264,128]{2,1,0:T(8,128)S(1)} %slice.79), channel_id=1, source_target_pairs={{0,6},{1,7},{2,0},{3,1},{4,2},{5,3},{6,4},{7,5},{8,14},{9,15},{10,... | collective-permute-start | bytes 811016 | tf_op jit(solution)/shard_map/ppermute | solution.py:228
  183.2 3.2 %collective-permute-done.16.far_top = f32[2,264,128]{2,1,0:T(8,128)S(1)} collective-permute-done((f32[2,264,128]{2,1,0:T(8,128)S(1)}, f32[2,264,128]{2,1,0:T(8,128)S(1)}, u32[]{:S(2)}, u32[]{:S(2)}) %collective-permute-start.16) | collective-permute-done | bytes 270368 | tf_op jit(solution)/shard_map/ppermute | solution.py:228
  187.8 3.5 %collective-permute-start.18 = (f32[16,136,128]{2,1,0:T(8,128)S(1)}, f32[16,136,128]{2,1,0:T(8,128)S(1)}, u32[]{:S(2)}, u32[]{:S(2)}) collective-permute-start(f32[16,136,128]{2,1,0:T(8,128)S(1)} %pick_for_partner.5), channel_id=1, source_target_pairs={{0,1},{1,0},{2,3},{3,2},{4,5},{5,4},{6,7},{7,6},{8,9},{9,8},{10,11... | collective-permute-start | bytes 3342344 | tf_op jit(solution)/shard_map/ppermute | solution.py:249
  191.3 2.4 %collective-permute-done.18.other = f32[16,136,128]{2,1,0:T(8,128)S(1)} collective-permute-done((f32[16,136,128]{2,1,0:T(8,128)S(1)}, f32[16,136,128]{2,1,0:T(8,128)S(1)}, u32[]{:S(2)}, u32[]{:S(2)}) %collective-permute-start.18) | collective-permute-done | bytes 1114144 | tf_op jit(solution)/shard_map/ppermute | solution.py:249
  194.7 2.5 %multiply.5 = f32[8,264,128]{2,1,0:T(8,128)S(1)} custom-call(s32[3]{0:T(128)S(1)} %pad_add_fusion.place, s32[32]{0:T(128)S(1)} %copy-done.16, s32[32]{0:T(128)S(1)} %copy-done.17, bf16[32,128,256]{2,1,0:T(8,128)(2,1)} %copy-done, f32[4,264,128]{2,1,0:T(8,128)S(1)} %maximum_maximum_fusion.near, f32[4,264,128]{2,1,0:T(8,128)S(1)} %copy-done.2, ...), custom_call_target="tpu_custom_call" | custom-call | tf_op jit(solution)/shard_map/multiply/pallas_call | solution.py:146
  197.3 22.6 %all_to_all.20.refs_0_ = f32[8,264,128]{2,1,0:T(8,128)S(1)} all-to-all(f32[8,264,128]{2,1,0:T(8,128)S(1)} %multiply.5), channel_id=1, replica_groups=mesh['row'=8,'col'=32] {'row'}, dimensions={0} | all-to-all | bytes 2162688 | tf_op jit(solution)/shard_map/all_to_all | solution.py:267
  (106 shorter events, 15.6 us)
Async XLA Ops:
  1.6 94.2 %copy-start.6 = (f32[256,128]{1,0:T(8,128)}, f32[256,128]{1,0:T(8,128)S(1)}, u32[]{:S(2)}) copy-start(f32[256,128]{1,0:T(8,128)S(1)} %get-tuple-element.3.vector.refs_5_) | copy-start | bytes 393220
  1.6 147.9 %copy-start.8 = (f32[256,128]{1,0:T(8,128)}, f32[256,128]{1,0:T(8,128)S(1)}, u32[]{:S(2)}) copy-start(f32[256,128]{1,0:T(8,128)S(1)} %get-tuple-element.6.vector.refs_2_) | copy-start | bytes 393220
  1.7 10.7 %collective-permute-start.19 = (f32[1,256,128]{2,1,0:T(8,128)S(1)}, f32[1,256,128]{2,1,0:T(8,128)S(1)}, u32[]{:S(2)}, u32[]{:S(2)}) collective-permute-start(f32[1,256,128]{2,1,0:T(8,128)S(1)} %get-tuple-element.5), channel_id=1, source_target_pairs={{0,8},{1,9},{2,10},{3,11},{4,12},{5,13},{6,14},{7,15},{8,16},{9,17... | collective-permute-start | bytes 393224 | tf_op jit(solution)/shard_map/ppermute | solution.py:228
  5.6 10.5 %collective-permute-start.20 = (f32[1,256,128]{2,1,0:T(8,128)S(1)}, f32[1,256,128]{2,1,0:T(8,128)S(1)}, u32[]{:S(2)}, u32[]{:S(2)}) collective-permute-start(f32[1,256,128]{2,1,0:T(8,128)S(1)} %get-tuple-element.5), channel_id=1, source_target_pairs={{0,24},{1,25},{2,26},{3,27},{4,28},{5,29},{6,30},{7,31},{8,0},{9,1... | collective-permute-start | bytes 393224 | tf_op jit(solution)/shard_map/ppermute | solution.py:228
  12.4 24.2 %copy-start.16 = (s32[32]{0:T(128)S(1)}, s32[32]{0:T(128)}, u32[]{:S(2)}) copy-start(s32[32]{0:T(128)} %rows.7) | copy-start | bytes 388
  12.4 6.0 %collective-permute-start.21 = (f32[1,128,128]{2,1,0:T(8,128)S(1)}, f32[1,128,128]{2,1,0:T(8,128)S(1)}, u32[]{:S(2)}, u32[]{:S(2)}) collective-permute-start(f32[1,128,128]{2,1,0:T(8,128)S(1)} %slice.80), channel_id=1, source_target_pairs={{0,8},{1,9},{2,10},{3,11},{4,12},{5,13},{6,14},{7,15},{8,16},{9,17... | collective-permute-start | bytes 196616 | tf_op jit(solution)/shard_map/ppermute | solution.py:228
  16.1 5.4 %collective-permute-start.22 = (f32[1,128,128]{2,1,0:T(8,128)S(1)}, f32[1,128,128]{2,1,0:T(8,128)S(1)}, u32[]{:S(2)}, u32[]{:S(2)}) collective-permute-start(f32[1,128,128]{2,1,0:T(8,128)S(1)} %slice.81), channel_id=1, source_target_pairs={{0,24},{1,25},{2,26},{3,27},{4,28},{5,29},{6,30},{7,31},{8,0},{9,1... | collective-permute-start | bytes 196616 | tf_op jit(solution)/shard_map/ppermute | solution.py:228
  21.5 12.2 %collective-permute-start.23 = (f32[4,256,128]{2,1,0:T(8,128)S(1)}, f32[4,256,128]{2,1,0:T(8,128)S(1)}, u32[]{:S(2)}, u32[]{:S(2)}) collective-permute-start(f32[4,256,128]{2,1,0:T(8,128)S(1)} %maximum_maximum_fusion.3.near), channel_id=1, source_target_pairs={{0,2},{1,3},{2,4},{3,5},{4,6},{5,7},{6,0},{7,1},{8,10},{9,11},{10,... | collective-permute-start | bytes 1572872 | tf_op jit(solution)/shard_map/ppermute | solution.py:228
  22.8 11.1 %collective-permute-start.24 = (f32[4,256,128]{2,1,0:T(8,128)S(1)}, f32[4,256,128]{2,1,0:T(8,128)S(1)}, u32[]{:S(2)}, u32[]{:S(2)}) collective-permute-start(f32[4,256,128]{2,1,0:T(8,128)S(1)} %maximum_maximum_fusion.3.near), channel_id=1, source_target_pairs={{0,6},{1,7},{2,0},{3,1},{4,2},{5,3},{6,4},{7,5},{8,14},{9,15},{10,... | collective-permute-start | bytes 1572872 | tf_op jit(solution)/shard_map/ppermute | solution.py:228
  33.8 7.6 %collective-permute-start.25 = (f32[2,256,128]{2,1,0:T(8,128)S(1)}, f32[2,256,128]{2,1,0:T(8,128)S(1)}, u32[]{:S(2)}, u32[]{:S(2)}) collective-permute-start(f32[2,256,128]{2,1,0:T(8,128)S(1)} %slice.82), channel_id=1, source_target_pairs={{0,2},{1,3},{2,4},{3,5},{4,6},{5,7},{6,0},{7,1},{8,10},{9,11},{10,... | collective-permute-start | bytes 786440 | tf_op jit(solution)/shard_map/ppermute | solution.py:228
  33.9 7.5 %collective-permute-start.26 = (f32[2,256,128]{2,1,0:T(8,128)S(1)}, f32[2,256,128]{2,1,0:T(8,128)S(1)}, u32[]{:S(2)}, u32[]{:S(2)}) collective-permute-start(f32[2,256,128]{2,1,0:T(8,128)S(1)} %slice.83), channel_id=1, source_target_pairs={{0,6},{1,7},{2,0},{3,1},{4,2},{5,3},{6,4},{7,5},{8,14},{9,15},{10,... | collective-permute-start | bytes 786440 | tf_op jit(solution)/shard_map/ppermute | solution.py:228
  36.6 4.8 %collective-permute-start.8 = (s32[32]{0:T(128)S(1)}, s32[32]{0:T(128)S(1)}, u32[]{:S(2)}, u32[]{:S(2)}) collective-permute-start(s32[32]{0:T(128)S(1)} %copy-done.16), channel_id=1, source_target_pairs={{0,1},{1,0},{2,3},{3,2},{4,5},{5,4},{6,7},{7,6},{8,9},{9,8},{10,11... | collective-permute-start | bytes 392 | tf_op jit(solution)/shard_map/ppermute | solution.py:249
  40.6 19.4 %copy-start.3 = (f32[32,128,128]{2,1,0:T(8,128)S(1)}, f32[32,128,128]{2,1,0:T(8,128)}, u32[]{:S(2)}) copy-start(f32[32,128,128]{2,1,0:T(8,128)} %blocks.1) | copy-start | bytes 6291460
  42.0 20.2 %collective-permute-start.27 = (f32[16,128,128]{2,1,0:T(8,128)S(1)}, f32[16,128,128]{2,1,0:T(8,128)S(1)}, u32[]{:S(2)}, u32[]{:S(2)}) collective-permute-start(f32[16,128,128]{2,1,0:T(8,128)S(1)} %pick_for_partner.6), channel_id=1, source_target_pairs={{0,1},{1,0},{2,3},{3,2},{4,5},{5,4},{6,7},{7,6},{8,9},{9,8},{10,11... | collective-permute-start | bytes 3145736 | tf_op jit(solution)/shard_map/ppermute | solution.py:249
  45.5 9.9 %collective-permute-start = (f32[1,256,128]{2,1,0:T(8,128)S(1)}, f32[1,256,128]{2,1,0:T(8,128)S(1)}, u32[]{:S(2)}, u32[]{:S(2)}) collective-permute-start(f32[1,256,128]{2,1,0:T(8,128)S(1)} %get-tuple-element.4), channel_id=1, source_target_pairs={{0,8},{1,9},{2,10},{3,11},{4,12},{5,13},{6,14},{7,15},{8,16},{9,17... | collective-permute-start | bytes 393224 | tf_op jit(solution)/shard_map/ppermute | solution.py:228
  49.0 8.0 %collective-permute-start.1 = (f32[1,256,128]{2,1,0:T(8,128)S(1)}, f32[1,256,128]{2,1,0:T(8,128)S(1)}, u32[]{:S(2)}, u32[]{:S(2)}) collective-permute-start(f32[1,256,128]{2,1,0:T(8,128)S(1)} %get-tuple-element.4), channel_id=1, source_target_pairs={{0,24},{1,25},{2,26},{3,27},{4,28},{5,29},{6,30},{7,31},{8,0},{9,1... | collective-permute-start | bytes 393224 | tf_op jit(solution)/shard_map/ppermute | solution.py:228
  55.4 14.4 %collective-permute-start.2 = (f32[1,128,128]{2,1,0:T(8,128)S(1)}, f32[1,128,128]{2,1,0:T(8,128)S(1)}, u32[]{:S(2)}, u32[]{:S(2)}) collective-permute-start(f32[1,128,128]{2,1,0:T(8,128)S(1)} %slice.72), channel_id=1, source_target_pairs={{0,8},{1,9},{2,10},{3,11},{4,12},{5,13},{6,14},{7,15},{8,16},{9,17... | collective-permute-start | bytes 196616 | tf_op jit(solution)/shard_map/ppermute | solution.py:228
  57.1 12.8 %collective-permute-start.3 = (f32[1,128,128]{2,1,0:T(8,128)S(1)}, f32[1,128,128]{2,1,0:T(8,128)S(1)}, u32[]{:S(2)}, u32[]{:S(2)}) collective-permute-start(f32[1,128,128]{2,1,0:T(8,128)S(1)} %slice.73), channel_id=1, source_target_pairs={{0,24},{1,25},{2,26},{3,27},{4,28},{5,29},{6,30},{7,31},{8,0},{9,1... | collective-permute-start | bytes 196616 | tf_op jit(solution)/shard_map/ppermute | solution.py:228
  65.7 30.0 %all-to-all-start.2 = ((f32[8,256,128]{2,1,0:T(8,128)}), f32[8,256,128]{2,1,0:T(8,128)S(1)}, u32[]{:S(2)}, u32[]{:S(2)}) async-start(f32[8,256,128]{2,1,0:T(8,128)} %multiply.6), calls=%async_computation.2 | async-start | bytes 2097152 | tf_op jit(solution)/shard_map/all_to_all | solution.py:267
  69.9 14.1 %collective-permute-start.4 = (f32[4,256,128]{2,1,0:T(8,128)S(1)}, f32[4,256,128]{2,1,0:T(8,128)S(1)}, u32[]{:S(2)}, u32[]{:S(2)}) collective-permute-start(f32[4,256,128]{2,1,0:T(8,128)S(1)} %maximum_maximum_fusion.2.near), channel_id=1, source_target_pairs={{0,2},{1,3},{2,4},{3,5},{4,6},{5,7},{6,0},{7,1},{8,10},{9,11},{10,... | collective-permute-start | bytes 1572872 | tf_op jit(solution)/shard_map/ppermute | solution.py:228
  70.8 13.3 %collective-permute-start.5 = (f32[4,256,128]{2,1,0:T(8,128)S(1)}, f32[4,256,128]{2,1,0:T(8,128)S(1)}, u32[]{:S(2)}, u32[]{:S(2)}) collective-permute-start(f32[4,256,128]{2,1,0:T(8,128)S(1)} %maximum_maximum_fusion.2.near), channel_id=1, source_target_pairs={{0,6},{1,7},{2,0},{3,1},{4,2},{5,3},{6,4},{7,5},{8,14},{9,15},{10,... | collective-permute-start | bytes 1572872 | tf_op jit(solution)/shard_map/ppermute | solution.py:228
  84.1 7.0 %collective-permute-start.6 = (f32[2,256,128]{2,1,0:T(8,128)S(1)}, f32[2,256,128]{2,1,0:T(8,128)S(1)}, u32[]{:S(2)}, u32[]{:S(2)}) collective-permute-start(f32[2,256,128]{2,1,0:T(8,128)S(1)} %slice.74), channel_id=1, source_target_pairs={{0,2},{1,3},{2,4},{3,5},{4,6},{5,7},{6,0},{7,1},{8,10},{9,11},{10,... | collective-permute-start | bytes 786440 | tf_op jit(solution)/shard_map/ppermute | solution.py:228
  84.2 6.9 %collective-permute-start.7 = (f32[2,256,128]{2,1,0:T(8,128)S(1)}, f32[2,256,128]{2,1,0:T(8,128)S(1)}, u32[]{:S(2)}, u32[]{:S(2)}) collective-permute-start(f32[2,256,128]{2,1,0:T(8,128)S(1)} %slice.75), channel_id=1, source_target_pairs={{0,6},{1,7},{2,0},{3,1},{4,2},{5,3},{6,4},{7,5},{8,14},{9,15},{10,... | collective-permute-start | bytes 786440 | tf_op jit(solution)/shard_map/ppermute | solution.py:228
  92.7 5.7 %collective-permute-start.9 = (f32[16,128,128]{2,1,0:T(8,128)}, f32[16,128,128]{2,1,0:T(8,128)}, u32[]{:S(2)}, u32[]{:S(2)}) collective-permute-start(f32[16,128,128]{2,1,0:T(8,128)} %pick_for_partner.4), channel_id=1, source_target_pairs={{0,1},{1,0},{2,3},{3,2},{4,5},{5,4},{6,7},{7,6},{8,9},{9,8},{10,11... | collective-permute-start | bytes 3145736 | tf_op jit(solution)/shard_map/ppermute | solution.py:249
  96.0 11.0 %collective-permute-start.29 = (f32[1,264,128]{2,1,0:T(8,128)S(1)}, f32[1,264,128]{2,1,0:T(8,128)S(1)}, u32[]{:S(2)}, u32[]{:S(2)}) collective-permute-start(f32[1,264,128]{2,1,0:T(8,128)S(1)} %bitcast.9), channel_id=1, source_target_pairs={{0,24},{1,25},{2,26},{3,27},{4,28},{5,29},{6,30},{7,31},{8,0},{9,1... | collective-permute-start | bytes 405512 | tf_op jit(solution)/shard_map/ppermute | solution.py:228
  96.0 12.3 %collective-permute-start.28 = (f32[1,264,128]{2,1,0:T(8,128)S(1)}, f32[1,264,128]{2,1,0:T(8,128)}, u32[]{:S(2)}, u32[]{:S(2)}) collective-permute-start(f32[1,264,128]{2,1,0:T(8,128)S(1)} %bitcast.10), channel_id=1, source_target_pairs={{0,8},{1,9},{2,10},{3,11},{4,12},{5,13},{6,14},{7,15},{8,16},{9,17... | collective-permute-start | bytes 405512 | tf_op jit(solution)/shard_map/ppermute | solution.py:228
  102.1 47.4 %all-to-all-start = ((f32[8,256,128]{2,1,0:T(8,128)}), f32[8,256,128]{2,1,0:T(8,128)S(1)}, u32[]{:S(2)}, u32[]{:S(2)}) async-start(f32[8,256,128]{2,1,0:T(8,128)} %multiply.4), calls=%async_computation | async-start | bytes 2097152 | tf_op jit(solution)/shard_map/all_to_all | solution.py:267
  107.0 15.7 %collective-permute-start.31 = (f32[1,136,128]{2,1,0:T(8,128)S(1)}, f32[1,136,128]{2,1,0:T(8,128)S(1)}, u32[]{:S(2)}, u32[]{:S(2)}) collective-permute-start(f32[1,136,128]{2,1,0:T(8,128)S(1)} %slice.85), channel_id=1, source_target_pairs={{0,24},{1,25},{2,26},{3,27},{4,28},{5,29},{6,30},{7,31},{8,0},{9,1... | collective-permute-start | bytes 208904 | tf_op jit(solution)/shard_map/ppermute | solution.py:228
  109.2 13.4 %collective-permute-start.30 = (f32[1,128,128]{2,1,0:T(8,128)S(1)}, f32[1,128,128]{2,1,0:T(8,128)S(1)}, u32[]{:S(2)}, u32[]{:S(2)}) collective-permute-start(f32[1,128,128]{2,1,0:T(8,128)S(1)} %slice.84), channel_id=1, source_target_pairs={{0,8},{1,9},{2,10},{3,11},{4,12},{5,13},{6,14},{7,15},{8,16},{9,17... | collective-permute-start | bytes 196616 | tf_op jit(solution)/shard_map/ppermute | solution.py:228
  123.6 14.1 %collective-permute-start.32 = (f32[4,264,128]{2,1,0:T(8,128)S(1)}, f32[4,264,128]{2,1,0:T(8,128)S(1)}, u32[]{:S(2)}, u32[]{:S(2)}) collective-permute-start(f32[4,264,128]{2,1,0:T(8,128)S(1)} %maximum_maximum_fusion.1.near), channel_id=1, source_target_pairs={{0,2},{1,3},{2,4},{3,5},{4,6},{5,7},{6,0},{7,1},{8,10},{9,11},{10,... | collective-permute-start | bytes 1622024 | tf_op jit(solution)/shard_map/ppermute | solution.py:228
  124.0 13.8 %collective-permute-start.33 = (f32[4,264,128]{2,1,0:T(8,128)S(1)}, f32[4,264,128]{2,1,0:T(8,128)S(1)}, u32[]{:S(2)}, u32[]{:S(2)}) collective-permute-start(f32[4,264,128]{2,1,0:T(8,128)S(1)} %maximum_maximum_fusion.1.near), channel_id=1, source_target_pairs={{0,6},{1,7},{2,0},{3,1},{4,2},{5,3},{6,4},{7,5},{8,14},{9,15},{10,... | collective-permute-start | bytes 1622024 | tf_op jit(solution)/shard_map/ppermute | solution.py:228
  137.7 7.0 %collective-permute-start.34 = (f32[2,264,128]{2,1,0:T(8,128)S(1)}, f32[2,264,128]{2,1,0:T(8,128)S(1)}, u32[]{:S(2)}, u32[]{:S(2)}) collective-permute-start(f32[2,264,128]{2,1,0:T(8,128)S(1)} %slice.86), channel_id=1, source_target_pairs={{0,2},{1,3},{2,4},{3,5},{4,6},{5,7},{6,0},{7,1},{8,10},{9,11},{10,... | collective-permute-start | bytes 811016 | tf_op jit(solution)/shard_map/ppermute | solution.py:228
  137.8 6.9 %collective-permute-start.35 = (f32[2,264,128]{2,1,0:T(8,128)S(1)}, f32[2,264,128]{2,1,0:T(8,128)S(1)}, u32[]{:S(2)}, u32[]{:S(2)}) collective-permute-start(f32[2,264,128]{2,1,0:T(8,128)S(1)} %slice.87), channel_id=1, source_target_pairs={{0,6},{1,7},{2,0},{3,1},{4,2},{5,3},{6,4},{7,5},{8,14},{9,15},{10,... | collective-permute-start | bytes 811016 | tf_op jit(solution)/shard_map/ppermute | solution.py:228
  146.3 22.2 %collective-permute-start.36 = (f32[16,136,128]{2,1,0:T(8,128)}, f32[16,136,128]{2,1,0:T(8,128)}, u32[]{:S(2)}, u32[]{:S(2)}) collective-permute-start(f32[16,136,128]{2,1,0:T(8,128)} %pick_for_partner.7), channel_id=1, source_target_pairs={{0,1},{1,0},{2,3},{3,2},{4,5},{5,4},{6,7},{7,6},{8,9},{9,8},{10,11... | collective-permute-start | bytes 3342344 | tf_op jit(solution)/shard_map/ppermute | solution.py:249
  149.5 19.0 %copy-start.13 = (f32[2,264,128]{2,1,0:T(8,128)S(1)}, f32[2,264,128]{2,1,0:T(8,128)}, u32[]{:S(2)}) copy-start(f32[2,264,128]{2,1,0:T(8,128)} %copy-done.12) | copy-start | bytes 811012
  149.7 6.9 %collective-permute-start.11 = (f32[1,264,128]{2,1,0:T(8,128)S(1)}, f32[1,264,128]{2,1,0:T(8,128)S(1)}, u32[]{:S(2)}, u32[]{:S(2)}) collective-permute-start(f32[1,264,128]{2,1,0:T(8,128)S(1)} %bitcast.12), channel_id=1, source_target_pairs={{0,24},{1,25},{2,26},{3,27},{4,28},{5,29},{6,30},{7,31},{8,0},{9,1... | collective-permute-start | bytes 405512 | tf_op jit(solution)/shard_map/ppermute | solution.py:228
  152.5 7.6 %collective-permute-start.10 = (f32[1,264,128]{2,1,0:T(8,128)S(1)}, f32[1,264,128]{2,1,0:T(8,128)S(1)}, u32[]{:S(2)}, u32[]{:S(2)}) collective-permute-start(f32[1,264,128]{2,1,0:T(8,128)S(1)} %bitcast.13), channel_id=1, source_target_pairs={{0,8},{1,9},{2,10},{3,11},{4,12},{5,13},{6,14},{7,15},{8,16},{9,17... | collective-permute-start | bytes 405512 | tf_op jit(solution)/shard_map/ppermute | solution.py:228
  156.6 8.9 %collective-permute-start.13 = (f32[1,136,128]{2,1,0:T(8,128)S(1)}, f32[1,136,128]{2,1,0:T(8,128)S(1)}, u32[]{:S(2)}, u32[]{:S(2)}) collective-permute-start(f32[1,136,128]{2,1,0:T(8,128)S(1)} %slice.77), channel_id=1, source_target_pairs={{0,24},{1,25},{2,26},{3,27},{4,28},{5,29},{6,30},{7,31},{8,0},{9,1... | collective-permute-start | bytes 208904 | tf_op jit(solution)/shard_map/ppermute | solution.py:228
  160.1 5.3 %collective-permute-start.12 = (f32[1,128,128]{2,1,0:T(8,128)S(1)}, f32[1,128,128]{2,1,0:T(8,128)S(1)}, u32[]{:S(2)}, u32[]{:S(2)}) collective-permute-start(f32[1,128,128]{2,1,0:T(8,128)S(1)} %slice.76), channel_id=1, source_target_pairs={{0,8},{1,9},{2,10},{3,11},{4,12},{5,13},{6,14},{7,15},{8,16},{9,17... | collective-permute-start | bytes 196616 | tf_op jit(solution)/shard_map/ppermute | solution.py:228
  165.5 13.9 %collective-permute-start.14 = (f32[4,264,128]{2,1,0:T(8,128)S(1)}, f32[4,264,128]{2,1,0:T(8,128)S(1)}, u32[]{:S(2)}, u32[]{:S(2)}) collective-permute-start(f32[4,264,128]{2,1,0:T(8,128)S(1)} %maximum_maximum_fusion.near), channel_id=1, source_target_pairs={{0,2},{1,3},{2,4},{3,5},{4,6},{5,7},{6,0},{7,1},{8,10},{9,11},{10,... | collective-permute-start | bytes 1622024 | tf_op jit(solution)/shard_map/ppermute | solution.py:228
  165.6 13.9 %collective-permute-start.15 = (f32[4,264,128]{2,1,0:T(8,128)S(1)}, f32[4,264,128]{2,1,0:T(8,128)}, u32[]{:S(2)}, u32[]{:S(2)}) collective-permute-start(f32[4,264,128]{2,1,0:T(8,128)S(1)} %maximum_maximum_fusion.near), channel_id=1, source_target_pairs={{0,6},{1,7},{2,0},{3,1},{4,2},{5,3},{6,4},{7,5},{8,14},{9,15},{10,... | collective-permute-start | bytes 1622024 | tf_op jit(solution)/shard_map/ppermute | solution.py:228
  172.3 25.0 %all-to-all-start.3 = ((f32[8,264,128]{2,1,0:T(8,128)}), f32[8,264,128]{2,1,0:T(8,128)S(1)}, u32[]{:S(2)}, u32[]{:S(2)}) async-start(f32[8,264,128]{2,1,0:T(8,128)} %multiply.7), calls=%async_computation.3 | async-start | bytes 2162688 | tf_op jit(solution)/shard_map/all_to_all | solution.py:267
  179.4 7.0 %collective-permute-start.16 = (f32[2,264,128]{2,1,0:T(8,128)S(1)}, f32[2,264,128]{2,1,0:T(8,128)S(1)}, u32[]{:S(2)}, u32[]{:S(2)}) collective-permute-start(f32[2,264,128]{2,1,0:T(8,128)S(1)} %slice.78), channel_id=1, source_target_pairs={{0,2},{1,3},{2,4},{3,5},{4,6},{5,7},{6,0},{7,1},{8,10},{9,11},{10,... | collective-permute-start | bytes 811016 | tf_op jit(solution)/shard_map/ppermute | solution.py:228
  180.6 6.1 %collective-permute-start.17 = (f32[2,264,128]{2,1,0:T(8,128)S(1)}, f32[2,264,128]{2,1,0:T(8,128)S(1)}, u32[]{:S(2)}, u32[]{:S(2)}) collective-permute-start(f32[2,264,128]{2,1,0:T(8,128)S(1)} %slice.79), channel_id=1, source_target_pairs={{0,6},{1,7},{2,0},{3,1},{4,2},{5,3},{6,4},{7,5},{8,14},{9,15},{10,... | collective-permute-start | bytes 811016 | tf_op jit(solution)/shard_map/ppermute | solution.py:228
  187.8 5.9 %collective-permute-start.18 = (f32[16,136,128]{2,1,0:T(8,128)S(1)}, f32[16,136,128]{2,1,0:T(8,128)S(1)}, u32[]{:S(2)}, u32[]{:S(2)}) collective-permute-start(f32[16,136,128]{2,1,0:T(8,128)S(1)} %pick_for_partner.5), channel_id=1, source_target_pairs={{0,1},{1,0},{2,3},{3,2},{4,5},{5,4},{6,7},{7,6},{8,9},{9,8},{10,11... | collective-permute-start | bytes 3342344 | tf_op jit(solution)/shard_map/ppermute | solution.py:249
  197.3 22.7 %copy-start.5 = (f32[264,128]{1,0:T(8,128)S(1)}, f32[264,128]{1,0:T(8,128)}, u32[]{:S(2)}) copy-start(f32[264,128]{1,0:T(8,128)} %copy-done.4) | copy-start | bytes 405508
  197.3 22.7 %copy-start.7 = (f32[256,128]{1,0:T(8,128)S(1)}, f32[256,128]{1,0:T(8,128)}, u32[]{:S(2)}) copy-start(f32[256,128]{1,0:T(8,128)} %copy-done.6) | copy-start | bytes 393220
  197.3 22.7 %copy-start.9 = (f32[256,128]{1,0:T(8,128)S(1)}, f32[256,128]{1,0:T(8,128)}, u32[]{:S(2)}) copy-start(f32[256,128]{1,0:T(8,128)} %copy-done.8) | copy-start | bytes 393220
  (11 other events, 66.9 us)

commit v2 on v1

v2 whole, which is shorter than its diff:
```python
import functools

import jax
import jax.numpy as jnp
from jax import lax
from jax.experimental import pallas as pl
from jax.experimental.pallas import tpu as pltpu
from jax.sharding import PartitionSpec as P

TILE = 128
WIDTH = 256
STAT = 8
LIMIT = 48 * 1024 * 1024


def col_index(z, x, core):
    return (z % 4) * 8 + (x % 4) * 2 + core


def col_pairs(along_z):
    pairs = []
    for z in range(4):
        for x in range(4):
            for core, step in ((0, 1), (1, 3)):
                to = (z + step, x) if along_z else (z, x + step)
                pairs.append((col_index(z, x, core), col_index(*to, core)))
    return pairs


def smem():
    return pl.BlockSpec(memory_space=pltpu.SMEM)


def vmem():
    return pl.BlockSpec(memory_space=pltpu.VMEM)


def params():
    return pltpu.CompilerParams(vmem_limit_bytes=LIMIT)


def split_blocks_kernel(counts, blocks, out):
    base = pl.program_id(0) * blocks.shape[0]
    for i in range(blocks.shape[0]):
        block = jnp.where(base + i < counts[0], blocks[i], 0.0).T
        high = block.astype(jnp.bfloat16)
        low = (block - high.astype(jnp.float32)).astype(jnp.bfloat16)
        out[i, :, :TILE] = high
        out[i, :, TILE:] = low


def split_blocks(counts, blocks):
    n, step = blocks.shape[0], 8
    return pl.pallas_call(
        split_blocks_kernel,
        grid=(n // step,),
        out_shape=jax.ShapeDtypeStruct((n, TILE, 2 * TILE), jnp.bfloat16),
        in_specs=[smem(), pl.BlockSpec((step, TILE, TILE), lambda i: (i, 0, 0))],
        out_specs=pl.BlockSpec((step, TILE, 2 * TILE), lambda i: (i, 0, 0)),
        compiler_params=params(),
        name="split_blocks",
    )(counts, blocks)


NONE, WAY, AGAINST, TWO = range(4)
CHIP = ((NONE, 1), (NONE, 0))
MID = ((WAY, 1), (WAY, 0), (AGAINST, 0), (AGAINST, 1))
LAST = ((TWO, 1), (TWO, 0))


def named(dx, keys, ref):
    return [(dx, *key, ref, i) for i, key in enumerate(keys)]


def early_pieces(chip, mid, last):
    return named(NONE, CHIP, chip) + named(NONE, MID, mid) + named(NONE, LAST, last)


def early_brought(chip, mid, last, far):
    return named(WAY, CHIP, chip) + named(WAY, MID, mid) + named(WAY, LAST, last) + named(TWO, CHIP[1:], far)


def late_brought(mid, last):
    return named(TWO, MID[:2], mid) + named(TWO, LAST[1:], last)


def slot_of(place, dx, dz, other, core):
    steps = (0, 3 - 2 * core, 1 + 2 * core, 2)
    number = 1 - core if other else core
    return ((place[0] + steps[dz]) & 3) * 8 + ((place[1] + steps[dx]) & 3) * 2 + number


def pick_kernel(layout, place, rows, *refs):
    *brought, out = refs
    for n, (dx, dz, other, ref, i) in enumerate(layout(*brought)):
        slot = slot_of(place, dx, dz, other, place[2])
        start = pl.multiple_of((rows[slot] & 1) * TILE, TILE)
        out[n, :TILE] = ref[i, pl.ds(start, TILE)]
        if out.shape[1] > TILE:
            out[n, TILE:] = ref[i, 2 * TILE :]


def pick_for_partner(layout, place, partner_rows, brought):
    extra = brought[0].shape[1] - 2 * TILE
    return pl.pallas_call(
        functools.partial(pick_kernel, layout),
        out_shape=jax.ShapeDtypeStruct((len(layout(*brought)), TILE + extra, WIDTH), jnp.float32),
        in_specs=[smem(), smem()] + [vmem()] * len(brought),
        out_specs=vmem(),
        compiler_params=params(),
        name="pick_for_partner",
    )(place, partner_rows, *brought)


def merge(stats):
    squares, inner, rest = stats
    ratio = jnp.where(squares > 0, inner / jnp.where(squares > 0, squares, 1.0), 0.0)
    total, inner_total = jnp.sum(squares, axis=0), jnp.sum(inner, axis=0)
    safe = jnp.where(total > 0, total, 1.0)
    mean_ratio = jnp.where(total > 0, inner_total / safe, 0.0)
    away = ratio - mean_ratio[None]
    return total, inner_total, jnp.sum(rest + squares * away * away, axis=0), mean_ratio


def add_products(place, rows, cols, split, own, brought, other, out, stats):
    core = place[2]

    def add(slot, source):
        high = source.astype(jnp.bfloat16)
        low = (source - high.astype(jnp.float32)).astype(jnp.bfloat16)
        both = split[slot]
        total = jnp.dot(
            both, jnp.concatenate([high, high], axis=0), preferred_element_type=jnp.float32
        ) + jnp.dot(both, jnp.concatenate([low, low], axis=0), preferred_element_type=jnp.float32)
        target = cols[slot]
        owner = lax.shift_right_logical(target, 6)
        start = pl.multiple_of((target & 1) * TILE, TILE)
        out[owner, pl.ds(start, TILE)] += total

    for dx, dz, foreign, ref, i in own + brought:
        slot = slot_of(place, dx, dz, foreign, core)
        start = pl.multiple_of((rows[slot] & 1) * TILE, TILE)
        add(slot, ref[i, pl.ds(start, TILE)])
        if stats is not None:
            stats[slot] = ref[i, 2 * TILE :]
    for n, (dx, dz, foreign, _, _) in enumerate(brought):
        slot = slot_of(place, dx, dz, foreign, 1 - core)
        add(slot, other[n, :TILE])
        if stats is not None:
            stats[slot] = other[n, TILE:]


def early_kernel(place, rows, cols, split, *refs):
    out, stats = refs[8], refs[9] if len(refs) > 9 else None
    out[...] = jnp.zeros_like(out)
    if stats is not None:
        stats[...] = jnp.zeros_like(stats)
    own, brought = early_pieces(*refs[:3]), early_brought(*refs[3:7])
    add_products(place, rows, cols, split, own, brought, refs[7], out, stats)


def multiply_early(place, rows, cols, split, gathered, other):
    height = gathered[0].shape[1]
    shapes = [jax.ShapeDtypeStruct((8, height, WIDTH), jnp.float32)]
    if height > 2 * TILE:
        shapes.append(jax.ShapeDtypeStruct((32, STAT, WIDTH), jnp.float32))
    return pl.pallas_call(
        early_kernel,
        out_shape=shapes,
        in_specs=[smem()] * 3 + [vmem()] * (2 + len(gathered)),
        out_specs=[vmem()] * len(shapes),
        compiler_params=params(),
        name="multiply_early",
    )(place, rows, cols, split, *gathered, other)


def late_kernel(place, rows, cols, split, mid, last, other, sums, *refs):
    if len(refs) == 1:
        out, stats = refs[0], None
    else:
        known, out, stats = refs
        stats[...] = known[...]
    out[...] = sums[...]
    add_products(place, rows, cols, split, [], late_brought(mid, last), other, out, stats)
    if stats is not None:
        total, inner, rest, _ = merge([stats[:, k : k + 1, :] for k in range(3)])
        joined = jnp.concatenate([total, inner, rest, jnp.zeros((STAT - 3, WIDTH), jnp.float32)], axis=0)
        for owner in range(out.shape[0]):
            out[owner, 2 * TILE :] = joined


def multiply_late(place, rows, cols, split, gathered, other, sums, *stats):
    return pl.pallas_call(
        late_kernel,
        out_shape=jax.ShapeDtypeStruct(sums.shape, jnp.float32),
        in_specs=[smem()] * 3 + [vmem()] * (5 + len(stats)),
        out_specs=vmem(),
        scratch_shapes=[pltpu.VMEM(each.shape, jnp.float32) for each in stats],
        compiler_params=params(),
        name="multiply_late",
    )(place, rows, cols, split, *gathered, other, sums, *stats)


def sum_terms(terms, diagonal, source):
    total = terms[0, : 2 * TILE]
    for k in range(1, terms.shape[0]):
        total = total + terms[k, : 2 * TILE]
    return diagonal[...] * source + total


def first_image_kernel(terms, diagonal, vector, out):
    v = vector[...]
    w = sum_terms(terms, diagonal, v)
    out[: 2 * TILE] = w
    squares = jnp.sum(v * v, axis=0, keepdims=True)
    inner = jnp.sum(w * v, axis=0, keepdims=True)
    ratio = jnp.where(squares > 0, inner / jnp.where(squares > 0, squares, 1.0), 0.0)
    away = w - ratio * v
    rest = jnp.sum(away * away, axis=0, keepdims=True)
    out[2 * TILE :] = jnp.concatenate(
        [squares, inner, rest, jnp.zeros((STAT - 3, WIDTH), jnp.float32)], axis=0
    )


def first_image(terms, diagonal, vector):
    return pl.pallas_call(
        first_image_kernel,
        out_shape=jax.ShapeDtypeStruct((2 * TILE + STAT, WIDTH), jnp.float32),
        in_specs=[vmem()] * 3,
        out_specs=vmem(),
        compiler_params=params(),
        name="first_image",
    )(terms, diagonal, vector)


def finish_kernel(count, diagonal, terms, image, vector, basis, second, column):
    stats = [terms[:, 2 * TILE + k : 2 * TILE + k + 1, :] for k in range(3)]
    squares, inner, rest, ratio = merge(stats)
    mean = squares / count + 1e-06
    magnitude = jnp.sqrt(mean)
    projection = inner / count / mean
    gap = projection - ratio
    left_over = rest + squares * gap * gap
    norm = jnp.sqrt(left_over / count / mean + 1e-06)
    column[0:1] = projection
    column[1:2] = norm
    w = image[: 2 * TILE]
    scale = 1.0 / (magnitude * norm)
    basis[...] = (w - projection * vector[...]) * scale
    second[...] = (sum_terms(terms, diagonal, w) - projection * w) * scale


def finish(count, diagonal, terms, image, vector):
    return pl.pallas_call(
        functools.partial(finish_kernel, count),
        out_shape=(
            jax.ShapeDtypeStruct((2 * TILE, WIDTH), jnp.float32),
            jax.ShapeDtypeStruct((2 * TILE, WIDTH), jnp.float32),
            jax.ShapeDtypeStruct((2, WIDTH), jnp.float32),
        ),
        in_specs=[vmem()] * 4,
        out_specs=(vmem(),) * 3,
        compiler_params=params(),
        name="finish",
    )(diagonal, terms, image, vector)


def after(value, *earlier):
    return lax.optimization_barrier((value, earlier))[0]


def swap_cores(part):
    return lax.ppermute(part, "col", [(i, i ^ 1) for i in range(32)])


def send_z(part):
    return lax.ppermute(part, "col", col_pairs(True))


def send_x(part):
    return lax.ppermute(part, "col", col_pairs(False))


def join(*parts):
    return jnp.concatenate([part if part.ndim == 3 else part[None] for part in parts], axis=0)


def per_device(blocks, block_row, block_col, counts, diagonal, vector):
    count = vector.shape[0] * lax.axis_size("row") * lax.axis_size("col")
    index = lax.axis_index("col")
    place = jnp.stack([index // 8, index // 2 % 4, index % 2]).astype(jnp.int32)
    partner_rows = swap_cores(block_row)
    diagonal = jnp.broadcast_to(diagonal[:, None], (2 * TILE, WIDTH))
    split = split_blocks(counts, blocks)
    slots = (place, block_row, block_col, split)

    def product(own):
        chip = join(swap_cores(own), own)
        z_chip = send_z(chip)
        x_chip = send_x(chip)
        z_chip = after(z_chip, x_chip, split, partner_rows)
        mid = join(z_chip, swap_cores(z_chip))
        z_far = send_z(z_chip[1])
        far_chip = send_x(x_chip[1])[None]
        x_mid = send_x(mid)
        last = join(swap_cores(z_far), z_far)
        x_last = send_x(last)
        x_mid = after(x_mid, last, far_chip)
        far_mid = send_x(x_mid[:2])
        far_last = send_x(x_last[1])[None]
        brought = (x_chip, x_mid, x_last, far_chip)
        other = swap_cores(pick_for_partner(early_brought, place, partner_rows, brought))
        sums = multiply_early(*slots, (chip, mid, last, *brought), other)
        brought = after((far_mid, far_last), sums)
        other = swap_cores(pick_for_partner(late_brought, place, partner_rows, brought))
        return lax.all_to_all(multiply_late(*slots, brought, other, *sums), "row", 0, 0, tiled=True)

    image = first_image(product(vector), diagonal, vector)
    return finish(count, diagonal, product(image), image, vector)


def solution(mesh):
    return jax.shard_map(
        per_device,
        mesh=mesh,
        in_specs=(
            P(("row", "col"), None, None),
            P(("row", "col")),
            P(("row", "col")),
            P(("row", "col")),
            P(("row", "col")),
            P(("row", "col"), None),
        ),
        out_specs=(P(("row", "col"), None), P(("row", "col"), None), P()),
        check_vma=False,
    )
```

time: 223 us -> 199 us (0.89)
  starting transfers between devices: 87.9 us -> 39.1 us
  blocking collectives: 22.6 us -> 59.8 us
  waiting for transfers between devices: 81.5 us -> 75.9 us
  local copies, waits for them, and re-layouts: 5.62 us -> 2.75 us
  Pallas kernels: 20.5 us -> 17.9 us
    all_to_all x1 -> x2, blocking collectives: 22.6 us -> 59.8 us  [product(): lax.all_to_all(multiply_late(*slots, brought, other, *sums), 'row', 0, 0,...]
    ppermute x32 -> x16, starting transfers between devices: 54.5 us -> 19.3 us  [the longest x4 14.8 us: send_z(): return lax.ppermute(part, 'col', col_pairs(True))]
    all_to_all x3 -> x0, starting transfers between devices: 16.2 us -> none  [product(): terms.append(lax.all_to_all(partial, 'row', 0, 0, tiled=True))]
    ppermute x32 -> x16, waiting for transfers between devices: 78.4 us -> 64.4 us  [the longest x4 33.4 us: send_z(): return lax.ppermute(part, 'col', col_pairs(True))]
    ppermute x5 -> x11, waiting for transfers between devices: 3.13 us -> 11.6 us  [swap_cores(): return lax.ppermute(part, 'col', [(i, i ^ 1) for i in range(32)])]
    slice x17 -> x2, local copies, waits for them, and re-layouts: 3.06 us -> 0.07 us  [product(): far_mid = send_x(x_mid[:2])]
    ppermute x5 -> x11, starting transfers between devices: 17.2 us -> 19.8 us  [swap_cores(): return lax.ppermute(part, 'col', [(i, i ^ 1) for i in range(32)])]
    pallas_call x8, Pallas kernels: 18.3 us -> 15.8 us  [the longest x2 8.99 us: multiply_early(): pl.pallas_call(early_kernel, out_shape=shapes, in_specs=[smem()] * 3 + [v...]
  transfers between devices with their start and end apart: 40 -> 27, of which waited for: 17 -> 16; matrix products, arithmetic and copies ran while one was open for 1% -> 1% of each run, Pallas kernels for 9% -> 5%
where the time goes in v2:
time: 199 us
  waiting for transfers between devices  75.9 us (38%)
  blocking collectives  59.8 us (30%)
  starting transfers between devices  39.1 us (20%)
  Pallas kernels  17.9 us (9%)
  local copies, waits for them, and re-layouts  2.75 us (1%)
    all_to_all x2, blocking collectives, product(): lax.all_to_all(multiply_late(*slots, brought, other, *sums), 'row', 0, 0,...  59.8 us
    ppermute x4, waiting for transfers between devices, send_z(): return lax.ppermute(part, 'col', col_pairs(True))  33.4 us
    ppermute x12, waiting for transfers between devices, send_x(): return lax.ppermute(part, 'col', col_pairs(False))  30.9 us
    ppermute x11, starting transfers between devices, swap_cores(): return lax.ppermute(part, 'col', [(i, i ^ 1) for i in range(32)])  19.8 us
    ppermute x4, starting transfers between devices, send_z(): return lax.ppermute(part, 'col', col_pairs(True))  14.8 us
    ppermute x11, waiting for transfers between devices, swap_cores(): return lax.ppermute(part, 'col', [(i, i ^ 1) for i in range(32)])  11.6 us
    pallas_call x2, Pallas kernels, multiply_early(): pl.pallas_call(early_kernel, out_shape=shapes, in_specs=[smem()] * 3 + [v...  8.99 us
    ppermute x12, starting transfers between devices, send_x(): return lax.ppermute(part, 'col', col_pairs(False))  4.56 us
  transfers between devices with their start and end apart: 27, of which 16 were waited for; matrix products, arithmetic and copies ran while one was open for 1% of the time, Pallas kernels for 5%

profile of v2, /device:TPU:1, one launch (start us, length us, event | category | flops | bytes accessed | tf_op | source)
XLA Modules:
  0.0 199.1 jit_solution(18085006379128955573)
XLA Ops:
  0.6 3.3 %collective-permute-start = (f32[256,256]{1,0:T(8,128)}, f32[256,256]{1,0:T(8,128)S(1)}, u32[]{:S(2)}, u32[]{:S(2)}) collective-permute-start(f32[256,256]{1,0:T(8,128)} %vector.3), channel_id=1, source_target_pairs={{0,1},{1,0},{2,3},{3,2},{4,5},{5,4},{6,7},{7,6},{8,9},{9,8},{10,11... | collective-permute-start | bytes 786440 | tf_op jit(solution)/shard_map/ppermute | solution.py:273
  4.0 1.4 collective-permute-done
  5.3 1.0 pad_maximum_fusion.2.refs_0_
  6.3 0.8 collective-permute-start.2
  7.1 6.0 %collective-permute-start.1 = (f32[2,256,256]{2,1,0:T(8,128)S(1)}, f32[2,256,256]{2,1,0:T(8,128)S(1)}, u32[]{:S(2)}, u32[]{:S(2)}) collective-permute-start(f32[2,256,256]{2,1,0:T(8,128)S(1)} %pad_maximum_fusion.2.refs_0_), channel_id=1, source_target_pairs={{0,8},{1,25},{2,10},{3,27},{4,12},{5,29},{6,14},{7,31},{8,16},{9,1... | collective-permute-start | bytes 1572872 | tf_op jit(solution)/shard_map/ppermute | solution.py:277
  13.8 1.6 copy-done.4
  15.4 0.9 split_blocks.1.split
  16.3 8.6 %collective-permute-done.1 = f32[2,256,256]{2,1,0:T(8,128)S(1)} collective-permute-done((f32[2,256,256]{2,1,0:T(8,128)S(1)}, f32[2,256,256]{2,1,0:T(8,128)S(1)}, u32[]{:S(2)}, u32[]{:S(2)}) %collective-permute-start.1) | collective-permute-done | bytes 524320 | tf_op jit(solution)/shard_map/ppermute | solution.py:277
  24.9 4.1 %collective-permute-start.6 = (f32[256,256]{1,0:T(8,128)S(1)}, f32[256,256]{1,0:T(8,128)S(1)}, u32[]{:S(2)}, u32[]{:S(2)}) collective-permute-start(f32[256,256]{1,0:T(8,128)S(1)} %slice_bitcast_fusion.5), channel_id=1, source_target_pairs={{0,8},{1,25},{2,10},{3,27},{4,12},{5,29},{6,14},{7,31},{8,16},{9,1... | collective-permute-start | bytes 786440 | tf_op jit(solution)/shard_map/ppermute | solution.py:277
  29.1 0.9 collective-permute-start.5
  30.0 4.5 %collective-permute-done.6 = f32[256,256]{1,0:T(8,128)S(1)} collective-permute-done((f32[256,256]{1,0:T(8,128)S(1)}, f32[256,256]{1,0:T(8,128)S(1)}, u32[]{:S(2)}, u32[]{:S(2)}) %collective-permute-start.6) | collective-permute-done | bytes 262176 | tf_op jit(solution)/shard_map/ppermute | solution.py:277
  34.5 2.4 %collective-permute-start.7 = (f32[256,256]{1,0:T(8,128)S(1)}, f32[256,256]{1,0:T(8,128)S(1)}, u32[]{:S(2)}, u32[]{:S(2)}) collective-permute-start(f32[256,256]{1,0:T(8,128)S(1)} %collective-permute-done.6), channel_id=1, source_target_pairs={{0,1},{1,0},{2,3},{3,2},{4,5},{5,4},{6,7},{7,6},{8,9},{9,8},{10,11... | collective-permute-start | bytes 786440 | tf_op jit(solution)/shard_map/ppermute | solution.py:273
  37.0 1.2 collective-permute-done.7
  38.1 0.8 pad_maximum_fusion.3.refs_2_
  39.5 0.7 slice_bitcast_fusion.4
  40.2 1.1 collective-permute-start.8
  41.4 10.2 %collective-permute-done.8 = f32[256,256]{1,0:T(8,128)S(1)} collective-permute-done((f32[256,256]{1,0:T(8,128)}, f32[256,256]{1,0:T(8,128)S(1)}, u32[]{:S(2)}, u32[]{:S(2)}) %collective-permute-start.8) | collective-permute-done | bytes 262176 | tf_op jit(solution)/shard_map/ppermute | solution.py:281
  51.6 0.6 pick_for_partner.4
  52.3 1.3 collective-permute-start.12
  53.6 0.7 collective-permute-start.9
  54.4 1.6 collective-permute-done.12.refs_7_
  56.0 4.5 %multiply_early.2.sums = f32[8,256,256]{2,1,0:T(8,128)} custom-call(s32[3]{0:T(128)S(1)} %pad_add_fusion.place, s32[32]{0:T(128)S(1)} %copy-done.7, s32[32]{0:T(128)S(1)} %copy-done.8, bf16[32,128,256]{2,1,0:T(8,128)(2,1)} %copy-done, f32[2,256,256]{2,1,0:T(8,128)S(1)} %copy-done.6, f32[4,256,256]{2,1,0:T(8,128)S(1)} %constant_dynamic-update-slice_fusion.refs_1_, ...), custom_call_target="tpu_custom_call" | custom-call | tf_op jit(solution)/shard_map/multiply_early/pallas_call | solution.py:167
  60.5 4.3 %collective-permute-done.11 = f32[256,256]{1,0:T(8,128)S(1)} collective-permute-done((f32[256,256]{1,0:T(8,128)S(1)}, f32[256,256]{1,0:T(8,128)S(1)}, u32[]{:S(2)}, u32[]{:S(2)}) %collective-permute-start.11) | collective-permute-done | bytes 262176 | tf_op jit(solution)/shard_map/ppermute | solution.py:281
  64.8 0.6 pick_for_partner.5
  65.4 2.2 %collective-permute-start.13 = (f32[3,128,256]{2,1,0:T(8,128)S(1)}, f32[3,128,256]{2,1,0:T(8,128)S(1)}, u32[]{:S(2)}, u32[]{:S(2)}) collective-permute-start(f32[3,128,256]{2,1,0:T(8,128)S(1)} %pick_for_partner.5), channel_id=1, source_target_pairs={{0,1},{1,0},{2,3},{3,2},{4,5},{5,4},{6,7},{7,6},{8,9},{9,8},{10,11... | collective-permute-start | bytes 1179656 | tf_op jit(solution)/shard_map/ppermute | solution.py:273
  67.5 1.3 collective-permute-done.13.other
  68.9 2.1 %multiply_late.2 = f32[8,256,256]{2,1,0:T(8,128)S(1)} custom-call(s32[3]{0:T(128)S(1)} %pad_add_fusion.place, s32[32]{0:T(128)S(1)} %copy-done.7, s32[32]{0:T(128)S(1)} %copy-done.8, bf16[32,128,256]{2,1,0:T(8,128)(2,1)S(1)} %copy-done.1, f32[2,256,256]{2,1,0:T(8,128)S(1)} %collective-permute-done.9.refs_0_.mid, f32[1,256,256]{2,1,0:T(8,128)S(1)} %bitcast.34, ...), custom_call_target="tpu_custom_call" | custom-call | tf_op jit(solution)/shard_map/multiply_late/pallas_call | solution.py:193
  71.1 30.2 %all_to_all.10.terms = f32[8,256,256]{2,1,0:T(8,128)S(1)} all-to-all(f32[8,256,256]{2,1,0:T(8,128)S(1)} %multiply_late.2), channel_id=1, replica_groups=mesh['row'=8,'col'=32] {'row'}, dimensions={0} | all-to-all | bytes 4194304 | tf_op jit(solution)/shard_map/all_to_all | solution.py:316
  101.7 1.9 collective-permute-start.14
  103.6 1.2 collective-permute-done.14
  104.8 2.9 %collective-permute-start.15 = (f32[2,264,256]{2,1,0:T(8,128)S(1)}, f32[2,264,256]{2,1,0:T(8,128)S(1)}, u32[]{:S(2)}, u32[]{:S(2)}) collective-permute-start(f32[2,264,256]{2,1,0:T(8,128)S(1)} %pad_maximum_fusion.refs_0_), channel_id=1, source_target_pairs={{0,8},{1,25},{2,10},{3,27},{4,12},{5,29},{6,14},{7,31},{8,16},{9,1... | collective-permute-start | bytes 1622024 | tf_op jit(solution)/shard_map/ppermute | solution.py:277
  107.6 12.9 %collective-permute-done.15 = f32[2,264,256]{2,1,0:T(8,128)S(1)} collective-permute-done((f32[2,264,256]{2,1,0:T(8,128)S(1)}, f32[2,264,256]{2,1,0:T(8,128)S(1)}, u32[]{:S(2)}, u32[]{:S(2)}) %collective-permute-start.15) | collective-permute-done | bytes 540704 | tf_op jit(solution)/shard_map/ppermute | solution.py:277
  120.5 1.4 collective-permute-start.17
  121.9 1.8 collective-permute-start.19
  123.9 7.5 %collective-permute-done.19 = f32[264,256]{1,0:T(8,128)S(1)} collective-permute-done((f32[264,256]{1,0:T(8,128)S(1)}, f32[264,256]{1,0:T(8,128)S(1)}, u32[]{:S(2)}, u32[]{:S(2)}) %collective-permute-start.19) | collective-permute-done | bytes 270368 | tf_op jit(solution)/shard_map/ppermute | solution.py:277
  131.4 2.1 %collective-permute-start.20 = (f32[264,256]{1,0:T(8,128)S(1)}, f32[264,256]{1,0:T(8,128)S(1)}, u32[]{:S(2)}, u32[]{:S(2)}) collective-permute-start(f32[264,256]{1,0:T(8,128)S(1)} %collective-permute-done.19), channel_id=1, source_target_pairs={{0,1},{1,0},{2,3},{3,2},{4,5},{5,4},{6,7},{7,6},{8,9},{9,8},{10,11... | collective-permute-start | bytes 811016 | tf_op jit(solution)/shard_map/ppermute | solution.py:273
  133.5 1.2 collective-permute-done.20
  134.9 12.0 %collective-permute-done.21 = f32[264,256]{1,0:T(8,128)S(1)} collective-permute-done((f32[264,256]{1,0:T(8,128)S(1)}, f32[264,256]{1,0:T(8,128)S(1)}, u32[]{:S(2)}, u32[]{:S(2)}) %collective-permute-start.21) | collective-permute-done | bytes 270368 | tf_op jit(solution)/shard_map/ppermute | solution.py:281
  146.9 0.6 pick_for_partner.6
  147.5 3.0 %collective-permute-start.25 = (f32[9,136,256]{2,1,0:T(8,128)S(1)}, f32[9,136,256]{2,1,0:T(8,128)S(1)}, u32[]{:S(2)}, u32[]{:S(2)}) collective-permute-start(f32[9,136,256]{2,1,0:T(8,128)S(1)} %pick_for_partner.6), channel_id=1, source_target_pairs={{0,1},{1,0},{2,3},{3,2},{4,5},{5,4},{6,7},{7,6},{8,9},{9,8},{10,11... | collective-permute-start | bytes 3760136 | tf_op jit(solution)/shard_map/ppermute | solution.py:273
  150.8 2.3 %collective-permute-done.25.refs_7_ = f32[9,136,256]{2,1,0:T(8,128)S(1)} collective-permute-done((f32[9,136,256]{2,1,0:T(8,128)S(1)}, f32[9,136,256]{2,1,0:T(8,128)S(1)}, u32[]{:S(2)}, u32[]{:S(2)}) %collective-permute-start.25) | collective-permute-done | bytes 1253408 | tf_op jit(solution)/shard_map/ppermute | solution.py:273
  153.2 4.5 %multiply_early.3 = (f32[8,264,256]{2,1,0:T(8,128)}, f32[32,8,256]{2,1,0:T(8,128)S(1)}) custom-call(s32[3]{0:T(128)S(1)} %pad_add_fusion.place, s32[32]{0:T(128)S(1)} %copy-done.7, s32[32]{0:T(128)S(1)} %copy-done.8, bf16[32,128,256]{2,1,0:T(8,128)(2,1)} %copy-done, f32[2,264,256]{2,1,0:T(8,128)S(1)} %pad_maximum_fusion.refs_0_, ...), custom_call_target="tpu_custom_call" | custom-call | tf_op jit(solution)/shard_map/multiply_early/pallas_call | solution.py:167
  157.7 4.4 %collective-permute-done.24 = f32[264,256]{1,0:T(8,128)S(1)} collective-permute-done((f32[264,256]{1,0:T(8,128)S(1)}, f32[264,256]{1,0:T(8,128)S(1)}, u32[]{:S(2)}, u32[]{:S(2)}) %collective-permute-start.24) | collective-permute-done | bytes 270368 | tf_op jit(solution)/shard_map/ppermute | solution.py:281
  162.7 2.2 %collective-permute-start.26 = (f32[3,136,256]{2,1,0:T(8,128)S(1)}, f32[3,136,256]{2,1,0:T(8,128)S(1)}, u32[]{:S(2)}, u32[]{:S(2)}) collective-permute-start(f32[3,136,256]{2,1,0:T(8,128)S(1)} %pick_for_partner.7), channel_id=1, source_target_pairs={{0,1},{1,0},{2,3},{3,2},{4,5},{5,4},{6,7},{7,6},{8,9},{9,8},{10,11... | collective-permute-start | bytes 1253384 | tf_op jit(solution)/shard_map/ppermute | solution.py:273
  164.9 1.4 collective-permute-done.26.other
  166.3 2.2 %multiply_late.3 = f32[8,264,256]{2,1,0:T(8,128)S(1)} custom-call(s32[3]{0:T(128)S(1)} %pad_add_fusion.place, s32[32]{0:T(128)S(1)} %copy-done.7, s32[32]{0:T(128)S(1)} %copy-done.8, bf16[32,128,256]{2,1,0:T(8,128)(2,1)S(1)} %copy-done.2, f32[2,264,256]{2,1,0:T(8,128)S(1)} %collective-permute-done.22.refs_0_.mid, f32[1,264,256]{2,1,0:T(8,128)S(1)} %bitcast.30, ...), custom_call_target="tpu_custom_call" | custom-call | tf_op jit(solution)/shard_map/multiply_late/pallas_call | solution.py:193
  168.5 29.6 %all_to_all.11.terms = f32[8,264,256]{2,1,0:T(8,128)S(1)} all-to-all(f32[8,264,256]{2,1,0:T(8,128)S(1)} %multiply_late.3), channel_id=1, replica_groups=mesh['row'=8,'col'=32] {'row'}, dimensions={0} | all-to-all | bytes 4325376 | tf_op jit(solution)/shard_map/all_to_all | solution.py:316
  198.1 1.0 finish.1
  (57 shorter events, 2.6 us)
Async XLA Ops:
  0.6 4.7 %collective-permute-start = (f32[256,256]{1,0:T(8,128)}, f32[256,256]{1,0:T(8,128)S(1)}, u32[]{:S(2)}, u32[]{:S(2)}) collective-permute-start(f32[256,256]{1,0:T(8,128)} %vector.3), channel_id=1, source_target_pairs={{0,1},{1,0},{2,3},{3,2},{4,5},{5,4},{6,7},{7,6},{8,9},{9,8},{10,11... | collective-permute-start | bytes 786440 | tf_op jit(solution)/shard_map/ppermute | solution.py:273
  6.3 10.0 %copy-start.5 = (f32[2,256,256]{2,1,0:T(8,128)}, f32[2,256,256]{2,1,0:T(8,128)S(1)}, u32[]{:S(2)}) copy-start(f32[2,256,256]{2,1,0:T(8,128)S(1)} %pad_maximum_fusion.2.refs_0_) | copy-start | bytes 1572868
  6.3 10.0 %collective-permute-start.2 = (f32[2,256,256]{2,1,0:T(8,128)S(1)}, f32[2,256,256]{2,1,0:T(8,128)S(1)}, u32[]{:S(2)}, u32[]{:S(2)}) collective-permute-start(f32[2,256,256]{2,1,0:T(8,128)S(1)} %pad_maximum_fusion.2.refs_0_), channel_id=1, source_target_pairs={{0,2},{1,7},{2,4},{3,1},{4,6},{5,3},{6,0},{7,5},{8,10},{9,15},{10,... | collective-permute-start | bytes 1572872 | tf_op jit(solution)/shard_map/ppermute | solution.py:281
  7.1 17.8 %collective-permute-start.1 = (f32[2,256,256]{2,1,0:T(8,128)S(1)}, f32[2,256,256]{2,1,0:T(8,128)S(1)}, u32[]{:S(2)}, u32[]{:S(2)}) collective-permute-start(f32[2,256,256]{2,1,0:T(8,128)S(1)} %pad_maximum_fusion.2.refs_0_), channel_id=1, source_target_pairs={{0,8},{1,25},{2,10},{3,27},{4,12},{5,29},{6,14},{7,31},{8,16},{9,1... | collective-permute-start | bytes 1572872 | tf_op jit(solution)/shard_map/ppermute | solution.py:277
  13.2 3.1 %collective-permute-start.3 = (s32[32]{0:T(128)}, s32[32]{0:T(128)S(1)}, u32[]{:S(2)}, u32[]{:S(2)}) collective-permute-start(s32[32]{0:T(128)} %rows.7), channel_id=1, source_target_pairs={{0,1},{1,0},{2,3},{3,2},{4,5},{5,4},{6,7},{7,6},{8,9},{9,8},{10,11... | collective-permute-start | bytes 392 | tf_op jit(solution)/shard_map/ppermute | solution.py:273
  13.8 1.6 copy-start.4
  16.3 12.8 %copy-start = (bf16[32,128,256]{2,1,0:T(8,128)(2,1)}, bf16[32,128,256]{2,1,0:T(8,128)(2,1)S(1)}, u32[]{:S(2)}) copy-start(bf16[32,128,256]{2,1,0:T(8,128)(2,1)S(1)} %split_blocks.1.split) | copy-start | bytes 6291460
  24.9 4.2 %collective-permute-start.4 = (f32[2,256,256]{2,1,0:T(8,128)S(1)}, f32[2,256,256]{2,1,0:T(8,128)S(1)}, u32[]{:S(2)}, u32[]{:S(2)}) collective-permute-start(f32[2,256,256]{2,1,0:T(8,128)S(1)} %collective-permute-done.1), channel_id=1, source_target_pairs={{0,1},{1,0},{2,3},{3,2},{4,5},{5,4},{6,7},{7,6},{8,9},{9,8},{10,11... | collective-permute-start | bytes 1572872 | tf_op jit(solution)/shard_map/ppermute | solution.py:273
  24.9 9.6 %collective-permute-start.6 = (f32[256,256]{1,0:T(8,128)S(1)}, f32[256,256]{1,0:T(8,128)S(1)}, u32[]{:S(2)}, u32[]{:S(2)}) collective-permute-start(f32[256,256]{1,0:T(8,128)S(1)} %slice_bitcast_fusion.5), channel_id=1, source_target_pairs={{0,8},{1,25},{2,10},{3,27},{4,12},{5,29},{6,14},{7,31},{8,16},{9,1... | collective-permute-start | bytes 786440 | tf_op jit(solution)/shard_map/ppermute | solution.py:277
  29.1 22.5 %collective-permute-start.5 = (f32[4,256,256]{2,1,0:T(8,128)S(1)}, f32[4,256,256]{2,1,0:T(8,128)S(1)}, u32[]{:S(2)}, u32[]{:S(2)}) collective-permute-start(f32[4,256,256]{2,1,0:T(8,128)S(1)} %constant_dynamic-update-slice_fusion.refs_1_), channel_id=1, source_target_pairs={{0,2},{1,7},{2,4},{3,1},{4,6},{5,3},{6,0},{7,5},{8,10},{9,15},{10,... | collective-permute-start | bytes 3145736 | tf_op jit(solution)/shard_map/ppermute | solution.py:281
  34.5 3.6 %collective-permute-start.7 = (f32[256,256]{1,0:T(8,128)S(1)}, f32[256,256]{1,0:T(8,128)S(1)}, u32[]{:S(2)}, u32[]{:S(2)}) collective-permute-start(f32[256,256]{1,0:T(8,128)S(1)} %collective-permute-done.6), channel_id=1, source_target_pairs={{0,1},{1,0},{2,3},{3,2},{4,5},{5,4},{6,7},{7,6},{8,9},{9,8},{10,11... | collective-permute-start | bytes 786440 | tf_op jit(solution)/shard_map/ppermute | solution.py:273
  39.0 12.6 %collective-permute-start.10 = (f32[2,256,256]{2,1,0:T(8,128)}, f32[2,256,256]{2,1,0:T(8,128)S(1)}, u32[]{:S(2)}, u32[]{:S(2)}) collective-permute-start(f32[2,256,256]{2,1,0:T(8,128)} %pad_maximum_fusion.3.refs_2_), channel_id=1, source_target_pairs={{0,2},{1,7},{2,4},{3,1},{4,6},{5,3},{6,0},{7,5},{8,10},{9,15},{10,... | collective-permute-start | bytes 1572872 | tf_op jit(solution)/shard_map/ppermute | solution.py:281
  40.2 11.3 %collective-permute-start.8 = (f32[256,256]{1,0:T(8,128)}, f32[256,256]{1,0:T(8,128)S(1)}, u32[]{:S(2)}, u32[]{:S(2)}) collective-permute-start(f32[256,256]{1,0:T(8,128)} %slice_bitcast_fusion.4), channel_id=1, source_target_pairs={{0,2},{1,7},{2,4},{3,1},{4,6},{5,3},{6,0},{7,5},{8,10},{9,15},{10,... | collective-permute-start | bytes 786440 | tf_op jit(solution)/shard_map/ppermute | solution.py:281
  52.2 3.8 %copy-start.6 = (f32[2,256,256]{2,1,0:T(8,128)S(1)}, f32[2,256,256]{2,1,0:T(8,128)}, u32[]{:S(2)}) copy-start(f32[2,256,256]{2,1,0:T(8,128)} %copy-done.5) | copy-start | bytes 1572868
  52.2 3.8 %copy-start.7 = (s32[32]{0:T(128)S(1)}, s32[32]{0:T(128)}, u32[]{:S(2)}) copy-start(s32[32]{0:T(128)} %rows.7) | copy-start | bytes 388
  52.3 3.8 %copy-start.8 = (s32[32]{0:T(128)S(1)}, s32[32]{0:T(128)}, u32[]{:S(2)}) copy-start(s32[32]{0:T(128)} %cols.7) | copy-start | bytes 388
  52.3 3.7 %collective-permute-start.12 = (f32[9,128,256]{2,1,0:T(8,128)S(1)}, f32[9,128,256]{2,1,0:T(8,128)S(1)}, u32[]{:S(2)}, u32[]{:S(2)}) collective-permute-start(f32[9,128,256]{2,1,0:T(8,128)S(1)} %pick_for_partner.4), channel_id=1, source_target_pairs={{0,1},{1,0},{2,3},{3,2},{4,5},{5,4},{6,7},{7,6},{8,9},{9,8},{10,11... | collective-permute-start | bytes 3538952 | tf_op jit(solution)/shard_map/ppermute | solution.py:273
  53.6 11.2 %collective-permute-start.9 = (f32[2,256,256]{2,1,0:T(8,128)S(1)}, f32[2,256,256]{2,1,0:T(8,128)S(1)}, u32[]{:S(2)}, u32[]{:S(2)}) collective-permute-start(f32[2,256,256]{2,1,0:T(8,128)S(1)} %slice.26), channel_id=1, source_target_pairs={{0,2},{1,7},{2,4},{3,1},{4,6},{5,3},{6,0},{7,5},{8,10},{9,15},{10,... | collective-permute-start | bytes 1572872 | tf_op jit(solution)/shard_map/ppermute | solution.py:281
  54.3 10.5 %collective-permute-start.11 = (f32[256,256]{1,0:T(8,128)S(1)}, f32[256,256]{1,0:T(8,128)S(1)}, u32[]{:S(2)}, u32[]{:S(2)}) collective-permute-start(f32[256,256]{1,0:T(8,128)S(1)} %slice_bitcast_fusion.3), channel_id=1, source_target_pairs={{0,2},{1,7},{2,4},{3,1},{4,6},{5,3},{6,0},{7,5},{8,10},{9,15},{10,... | collective-permute-start | bytes 786440 | tf_op jit(solution)/shard_map/ppermute | solution.py:281
  56.0 12.9 %copy-start.1 = (bf16[32,128,256]{2,1,0:T(8,128)(2,1)S(1)}, bf16[32,128,256]{2,1,0:T(8,128)(2,1)}, u32[]{:S(2)}) copy-start(bf16[32,128,256]{2,1,0:T(8,128)(2,1)} %copy-done) | copy-start | bytes 6291460
  65.4 3.5 %collective-permute-start.13 = (f32[3,128,256]{2,1,0:T(8,128)S(1)}, f32[3,128,256]{2,1,0:T(8,128)S(1)}, u32[]{:S(2)}, u32[]{:S(2)}) collective-permute-start(f32[3,128,256]{2,1,0:T(8,128)S(1)} %pick_for_partner.5), channel_id=1, source_target_pairs={{0,1},{1,0},{2,3},{3,2},{4,5},{5,4},{6,7},{7,6},{8,9},{9,8},{10,11... | collective-permute-start | bytes 1179656 | tf_op jit(solution)/shard_map/ppermute | solution.py:273
  71.0 30.2 %copy-start.9 = (f32[256]{0:T(256)S(1)}, f32[256]{0:T(256)}, u32[]{:S(2)}) copy-start(f32[256]{0:T(256)} %param.10) | copy-start | bytes 3076
  71.0 30.3 %copy-start.3 = (f32[256,256]{1,0:T(8,128)S(1)}, f32[256,256]{1,0:T(8,128)}, u32[]{:S(2)}) copy-start(f32[256,256]{1,0:T(8,128)} %vector.3) | copy-start | bytes 786436
  101.7 3.1 %collective-permute-start.14 = (f32[264,256]{1,0:T(8,128)S(1)}, f32[264,256]{1,0:T(8,128)S(1)}, u32[]{:S(2)}, u32[]{:S(2)}) collective-permute-start(f32[264,256]{1,0:T(8,128)S(1)} %first_image.1.image), channel_id=1, source_target_pairs={{0,1},{1,0},{2,3},{3,2},{4,5},{5,4},{6,7},{7,6},{8,9},{9,8},{10,11... | collective-permute-start | bytes 811016 | tf_op jit(solution)/shard_map/ppermute | solution.py:273
  104.8 15.7 %collective-permute-start.15 = (f32[2,264,256]{2,1,0:T(8,128)S(1)}, f32[2,264,256]{2,1,0:T(8,128)S(1)}, u32[]{:S(2)}, u32[]{:S(2)}) collective-permute-start(f32[2,264,256]{2,1,0:T(8,128)S(1)} %pad_maximum_fusion.refs_0_), channel_id=1, source_target_pairs={{0,8},{1,25},{2,10},{3,27},{4,12},{5,29},{6,14},{7,31},{8,16},{9,1... | collective-permute-start | bytes 1622024 | tf_op jit(solution)/shard_map/ppermute | solution.py:277
  107.6 12.9 %collective-permute-start.16 = (f32[2,264,256]{2,1,0:T(8,128)S(1)}, f32[2,264,256]{2,1,0:T(8,128)S(1)}, u32[]{:S(2)}, u32[]{:S(2)}) collective-permute-start(f32[2,264,256]{2,1,0:T(8,128)S(1)} %pad_maximum_fusion.refs_0_), channel_id=1, source_target_pairs={{0,2},{1,7},{2,4},{3,1},{4,6},{5,3},{6,0},{7,5},{8,10},{9,15},{10,... | collective-permute-start | bytes 1622024 | tf_op jit(solution)/shard_map/ppermute | solution.py:281
  120.5 3.3 %collective-permute-start.17 = (f32[2,264,256]{2,1,0:T(8,128)S(1)}, f32[2,264,256]{2,1,0:T(8,128)S(1)}, u32[]{:S(2)}, u32[]{:S(2)}) collective-permute-start(f32[2,264,256]{2,1,0:T(8,128)S(1)} %collective-permute-done.15), channel_id=1, source_target_pairs={{0,1},{1,0},{2,3},{3,2},{4,5},{5,4},{6,7},{7,6},{8,9},{9,8},{10,11... | collective-permute-start | bytes 1622024 | tf_op jit(solution)/shard_map/ppermute | solution.py:273
  121.9 9.5 %collective-permute-start.19 = (f32[264,256]{1,0:T(8,128)S(1)}, f32[264,256]{1,0:T(8,128)S(1)}, u32[]{:S(2)}, u32[]{:S(2)}) collective-permute-start(f32[264,256]{1,0:T(8,128)S(1)} %slice_bitcast_fusion.2), channel_id=1, source_target_pairs={{0,8},{1,25},{2,10},{3,27},{4,12},{5,29},{6,14},{7,31},{8,16},{9,1... | collective-permute-start | bytes 811016 | tf_op jit(solution)/shard_map/ppermute | solution.py:277
  123.8 23.1 %collective-permute-start.18 = (f32[4,264,256]{2,1,0:T(8,128)S(1)}, f32[4,264,256]{2,1,0:T(8,128)S(1)}, u32[]{:S(2)}, u32[]{:S(2)}) collective-permute-start(f32[4,264,256]{2,1,0:T(8,128)S(1)} %constant_dynamic-update-slice_fusion.2.refs_1_), channel_id=1, source_target_pairs={{0,2},{1,7},{2,4},{3,1},{4,6},{5,3},{6,0},{7,5},{8,10},{9,15},{10,... | collective-permute-start | bytes 3244040 | tf_op jit(solution)/shard_map/ppermute | solution.py:281
  131.4 3.3 %collective-permute-start.20 = (f32[264,256]{1,0:T(8,128)S(1)}, f32[264,256]{1,0:T(8,128)S(1)}, u32[]{:S(2)}, u32[]{:S(2)}) collective-permute-start(f32[264,256]{1,0:T(8,128)S(1)} %collective-permute-done.19), channel_id=1, source_target_pairs={{0,1},{1,0},{2,3},{3,2},{4,5},{5,4},{6,7},{7,6},{8,9},{9,8},{10,11... | collective-permute-start | bytes 811016 | tf_op jit(solution)/shard_map/ppermute | solution.py:273
  134.7 12.2 %collective-permute-start.23 = (f32[2,264,256]{2,1,0:T(8,128)S(1)}, f32[2,264,256]{2,1,0:T(8,128)S(1)}, u32[]{:S(2)}, u32[]{:S(2)}) collective-permute-start(f32[2,264,256]{2,1,0:T(8,128)S(1)} %pad_maximum_fusion.1.refs_2_), channel_id=1, source_target_pairs={{0,2},{1,7},{2,4},{3,1},{4,6},{5,3},{6,0},{7,5},{8,10},{9,15},{10,... | collective-permute-start | bytes 1622024 | tf_op jit(solution)/shard_map/ppermute | solution.py:281
  134.8 12.1 %collective-permute-start.21 = (f32[264,256]{1,0:T(8,128)S(1)}, f32[264,256]{1,0:T(8,128)S(1)}, u32[]{:S(2)}, u32[]{:S(2)}) collective-permute-start(f32[264,256]{1,0:T(8,128)S(1)} %slice_bitcast_fusion.1), channel_id=1, source_target_pairs={{0,2},{1,7},{2,4},{3,1},{4,6},{5,3},{6,0},{7,5},{8,10},{9,15},{10,... | collective-permute-start | bytes 811016 | tf_op jit(solution)/shard_map/ppermute | solution.py:281
  147.5 5.6 %collective-permute-start.25 = (f32[9,136,256]{2,1,0:T(8,128)S(1)}, f32[9,136,256]{2,1,0:T(8,128)S(1)}, u32[]{:S(2)}, u32[]{:S(2)}) collective-permute-start(f32[9,136,256]{2,1,0:T(8,128)S(1)} %pick_for_partner.6), channel_id=1, source_target_pairs={{0,1},{1,0},{2,3},{3,2},{4,5},{5,4},{6,7},{7,6},{8,9},{9,8},{10,11... | collective-permute-start | bytes 3760136 | tf_op jit(solution)/shard_map/ppermute | solution.py:273
  150.6 11.5 %collective-permute-start.22 = (f32[2,264,256]{2,1,0:T(8,128)S(1)}, f32[2,264,256]{2,1,0:T(8,128)S(1)}, u32[]{:S(2)}, u32[]{:S(2)}) collective-permute-start(f32[2,264,256]{2,1,0:T(8,128)S(1)} %slice.30), channel_id=1, source_target_pairs={{0,2},{1,7},{2,4},{3,1},{4,6},{5,3},{6,0},{7,5},{8,10},{9,15},{10,... | collective-permute-start | bytes 1622024 | tf_op jit(solution)/shard_map/ppermute | solution.py:281
  150.7 11.4 %collective-permute-start.24 = (f32[264,256]{1,0:T(8,128)S(1)}, f32[264,256]{1,0:T(8,128)S(1)}, u32[]{:S(2)}, u32[]{:S(2)}) collective-permute-start(f32[264,256]{1,0:T(8,128)S(1)} %slice_bitcast_fusion), channel_id=1, source_target_pairs={{0,2},{1,7},{2,4},{3,1},{4,6},{5,3},{6,0},{7,5},{8,10},{9,15},{10,... | collective-permute-start | bytes 811016 | tf_op jit(solution)/shard_map/ppermute | solution.py:281
  153.2 13.1 %copy-start.2 = (bf16[32,128,256]{2,1,0:T(8,128)(2,1)S(1)}, bf16[32,128,256]{2,1,0:T(8,128)(2,1)}, u32[]{:S(2)}) copy-start(bf16[32,128,256]{2,1,0:T(8,128)(2,1)} %copy-done) | copy-start | bytes 6291460
  162.7 3.6 %collective-permute-start.26 = (f32[3,136,256]{2,1,0:T(8,128)S(1)}, f32[3,136,256]{2,1,0:T(8,128)S(1)}, u32[]{:S(2)}, u32[]{:S(2)}) collective-permute-start(f32[3,136,256]{2,1,0:T(8,128)S(1)} %pick_for_partner.7), channel_id=1, source_target_pairs={{0,1},{1,0},{2,3},{3,2},{4,5},{5,4},{6,7},{7,6},{8,9},{9,8},{10,11... | collective-permute-start | bytes 1253384 | tf_op jit(solution)/shard_map/ppermute | solution.py:273

commit v3 on v2

--- a/solution.py
+++ b/solution.py
@@ -295,17 +295,18 @@
     slots = (place, block_row, block_col, split)
 
     def product(own):
-        chip = join(swap_cores(own), own)
-        z_chip = send_z(chip)
+        other = swap_cores(own)
+        z_own, z_other = send_z(own), send_z(other)
+        chip = join(other, own)
         x_chip = send_x(chip)
-        z_chip = after(z_chip, x_chip, split, partner_rows)
+        far_chip = send_x(x_chip[1])[None]
+        z_chip = after(join(z_other, z_own), far_chip, split, partner_rows)
         mid = join(z_chip, swap_cores(z_chip))
-        z_far = send_z(z_chip[1])
-        far_chip = send_x(x_chip[1])[None]
+        z_far = send_z(z_own)
         x_mid = send_x(mid)
         last = join(swap_cores(z_far), z_far)
         x_last = send_x(last)
-        x_mid = after(x_mid, last, far_chip)
+        x_mid = after(x_mid, last)
         far_mid = send_x(x_mid[:2])
         far_last = send_x(x_last[1])[None]
         brought = (x_chip, x_mid, x_last, far_chip)

time: 199 us -> 196 us (0.985)
  waiting for transfers between devices: 75.9 us -> 65 us
  starting transfers between devices: 39.1 us -> 47.2 us
    ppermute x4 -> x6, waiting for transfers between devices: 33.4 us -> 22 us  [send_z(): return lax.ppermute(part, 'col', col_pairs(True))]
    ppermute x12, starting transfers between devices: 4.56 us -> 9.03 us  [send_x(): return lax.ppermute(part, 'col', col_pairs(False))]
    ppermute x4 -> x6, starting transfers between devices: 14.8 us -> 18.5 us  [send_z(): return lax.ppermute(part, 'col', col_pairs(True))]
  transfers between devices with their start and end apart: 27 -> 29, of which waited for: 16 -> 21; matrix products, arithmetic and copies ran while one was open for 1% -> 1% of each run, Pallas kernels for 5% -> 5%
where the time goes in v3:
time: 196 us
  waiting for transfers between devices  65 us (33%)
  blocking collectives  60.2 us (31%)
  starting transfers between devices  47.2 us (24%)
  Pallas kernels  17.9 us (9%)
  other arithmetic  2.09 us (1%)
  local copies, waits for them, and re-layouts  2.01 us (1%)
    all_to_all x2, blocking collectives, product(): lax.all_to_all(multiply_late(*slots, brought, other, *sums), 'row', 0, 0,...  60.2 us
    ppermute x12, waiting for transfers between devices, send_x(): return lax.ppermute(part, 'col', col_pairs(False))  31.6 us
    ppermute x6, waiting for transfers between devices, send_z(): return lax.ppermute(part, 'col', col_pairs(True))  22 us
    ppermute x11, starting transfers between devices, swap_cores(): return lax.ppermute(part, 'col', [(i, i ^ 1) for i in range(32)])  19.7 us
    ppermute x6, starting transfers between devices, send_z(): return lax.ppermute(part, 'col', col_pairs(True))  18.5 us
    ppermute x11, waiting for transfers between devices, swap_cores(): return lax.ppermute(part, 'col', [(i, i ^ 1) for i in range(32)])  11.4 us
    ppermute x12, starting transfers between devices, send_x(): return lax.ppermute(part, 'col', col_pairs(False))  9.03 us
    pallas_call x2, Pallas kernels, multiply_early(): pl.pallas_call(early_kernel, out_shape=shapes, in_specs=[smem()] * 3 + [v...  8.98 us
  transfers between devices with their start and end apart: 29, of which 21 were waited for; matrix products, arithmetic and copies ran while one was open for 1% of the time, Pallas kernels for 5%

profile of v3, /device:TPU:1, one launch (start us, length us, event | category | flops | bytes accessed | tf_op | source)
XLA Modules:
  0.0 196.0 jit_solution(3847672222629508079)
XLA Ops:
  0.6 3.3 %collective-permute-start = (f32[256,256]{1,0:T(8,128)}, f32[256,256]{1,0:T(8,128)S(1)}, u32[]{:S(2)}, u32[]{:S(2)}) collective-permute-start(f32[256,256]{1,0:T(8,128)} %vector.3), channel_id=1, source_target_pairs={{0,1},{1,0},{2,3},{3,2},{4,5},{5,4},{6,7},{7,6},{8,9},{9,8},{10,11... | collective-permute-start | bytes 786440 | tf_op jit(solution)/shard_map/ppermute | solution.py:273
  4.0 1.4 collective-permute-done
  5.3 1.0 pad_maximum_fusion.4.refs_0_
  7.2 6.0 %collective-permute-start.2 = (f32[256,256]{1,0:T(8,128)}, f32[256,256]{1,0:T(8,128)S(1)}, u32[]{:S(2)}, u32[]{:S(2)}) collective-permute-start(f32[256,256]{1,0:T(8,128)} %vector.3), channel_id=1, source_target_pairs={{0,8},{1,25},{2,10},{3,27},{4,12},{5,29},{6,14},{7,31},{8,16},{9,1... | collective-permute-start | bytes 786440 | tf_op jit(solution)/shard_map/ppermute | solution.py:277
  13.2 1.2 collective-permute-start.1
  14.8 2.0 %collective-permute-start.4 = (f32[256,256]{1,0:T(8,128)S(1)}, f32[256,256]{1,0:T(8,128)S(1)}, u32[]{:S(2)}, u32[]{:S(2)}) collective-permute-start(f32[256,256]{1,0:T(8,128)S(1)} %slice_bitcast_fusion.3), channel_id=1, source_target_pairs={{0,2},{1,7},{2,4},{3,1},{4,6},{5,3},{6,0},{7,5},{8,10},{9,15},{10,... | collective-permute-start | bytes 786440 | tf_op jit(solution)/shard_map/ppermute | solution.py:281
  18.1 1.6 copy-done.4
  19.6 0.9 split_blocks.1.split
  20.5 4.6 %collective-permute-done.1 = f32[256,256]{1,0:T(8,128)S(1)} collective-permute-done((f32[256,256]{1,0:T(8,128)S(1)}, f32[256,256]{1,0:T(8,128)S(1)}, u32[]{:S(2)}, u32[]{:S(2)}) %collective-permute-start.1) | collective-permute-done | bytes 262176 | tf_op jit(solution)/shard_map/ppermute | solution.py:277
  25.3 4.1 %collective-permute-start.8 = (f32[256,256]{1,0:T(8,128)S(1)}, f32[256,256]{1,0:T(8,128)S(1)}, u32[]{:S(2)}, u32[]{:S(2)}) collective-permute-start(f32[256,256]{1,0:T(8,128)S(1)} %collective-permute-done.2), channel_id=1, source_target_pairs={{0,8},{1,25},{2,10},{3,27},{4,12},{5,29},{6,14},{7,31},{8,16},{9,1... | collective-permute-start | bytes 786440 | tf_op jit(solution)/shard_map/ppermute | solution.py:277
  30.3 5.2 %collective-permute-done.8 = f32[256,256]{1,0:T(8,128)S(1)} collective-permute-done((f32[256,256]{1,0:T(8,128)S(1)}, f32[256,256]{1,0:T(8,128)S(1)}, u32[]{:S(2)}, u32[]{:S(2)}) %collective-permute-start.8) | collective-permute-done | bytes 262176 | tf_op jit(solution)/shard_map/ppermute | solution.py:277
  35.5 1.5 collective-permute-start.9
  37.1 1.2 collective-permute-done.9
  39.9 3.6 %collective-permute-done.7.refs_1_.refs_4_ = f32[4,256,256]{2,1,0:T(8,128)S(1)} collective-permute-done((f32[4,256,256]{2,1,0:T(8,128)S(1)}, f32[4,256,256]{2,1,0:T(8,128)S(1)}, u32[]{:S(2)}, u32[]{:S(2)}) %collective-permute-start.7) | collective-permute-done | bytes 1048608 | tf_op jit(solution)/shard_map/ppermute | solution.py:281
  43.5 5.6 %collective-permute-done.11.refs_2_.refs_5_ = f32[2,256,256]{2,1,0:T(8,128)S(1)} collective-permute-done((f32[2,256,256]{2,1,0:T(8,128)}, f32[2,256,256]{2,1,0:T(8,128)S(1)}, u32[]{:S(2)}, u32[]{:S(2)}) %collective-permute-start.11) | collective-permute-done | bytes 524320 | tf_op jit(solution)/shard_map/ppermute | solution.py:281
  49.8 1.0 collective-permute-start.13
  51.8 1.4 collective-permute-done.13.refs_7_
  53.3 4.5 %multiply_early.2.sums = f32[8,256,256]{2,1,0:T(8,128)} custom-call(s32[3]{0:T(128)S(1)} %pad_add_fusion.place, s32[32]{0:T(128)S(1)} %copy-done.7, s32[32]{0:T(128)S(1)} %copy-done.8, bf16[32,128,256]{2,1,0:T(8,128)(2,1)} %copy-done, f32[2,256,256]{2,1,0:T(8,128)S(1)} %copy-done.6, f32[4,256,256]{2,1,0:T(8,128)S(1)} %constant_dynamic-update-slice_fusion.refs_1_, ...), custom_call_target="tpu_custom_call" | custom-call | tf_op jit(solution)/shard_map/multiply_early/pallas_call | solution.py:167
  57.7 4.3 %collective-permute-done.12 = f32[256,256]{1,0:T(8,128)S(1)} collective-permute-done((f32[256,256]{1,0:T(8,128)S(1)}, f32[256,256]{1,0:T(8,128)S(1)}, u32[]{:S(2)}, u32[]{:S(2)}) %collective-permute-start.12) | collective-permute-done | bytes 262176 | tf_op jit(solution)/shard_map/ppermute | solution.py:281
  62.6 2.4 %collective-permute-start.14 = (f32[3,128,256]{2,1,0:T(8,128)S(1)}, f32[3,128,256]{2,1,0:T(8,128)S(1)}, u32[]{:S(2)}, u32[]{:S(2)}) collective-permute-start(f32[3,128,256]{2,1,0:T(8,128)S(1)} %pick_for_partner.5), channel_id=1, source_target_pairs={{0,1},{1,0},{2,3},{3,2},{4,5},{5,4},{6,7},{7,6},{8,9},{9,8},{10,11... | collective-permute-start | bytes 1179656 | tf_op jit(solution)/shard_map/ppermute | solution.py:273
  65.0 1.3 collective-permute-done.14.other
  66.3 2.1 %multiply_late.2 = f32[8,256,256]{2,1,0:T(8,128)S(1)} custom-call(s32[3]{0:T(128)S(1)} %pad_add_fusion.place, s32[32]{0:T(128)S(1)} %copy-done.7, s32[32]{0:T(128)S(1)} %copy-done.8, bf16[32,128,256]{2,1,0:T(8,128)(2,1)S(1)} %copy-done.1, f32[2,256,256]{2,1,0:T(8,128)S(1)} %collective-permute-done.10.refs_0_.mid, f32[1,256,256]{2,1,0:T(8,128)S(1)} %bitcast.34, ...), custom_call_target="tpu_custom_call" | custom-call | tf_op jit(solution)/shard_map/multiply_late/pallas_call | solution.py:193
  68.5 30.5 %all_to_all.10.terms = f32[8,256,256]{2,1,0:T(8,128)S(1)} all-to-all(f32[8,256,256]{2,1,0:T(8,128)S(1)} %multiply_late.2), channel_id=1, replica_groups=mesh['row'=8,'col'=32] {'row'}, dimensions={0} | all-to-all | bytes 4194304 | tf_op jit(solution)/shard_map/all_to_all | solution.py:317
  99.4 1.9 collective-permute-start.15
  101.3 1.2 collective-permute-done.15
  102.6 3.0 %collective-permute-start.17 = (f32[264,256]{1,0:T(8,128)S(1)}, f32[264,256]{1,0:T(8,128)S(1)}, u32[]{:S(2)}, u32[]{:S(2)}) collective-permute-start(f32[264,256]{1,0:T(8,128)S(1)} %first_image.1.image), channel_id=1, source_target_pairs={{0,8},{1,25},{2,10},{3,27},{4,12},{5,29},{6,14},{7,31},{8,16},{9,1... | collective-permute-start | bytes 811016 | tf_op jit(solution)/shard_map/ppermute | solution.py:277
  105.6 1.3 collective-permute-start.16
  106.9 4.2 %collective-permute-done.18.refs_0_.refs_3_ = f32[2,264,256]{2,1,0:T(8,128)S(1)} collective-permute-done((f32[2,264,256]{2,1,0:T(8,128)S(1)}, f32[2,264,256]{2,1,0:T(8,128)S(1)}, u32[]{:S(2)}, u32[]{:S(2)}) %collective-permute-start.18) | collective-permute-done | bytes 540704 | tf_op jit(solution)/shard_map/ppermute | solution.py:281
  111.1 1.3 collective-permute-start.19
  112.4 3.0 %collective-permute-done.17 = f32[264,256]{1,0:T(8,128)S(1)} collective-permute-done((f32[264,256]{1,0:T(8,128)S(1)}, f32[264,256]{1,0:T(8,128)S(1)}, u32[]{:S(2)}, u32[]{:S(2)}) %collective-permute-start.17) | collective-permute-done | bytes 270368 | tf_op jit(solution)/shard_map/ppermute | solution.py:277
  115.4 2.9 %collective-permute-done.16 = f32[264,256]{1,0:T(8,128)S(1)} collective-permute-done((f32[264,256]{1,0:T(8,128)S(1)}, f32[264,256]{1,0:T(8,128)S(1)}, u32[]{:S(2)}, u32[]{:S(2)}) %collective-permute-start.16) | collective-permute-done | bytes 270368 | tf_op jit(solution)/shard_map/ppermute | solution.py:277
  118.4 3.0 %collective-permute-start.20 = (f32[2,264,256]{2,1,0:T(8,128)S(1)}, f32[2,264,256]{2,1,0:T(8,128)S(1)}, u32[]{:S(2)}, u32[]{:S(2)}) collective-permute-start(f32[2,264,256]{2,1,0:T(8,128)S(1)} %pad_maximum_fusion), channel_id=1, source_target_pairs={{0,1},{1,0},{2,3},{3,2},{4,5},{5,4},{6,7},{7,6},{8,9},{9,8},{10,11... | collective-permute-start | bytes 1622024 | tf_op jit(solution)/shard_map/ppermute | solution.py:273
  121.3 2.9 %collective-permute-start.22 = (f32[264,256]{1,0:T(8,128)S(1)}, f32[264,256]{1,0:T(8,128)S(1)}, u32[]{:S(2)}, u32[]{:S(2)}) collective-permute-start(f32[264,256]{1,0:T(8,128)S(1)} %collective-permute-done.17), channel_id=1, source_target_pairs={{0,8},{1,25},{2,10},{3,27},{4,12},{5,29},{6,14},{7,31},{8,16},{9,1... | collective-permute-start | bytes 811016 | tf_op jit(solution)/shard_map/ppermute | solution.py:277
  124.8 6.4 %collective-permute-done.22 = f32[264,256]{1,0:T(8,128)S(1)} collective-permute-done((f32[264,256]{1,0:T(8,128)S(1)}, f32[264,256]{1,0:T(8,128)S(1)}, u32[]{:S(2)}, u32[]{:S(2)}) %collective-permute-start.22) | collective-permute-done | bytes 270368 | tf_op jit(solution)/shard_map/ppermute | solution.py:277
  131.1 1.5 collective-permute-start.23
  132.6 1.2 collective-permute-done.23
  133.8 1.7 collective-permute-start.25
  135.5 3.2 %collective-permute-done.21.refs_1_.refs_4_ = f32[4,264,256]{2,1,0:T(8,128)S(1)} collective-permute-done((f32[4,264,256]{2,1,0:T(8,128)S(1)}, f32[4,264,256]{2,1,0:T(8,128)S(1)}, u32[]{:S(2)}, u32[]{:S(2)}) %collective-permute-start.21) | collective-permute-done | bytes 1081376 | tf_op jit(solution)/shard_map/ppermute | solution.py:281
  138.7 5.8 %collective-permute-done.25.refs_2_.refs_5_ = f32[2,264,256]{2,1,0:T(8,128)S(1)} collective-permute-done((f32[2,264,256]{2,1,0:T(8,128)S(1)}, f32[2,264,256]{2,1,0:T(8,128)S(1)}, u32[]{:S(2)}, u32[]{:S(2)}) %collective-permute-start.25) | collective-permute-done | bytes 540704 | tf_op jit(solution)/shard_map/ppermute | solution.py:281
  145.1 2.3 %collective-permute-start.27 = (f32[9,136,256]{2,1,0:T(8,128)S(1)}, f32[9,136,256]{2,1,0:T(8,128)S(1)}, u32[]{:S(2)}, u32[]{:S(2)}) collective-permute-start(f32[9,136,256]{2,1,0:T(8,128)S(1)} %pick_for_partner.6), channel_id=1, source_target_pairs={{0,1},{1,0},{2,3},{3,2},{4,5},{5,4},{6,7},{7,6},{8,9},{9,8},{10,11... | collective-permute-start | bytes 3760136 | tf_op jit(solution)/shard_map/ppermute | solution.py:273
  147.6 2.3 %collective-permute-done.27.refs_7_ = f32[9,136,256]{2,1,0:T(8,128)S(1)} collective-permute-done((f32[9,136,256]{2,1,0:T(8,128)S(1)}, f32[9,136,256]{2,1,0:T(8,128)S(1)}, u32[]{:S(2)}, u32[]{:S(2)}) %collective-permute-start.27) | collective-permute-done | bytes 1253408 | tf_op jit(solution)/shard_map/ppermute | solution.py:273
  150.0 4.5 %multiply_early.3 = (f32[8,264,256]{2,1,0:T(8,128)}, f32[32,8,256]{2,1,0:T(8,128)S(1)}) custom-call(s32[3]{0:T(128)S(1)} %pad_add_fusion.place, s32[32]{0:T(128)S(1)} %copy-done.7, s32[32]{0:T(128)S(1)} %copy-done.8, bf16[32,128,256]{2,1,0:T(8,128)(2,1)} %copy-done, f32[2,264,256]{2,1,0:T(8,128)S(1)} %pad_maximum_fusion.1.refs_0_, ...), custom_call_target="tpu_custom_call" | custom-call | tf_op jit(solution)/shard_map/multiply_early/pallas_call | solution.py:167
  154.5 4.4 %collective-permute-done.26 = f32[264,256]{1,0:T(8,128)S(1)} collective-permute-done((f32[264,256]{1,0:T(8,128)S(1)}, f32[264,256]{1,0:T(8,128)S(1)}, u32[]{:S(2)}, u32[]{:S(2)}) %collective-permute-start.26) | collective-permute-done | bytes 270368 | tf_op jit(solution)/shard_map/ppermute | solution.py:281
  159.5 2.2 %collective-permute-start.28 = (f32[3,136,256]{2,1,0:T(8,128)S(1)}, f32[3,136,256]{2,1,0:T(8,128)S(1)}, u32[]{:S(2)}, u32[]{:S(2)}) collective-permute-start(f32[3,136,256]{2,1,0:T(8,128)S(1)} %pick_for_partner.7), channel_id=1, source_target_pairs={{0,1},{1,0},{2,3},{3,2},{4,5},{5,4},{6,7},{7,6},{8,9},{9,8},{10,11... | collective-permute-start | bytes 1253384 | tf_op jit(solution)/shard_map/ppermute | solution.py:273
  161.7 1.4 collective-permute-done.28.other
  163.1 2.2 %multiply_late.3 = f32[8,264,256]{2,1,0:T(8,128)S(1)} custom-call(s32[3]{0:T(128)S(1)} %pad_add_fusion.place, s32[32]{0:T(128)S(1)} %copy-done.7, s32[32]{0:T(128)S(1)} %copy-done.8, bf16[32,128,256]{2,1,0:T(8,128)(2,1)S(1)} %copy-done.2, f32[2,264,256]{2,1,0:T(8,128)S(1)} %collective-permute-done.24.refs_0_.mid, f32[1,264,256]{2,1,0:T(8,128)S(1)} %bitcast.30, ...), custom_call_target="tpu_custom_call" | custom-call | tf_op jit(solution)/shard_map/multiply_late/pallas_call | solution.py:193
  165.3 29.7 %all_to_all.11.terms = f32[8,264,256]{2,1,0:T(8,128)S(1)} all-to-all(f32[8,264,256]{2,1,0:T(8,128)S(1)} %multiply_late.3), channel_id=1, replica_groups=mesh['row'=8,'col'=32] {'row'}, dimensions={0} | all-to-all | bytes 4325376 | tf_op jit(solution)/shard_map/all_to_all | solution.py:317
  195.0 1.0 finish.1
  (61 shorter events, 9.4 us)
Async XLA Ops:
  0.6 16.2 %copy-start.7 = (s32[32]{0:T(128)S(1)}, s32[32]{0:T(128)}, u32[]{:S(2)}) copy-start(s32[32]{0:T(128)} %rows.7) | copy-start | bytes 388
  0.6 4.7 %collective-permute-start = (f32[256,256]{1,0:T(8,128)}, f32[256,256]{1,0:T(8,128)S(1)}, u32[]{:S(2)}, u32[]{:S(2)}) collective-permute-start(f32[256,256]{1,0:T(8,128)} %vector.3), channel_id=1, source_target_pairs={{0,1},{1,0},{2,3},{3,2},{4,5},{5,4},{6,7},{7,6},{8,9},{9,8},{10,11... | collective-permute-start | bytes 786440 | tf_op jit(solution)/shard_map/ppermute | solution.py:273
  6.3 11.1 %copy-start.5 = (f32[2,256,256]{2,1,0:T(8,128)}, f32[2,256,256]{2,1,0:T(8,128)S(1)}, u32[]{:S(2)}) copy-start(f32[2,256,256]{2,1,0:T(8,128)S(1)} %pad_maximum_fusion.4.refs_0_) | copy-start | bytes 1572868
  6.3 8.4 %collective-permute-start.3 = (f32[2,256,256]{2,1,0:T(8,128)S(1)}, f32[2,256,256]{2,1,0:T(8,128)S(1)}, u32[]{:S(2)}, u32[]{:S(2)}) collective-permute-start(f32[2,256,256]{2,1,0:T(8,128)S(1)} %pad_maximum_fusion.4.refs_0_), channel_id=1, source_target_pairs={{0,2},{1,7},{2,4},{3,1},{4,6},{5,3},{6,0},{7,5},{8,10},{9,15},{10,... | collective-permute-start | bytes 1572872 | tf_op jit(solution)/shard_map/ppermute | solution.py:281
  7.2 13.4 %collective-permute-start.2 = (f32[256,256]{1,0:T(8,128)}, f32[256,256]{1,0:T(8,128)S(1)}, u32[]{:S(2)}, u32[]{:S(2)}) collective-permute-start(f32[256,256]{1,0:T(8,128)} %vector.3), channel_id=1, source_target_pairs={{0,8},{1,25},{2,10},{3,27},{4,12},{5,29},{6,14},{7,31},{8,16},{9,1... | collective-permute-start | bytes 786440 | tf_op jit(solution)/shard_map/ppermute | solution.py:277
  13.2 12.0 %collective-permute-start.1 = (f32[256,256]{1,0:T(8,128)S(1)}, f32[256,256]{1,0:T(8,128)S(1)}, u32[]{:S(2)}, u32[]{:S(2)}) collective-permute-start(f32[256,256]{1,0:T(8,128)S(1)} %collective-permute-done), channel_id=1, source_target_pairs={{0,8},{1,25},{2,10},{3,27},{4,12},{5,29},{6,14},{7,31},{8,16},{9,1... | collective-permute-start | bytes 786440 | tf_op jit(solution)/shard_map/ppermute | solution.py:277
  14.8 10.4 %collective-permute-start.4 = (f32[256,256]{1,0:T(8,128)S(1)}, f32[256,256]{1,0:T(8,128)S(1)}, u32[]{:S(2)}, u32[]{:S(2)}) collective-permute-start(f32[256,256]{1,0:T(8,128)S(1)} %slice_bitcast_fusion.3), channel_id=1, source_target_pairs={{0,2},{1,7},{2,4},{3,1},{4,6},{5,3},{6,0},{7,5},{8,10},{9,15},{10,... | collective-permute-start | bytes 786440 | tf_op jit(solution)/shard_map/ppermute | solution.py:281
  16.8 8.4 %collective-permute-start.5 = (s32[32]{0:T(128)S(1)}, s32[32]{0:T(128)S(1)}, u32[]{:S(2)}, u32[]{:S(2)}) collective-permute-start(s32[32]{0:T(128)S(1)} %copy-done.7), channel_id=1, source_target_pairs={{0,1},{1,0},{2,3},{3,2},{4,5},{5,4},{6,7},{7,6},{8,9},{9,8},{10,11... | collective-permute-start | bytes 392 | tf_op jit(solution)/shard_map/ppermute | solution.py:273
  18.0 1.6 copy-start.4
  20.5 9.0 %copy-start = (bf16[32,128,256]{2,1,0:T(8,128)(2,1)}, bf16[32,128,256]{2,1,0:T(8,128)(2,1)S(1)}, u32[]{:S(2)}) copy-start(bf16[32,128,256]{2,1,0:T(8,128)(2,1)S(1)} %split_blocks.1.split) | copy-start | bytes 6291460
  25.2 4.2 %collective-permute-start.6 = (f32[2,256,256]{2,1,0:T(8,128)S(1)}, f32[2,256,256]{2,1,0:T(8,128)S(1)}, u32[]{:S(2)}, u32[]{:S(2)}) collective-permute-start(f32[2,256,256]{2,1,0:T(8,128)S(1)} %pad_maximum_fusion.3), channel_id=1, source_target_pairs={{0,1},{1,0},{2,3},{3,2},{4,5},{5,4},{6,7},{7,6},{8,9},{9,8},{10,11... | collective-permute-start | bytes 1572872 | tf_op jit(solution)/shard_map/ppermute | solution.py:273
  25.3 10.2 %collective-permute-start.8 = (f32[256,256]{1,0:T(8,128)S(1)}, f32[256,256]{1,0:T(8,128)S(1)}, u32[]{:S(2)}, u32[]{:S(2)}) collective-permute-start(f32[256,256]{1,0:T(8,128)S(1)} %collective-permute-done.2), channel_id=1, source_target_pairs={{0,8},{1,25},{2,10},{3,27},{4,12},{5,29},{6,14},{7,31},{8,16},{9,1... | collective-permute-start | bytes 786440 | tf_op jit(solution)/shard_map/ppermute | solution.py:277
  29.5 14.0 %collective-permute-start.7 = (f32[4,256,256]{2,1,0:T(8,128)S(1)}, f32[4,256,256]{2,1,0:T(8,128)S(1)}, u32[]{:S(2)}, u32[]{:S(2)}) collective-permute-start(f32[4,256,256]{2,1,0:T(8,128)S(1)} %constant_dynamic-update-slice_fusion.refs_1_), channel_id=1, source_target_pairs={{0,2},{1,7},{2,4},{3,1},{4,6},{5,3},{6,0},{7,5},{8,10},{9,15},{10,... | collective-permute-start | bytes 3145736 | tf_op jit(solution)/shard_map/ppermute | solution.py:281
  35.5 2.7 %collective-permute-start.9 = (f32[256,256]{1,0:T(8,128)S(1)}, f32[256,256]{1,0:T(8,128)S(1)}, u32[]{:S(2)}, u32[]{:S(2)}) collective-permute-start(f32[256,256]{1,0:T(8,128)S(1)} %collective-permute-done.8), channel_id=1, source_target_pairs={{0,1},{1,0},{2,3},{3,2},{4,5},{5,4},{6,7},{7,6},{8,9},{9,8},{10,11... | collective-permute-start | bytes 786440 | tf_op jit(solution)/shard_map/ppermute | solution.py:273
  39.1 10.1 %collective-permute-start.11 = (f32[2,256,256]{2,1,0:T(8,128)}, f32[2,256,256]{2,1,0:T(8,128)S(1)}, u32[]{:S(2)}, u32[]{:S(2)}) collective-permute-start(f32[2,256,256]{2,1,0:T(8,128)} %pad_maximum_fusion.5.refs_2_), channel_id=1, source_target_pairs={{0,2},{1,7},{2,4},{3,1},{4,6},{5,3},{6,0},{7,5},{8,10},{9,15},{10,... | collective-permute-start | bytes 1572872 | tf_op jit(solution)/shard_map/ppermute | solution.py:281
  49.8 3.5 %copy-start.6 = (f32[2,256,256]{2,1,0:T(8,128)S(1)}, f32[2,256,256]{2,1,0:T(8,128)}, u32[]{:S(2)}) copy-start(f32[2,256,256]{2,1,0:T(8,128)} %copy-done.5) | copy-start | bytes 1572868
  49.8 3.5 %copy-start.8 = (s32[32]{0:T(128)S(1)}, s32[32]{0:T(128)}, u32[]{:S(2)}) copy-start(s32[32]{0:T(128)} %cols.7) | copy-start | bytes 388
  49.8 3.5 %collective-permute-start.13 = (f32[9,128,256]{2,1,0:T(8,128)S(1)}, f32[9,128,256]{2,1,0:T(8,128)S(1)}, u32[]{:S(2)}, u32[]{:S(2)}) collective-permute-start(f32[9,128,256]{2,1,0:T(8,128)S(1)} %pick_for_partner.4), channel_id=1, source_target_pairs={{0,1},{1,0},{2,3},{3,2},{4,5},{5,4},{6,7},{7,6},{8,9},{9,8},{10,11... | collective-permute-start | bytes 3538952 | tf_op jit(solution)/shard_map/ppermute | solution.py:273
  50.8 11.2 %collective-permute-start.10 = (f32[2,256,256]{2,1,0:T(8,128)S(1)}, f32[2,256,256]{2,1,0:T(8,128)S(1)}, u32[]{:S(2)}, u32[]{:S(2)}) collective-permute-start(f32[2,256,256]{2,1,0:T(8,128)S(1)} %slice.19), channel_id=1, source_target_pairs={{0,2},{1,7},{2,4},{3,1},{4,6},{5,3},{6,0},{7,5},{8,10},{9,15},{10,... | collective-permute-start | bytes 1572872 | tf_op jit(solution)/shard_map/ppermute | solution.py:281
  51.7 10.3 %collective-permute-start.12 = (f32[256,256]{1,0:T(8,128)S(1)}, f32[256,256]{1,0:T(8,128)S(1)}, u32[]{:S(2)}, u32[]{:S(2)}) collective-permute-start(f32[256,256]{1,0:T(8,128)S(1)} %slice_bitcast_fusion.2), channel_id=1, source_target_pairs={{0,2},{1,7},{2,4},{3,1},{4,6},{5,3},{6,0},{7,5},{8,10},{9,15},{10,... | collective-permute-start | bytes 786440 | tf_op jit(solution)/shard_map/ppermute | solution.py:281
  53.3 13.1 %copy-start.1 = (bf16[32,128,256]{2,1,0:T(8,128)(2,1)S(1)}, bf16[32,128,256]{2,1,0:T(8,128)(2,1)}, u32[]{:S(2)}) copy-start(bf16[32,128,256]{2,1,0:T(8,128)(2,1)} %copy-done) | copy-start | bytes 6291460
  62.6 3.7 %collective-permute-start.14 = (f32[3,128,256]{2,1,0:T(8,128)S(1)}, f32[3,128,256]{2,1,0:T(8,128)S(1)}, u32[]{:S(2)}, u32[]{:S(2)}) collective-permute-start(f32[3,128,256]{2,1,0:T(8,128)S(1)} %pick_for_partner.5), channel_id=1, source_target_pairs={{0,1},{1,0},{2,3},{3,2},{4,5},{5,4},{6,7},{7,6},{8,9},{9,8},{10,11... | collective-permute-start | bytes 1179656 | tf_op jit(solution)/shard_map/ppermute | solution.py:273
  68.5 30.5 %copy-start.9 = (f32[256]{0:T(256)S(1)}, f32[256]{0:T(256)}, u32[]{:S(2)}) copy-start(f32[256]{0:T(256)} %param.10) | copy-start | bytes 3076
  68.5 30.6 %copy-start.3 = (f32[256,256]{1,0:T(8,128)S(1)}, f32[256,256]{1,0:T(8,128)}, u32[]{:S(2)}) copy-start(f32[256,256]{1,0:T(8,128)} %vector.3) | copy-start | bytes 786436
  99.4 3.1 %collective-permute-start.15 = (f32[264,256]{1,0:T(8,128)S(1)}, f32[264,256]{1,0:T(8,128)S(1)}, u32[]{:S(2)}, u32[]{:S(2)}) collective-permute-start(f32[264,256]{1,0:T(8,128)S(1)} %first_image.1.image), channel_id=1, source_target_pairs={{0,1},{1,0},{2,3},{3,2},{4,5},{5,4},{6,7},{7,6},{8,9},{9,8},{10,11... | collective-permute-start | bytes 811016 | tf_op jit(solution)/shard_map/ppermute | solution.py:273
  102.6 8.6 %collective-permute-start.18 = (f32[2,264,256]{2,1,0:T(8,128)S(1)}, f32[2,264,256]{2,1,0:T(8,128)S(1)}, u32[]{:S(2)}, u32[]{:S(2)}) collective-permute-start(f32[2,264,256]{2,1,0:T(8,128)S(1)} %pad_maximum_fusion.1.refs_0_), channel_id=1, source_target_pairs={{0,2},{1,7},{2,4},{3,1},{4,6},{5,3},{6,0},{7,5},{8,10},{9,15},{10,... | collective-permute-start | bytes 1622024 | tf_op jit(solution)/shard_map/ppermute | solution.py:281
  102.6 12.8 %collective-permute-start.17 = (f32[264,256]{1,0:T(8,128)S(1)}, f32[264,256]{1,0:T(8,128)S(1)}, u32[]{:S(2)}, u32[]{:S(2)}) collective-permute-start(f32[264,256]{1,0:T(8,128)S(1)} %first_image.1.image), channel_id=1, source_target_pairs={{0,8},{1,25},{2,10},{3,27},{4,12},{5,29},{6,14},{7,31},{8,16},{9,1... | collective-permute-start | bytes 811016 | tf_op jit(solution)/shard_map/ppermute | solution.py:277
  105.6 12.7 %collective-permute-start.16 = (f32[264,256]{1,0:T(8,128)S(1)}, f32[264,256]{1,0:T(8,128)S(1)}, u32[]{:S(2)}, u32[]{:S(2)}) collective-permute-start(f32[264,256]{1,0:T(8,128)S(1)} %collective-permute-done.15), channel_id=1, source_target_pairs={{0,8},{1,25},{2,10},{3,27},{4,12},{5,29},{6,14},{7,31},{8,16},{9,1... | collective-permute-start | bytes 811016 | tf_op jit(solution)/shard_map/ppermute | solution.py:277
  111.1 7.2 %collective-permute-start.19 = (f32[264,256]{1,0:T(8,128)S(1)}, f32[264,256]{1,0:T(8,128)S(1)}, u32[]{:S(2)}, u32[]{:S(2)}) collective-permute-start(f32[264,256]{1,0:T(8,128)S(1)} %slice_bitcast_fusion.1), channel_id=1, source_target_pairs={{0,2},{1,7},{2,4},{3,1},{4,6},{5,3},{6,0},{7,5},{8,10},{9,15},{10,... | collective-permute-start | bytes 811016 | tf_op jit(solution)/shard_map/ppermute | solution.py:281
  118.4 5.9 %collective-permute-start.20 = (f32[2,264,256]{2,1,0:T(8,128)S(1)}, f32[2,264,256]{2,1,0:T(8,128)S(1)}, u32[]{:S(2)}, u32[]{:S(2)}) collective-permute-start(f32[2,264,256]{2,1,0:T(8,128)S(1)} %pad_maximum_fusion), channel_id=1, source_target_pairs={{0,1},{1,0},{2,3},{3,2},{4,5},{5,4},{6,7},{7,6},{8,9},{9,8},{10,11... | collective-permute-start | bytes 1622024 | tf_op jit(solution)/shard_map/ppermute | solution.py:273
  121.3 9.8 %collective-permute-start.22 = (f32[264,256]{1,0:T(8,128)S(1)}, f32[264,256]{1,0:T(8,128)S(1)}, u32[]{:S(2)}, u32[]{:S(2)}) collective-permute-start(f32[264,256]{1,0:T(8,128)S(1)} %collective-permute-done.17), channel_id=1, source_target_pairs={{0,8},{1,25},{2,10},{3,27},{4,12},{5,29},{6,14},{7,31},{8,16},{9,1... | collective-permute-start | bytes 811016 | tf_op jit(solution)/shard_map/ppermute | solution.py:277
  124.3 14.4 %collective-permute-start.21 = (f32[4,264,256]{2,1,0:T(8,128)S(1)}, f32[4,264,256]{2,1,0:T(8,128)S(1)}, u32[]{:S(2)}, u32[]{:S(2)}) collective-permute-start(f32[4,264,256]{2,1,0:T(8,128)S(1)} %constant_dynamic-update-slice_fusion.2.refs_1_), channel_id=1, source_target_pairs={{0,2},{1,7},{2,4},{3,1},{4,6},{5,3},{6,0},{7,5},{8,10},{9,15},{10,... | collective-permute-start | bytes 3244040 | tf_op jit(solution)/shard_map/ppermute | solution.py:281
  131.1 2.6 %collective-permute-start.23 = (f32[264,256]{1,0:T(8,128)S(1)}, f32[264,256]{1,0:T(8,128)S(1)}, u32[]{:S(2)}, u32[]{:S(2)}) collective-permute-start(f32[264,256]{1,0:T(8,128)S(1)} %collective-permute-done.22), channel_id=1, source_target_pairs={{0,1},{1,0},{2,3},{3,2},{4,5},{5,4},{6,7},{7,6},{8,9},{9,8},{10,11... | collective-permute-start | bytes 811016 | tf_op jit(solution)/shard_map/ppermute | solution.py:273
  133.8 10.7 %collective-permute-start.25 = (f32[2,264,256]{2,1,0:T(8,128)S(1)}, f32[2,264,256]{2,1,0:T(8,128)S(1)}, u32[]{:S(2)}, u32[]{:S(2)}) collective-permute-start(f32[2,264,256]{2,1,0:T(8,128)S(1)} %pad_maximum_fusion.2.refs_2_), channel_id=1, source_target_pairs={{0,2},{1,7},{2,4},{3,1},{4,6},{5,3},{6,0},{7,5},{8,10},{9,15},{10,... | collective-permute-start | bytes 1622024 | tf_op jit(solution)/shard_map/ppermute | solution.py:281
  145.1 4.8 %collective-permute-start.27 = (f32[9,136,256]{2,1,0:T(8,128)S(1)}, f32[9,136,256]{2,1,0:T(8,128)S(1)}, u32[]{:S(2)}, u32[]{:S(2)}) collective-permute-start(f32[9,136,256]{2,1,0:T(8,128)S(1)} %pick_for_partner.6), channel_id=1, source_target_pairs={{0,1},{1,0},{2,3},{3,2},{4,5},{5,4},{6,7},{7,6},{8,9},{9,8},{10,11... | collective-permute-start | bytes 3760136 | tf_op jit(solution)/shard_map/ppermute | solution.py:273
  147.4 11.5 %collective-permute-start.24 = (f32[2,264,256]{2,1,0:T(8,128)S(1)}, f32[2,264,256]{2,1,0:T(8,128)S(1)}, u32[]{:S(2)}, u32[]{:S(2)}) collective-permute-start(f32[2,264,256]{2,1,0:T(8,128)S(1)} %slice.22), channel_id=1, source_target_pairs={{0,2},{1,7},{2,4},{3,1},{4,6},{5,3},{6,0},{7,5},{8,10},{9,15},{10,... | collective-permute-start | bytes 1622024 | tf_op jit(solution)/shard_map/ppermute | solution.py:281
  147.5 11.4 %collective-permute-start.26 = (f32[264,256]{1,0:T(8,128)S(1)}, f32[264,256]{1,0:T(8,128)S(1)}, u32[]{:S(2)}, u32[]{:S(2)}) collective-permute-start(f32[264,256]{1,0:T(8,128)S(1)} %slice_bitcast_fusion), channel_id=1, source_target_pairs={{0,2},{1,7},{2,4},{3,1},{4,6},{5,3},{6,0},{7,5},{8,10},{9,15},{10,... | collective-permute-start | bytes 811016 | tf_op jit(solution)/shard_map/ppermute | solution.py:281
  150.0 13.1 %copy-start.2 = (bf16[32,128,256]{2,1,0:T(8,128)(2,1)S(1)}, bf16[32,128,256]{2,1,0:T(8,128)(2,1)}, u32[]{:S(2)}) copy-start(bf16[32,128,256]{2,1,0:T(8,128)(2,1)} %copy-done) | copy-start | bytes 6291460
  159.5 3.6 %collective-permute-start.28 = (f32[3,136,256]{2,1,0:T(8,128)S(1)}, f32[3,136,256]{2,1,0:T(8,128)S(1)}, u32[]{:S(2)}, u32[]{:S(2)}) collective-permute-start(f32[3,136,256]{2,1,0:T(8,128)S(1)} %pick_for_partner.7), channel_id=1, source_target_pairs={{0,1},{1,0},{2,3},{3,2},{4,5},{5,4},{6,7},{7,6},{8,9},{9,8},{10,11... | collective-permute-start | bytes 1253384 | tf_op jit(solution)/shard_map/ppermute | solution.py:273

commit v4 on v3

--- a/solution.py
+++ b/solution.py
@@ -72,12 +72,18 @@
     return [(dx, *key, ref, i) for i, key in enumerate(keys)]
 
 
-def early_pieces(chip, mid, last):
-    return named(NONE, CHIP, chip) + named(NONE, MID, mid) + named(NONE, LAST, last)
-
-
-def early_brought(chip, mid, last, far):
-    return named(WAY, CHIP, chip) + named(WAY, MID, mid) + named(WAY, LAST, last) + named(TWO, CHIP[1:], far)
+def early_pieces(own, other, mid, last):
+    return named(NONE, CHIP[1:], own) + named(NONE, CHIP[:1], other) + named(NONE, MID, mid) + named(NONE, LAST, last)
+
+
+def early_brought(own, other, mid, last, far):
+    return (
+        named(WAY, CHIP[1:], own)
+        + named(WAY, CHIP[:1], other)
+        + named(WAY, MID, mid)
+        + named(WAY, LAST, last)
+        + named(TWO, CHIP[1:], far)
+    )
 
 
 def late_brought(mid, last):
@@ -151,12 +157,12 @@
 
 
 def early_kernel(place, rows, cols, split, *refs):
-    out, stats = refs[8], refs[9] if len(refs) > 9 else None
+    out, stats = refs[10], refs[11] if len(refs) > 11 else None
     out[...] = jnp.zeros_like(out)
     if stats is not None:
         stats[...] = jnp.zeros_like(stats)
-    own, brought = early_pieces(*refs[:3]), early_brought(*refs[3:7])
-    add_products(place, rows, cols, split, own, brought, refs[7], out, stats)
+    own, brought = early_pieces(*refs[:4]), early_brought(*refs[4:9])
+    add_products(place, rows, cols, split, own, brought, refs[9], out, stats)
 
 
 def multiply_early(place, rows, cols, split, gathered, other):
@@ -295,12 +301,11 @@
     slots = (place, block_row, block_col, split)
 
     def product(own):
-        other = swap_cores(own)
-        z_own, z_other = send_z(own), send_z(other)
-        chip = join(other, own)
-        x_chip = send_x(chip)
-        far_chip = send_x(x_chip[1])[None]
-        z_chip = after(join(z_other, z_own), far_chip, split, partner_rows)
+        other_own = swap_cores(own)
+        z_own, z_other = send_z(own), send_z(other_own)
+        x_own, x_other = send_x(own), send_x(other_own)
+        far_own = send_x(x_own)
+        z_chip = after(join(z_other, z_own), far_own, x_other, split, partner_rows)
         mid = join(z_chip, swap_cores(z_chip))
         z_far = send_z(z_own)
         x_mid = send_x(mid)
@@ -309,9 +314,9 @@
         x_mid = after(x_mid, last)
         far_mid = send_x(x_mid[:2])
         far_last = send_x(x_last[1])[None]
-        brought = (x_chip, x_mid, x_last, far_chip)
+        brought = (x_own[None], x_other[None], x_mid, x_last, far_own[None])
         other = swap_cores(pick_for_partner(early_brought, place, partner_rows, brought))
-        sums = multiply_early(*slots, (chip, mid, last, *brought), other)
+        sums = multiply_early(*slots, (own[None], other_own[None], mid, last, *brought), other)
         brought = after((far_mid, far_last), sums)
         other = swap_cores(pick_for_partner(late_brought, place, partner_rows, brought))
         return lax.all_to_all(multiply_late(*slots, brought, other, *sums), "row", 0, 0, tiled=True)

time: 196 us -> 194 us (0.990)
  starting transfers between devices: 47.2 us -> 45.1 us
    ppermute x6, waiting for transfers between devices: 22 us -> 25.3 us  [send_z(): return lax.ppermute(part, 'col', col_pairs(True))]
    ppermute x11, waiting for transfers between devices: 11.4 us -> 8.17 us  [swap_cores(): return lax.ppermute(part, 'col', [(i, i ^ 1) for i in range(32)])]
    ppermute x12 -> x14, starting transfers between devices: 9.03 us -> 6.16 us  [send_x(): return lax.ppermute(part, 'col', col_pairs(False))]
    ppermute x12 -> x14, waiting for transfers between devices: 31.6 us -> 31 us  [send_x(): return lax.ppermute(part, 'col', col_pairs(False))]
  transfers between devices with their start and end apart: 29 -> 31, of which waited for: 21 -> 18; matrix products, arithmetic and copies ran while one was open for 1% -> 0% of each run, Pallas kernels for 5% -> 5%
where the time goes in v4:
time: 194 us; the launch traced here: 193 us
  waiting for transfers between devices  64.5 us (33%)
  blocking collectives  60 us (31%)
  starting transfers between devices  45.1 us (23%)
  Pallas kernels  17.9 us (9%)
  local copies, waits for them, and re-layouts  3.89 us (2%)
    all_to_all x2, blocking collectives, product(): lax.all_to_all(multiply_late(*slots, brought, other, *sums), 'row', 0, 0,...  60 us
    ppermute x14, waiting for transfers between devices, send_x(): return lax.ppermute(part, 'col', col_pairs(False))  31 us
    ppermute x6, waiting for transfers between devices, send_z(): return lax.ppermute(part, 'col', col_pairs(True))  25.3 us
    ppermute x11, starting transfers between devices, swap_cores(): return lax.ppermute(part, 'col', [(i, i ^ 1) for i in range(32)])  20 us
    ppermute x6, starting transfers between devices, send_z(): return lax.ppermute(part, 'col', col_pairs(True))  18.9 us
    pallas_call x2, Pallas kernels, multiply_early(): pl.pallas_call(early_kernel, out_shape=shapes, in_specs=[smem()] * 3 + [v...  8.92 us
    ppermute x11, waiting for transfers between devices, swap_cores(): return lax.ppermute(part, 'col', [(i, i ^ 1) for i in range(32)])  8.17 us
    ppermute x14, starting transfers between devices, send_x(): return lax.ppermute(part, 'col', col_pairs(False))  6.16 us
  transfers between devices with their start and end apart: 31, of which 18 were waited for; matrix products, arithmetic and copies ran while one was open for 0% of the time, Pallas kernels for 5%

profile of v4, /device:TPU:1, one launch (start us, length us, event | category | flops | bytes accessed | tf_op | source)
XLA Modules:
  0.0 193.2 jit_solution(14238615933296765506)
XLA Ops:
  0.6 3.3 %collective-permute-start = (f32[256,256]{1,0:T(8,128)}, f32[256,256]{1,0:T(8,128)S(1)}, u32[]{:S(2)}, u32[]{:S(2)}) collective-permute-start(f32[256,256]{1,0:T(8,128)} %vector.3), channel_id=1, source_target_pairs={{0,1},{1,0},{2,3},{3,2},{4,5},{5,4},{6,7},{7,6},{8,9},{9,8},{10,11... | collective-permute-start | bytes 786440 | tf_op jit(solution)/shard_map/ppermute | solution.py:279
  4.0 0.7 collective-permute-start.3
  4.7 6.0 %collective-permute-start.2 = (f32[256,256]{1,0:T(8,128)}, f32[256,256]{1,0:T(8,128)S(1)}, u32[]{:S(2)}, u32[]{:S(2)}) collective-permute-start(f32[256,256]{1,0:T(8,128)} %vector.3), channel_id=1, source_target_pairs={{0,8},{1,25},{2,10},{3,27},{4,12},{5,29},{6,14},{7,31},{8,16},{9,1... | collective-permute-start | bytes 786440 | tf_op jit(solution)/shard_map/ppermute | solution.py:283
  10.7 1.2 collective-permute-start.1
  12.7 1.6 collective-permute-start.6
  14.9 1.6 copy-done.4
  16.5 0.9 split_blocks.1.split
  17.4 5.3 %collective-permute-done.1 = f32[256,256]{1,0:T(8,128)S(1)} collective-permute-done((f32[256,256]{1,0:T(8,128)S(1)}, f32[256,256]{1,0:T(8,128)S(1)}, u32[]{:S(2)}, u32[]{:S(2)}) %collective-permute-start.1) | collective-permute-done | bytes 262176 | tf_op jit(solution)/shard_map/ppermute | solution.py:283
  22.9 4.1 %collective-permute-start.9 = (f32[256,256]{1,0:T(8,128)S(1)}, f32[256,256]{1,0:T(8,128)S(1)}, u32[]{:S(2)}, u32[]{:S(2)}) collective-permute-start(f32[256,256]{1,0:T(8,128)S(1)} %collective-permute-done.2), channel_id=1, source_target_pairs={{0,8},{1,25},{2,10},{3,27},{4,12},{5,29},{6,14},{7,31},{8,16},{9,1... | collective-permute-start | bytes 786440 | tf_op jit(solution)/shard_map/ppermute | solution.py:283
  27.7 4.5 %collective-permute-done.9 = f32[256,256]{1,0:T(8,128)S(1)} collective-permute-done((f32[256,256]{1,0:T(8,128)S(1)}, f32[256,256]{1,0:T(8,128)S(1)}, u32[]{:S(2)}, u32[]{:S(2)}) %collective-permute-start.9) | collective-permute-done | bytes 262176 | tf_op jit(solution)/shard_map/ppermute | solution.py:283
  32.2 2.6 %collective-permute-start.10 = (f32[256,256]{1,0:T(8,128)S(1)}, f32[256,256]{1,0:T(8,128)S(1)}, u32[]{:S(2)}, u32[]{:S(2)}) collective-permute-start(f32[256,256]{1,0:T(8,128)S(1)} %collective-permute-done.9), channel_id=1, source_target_pairs={{0,1},{1,0},{2,3},{3,2},{4,5},{5,4},{6,7},{7,6},{8,9},{9,8},{10,11... | collective-permute-start | bytes 786440 | tf_op jit(solution)/shard_map/ppermute | solution.py:279
  34.8 1.2 collective-permute-done.10
  36.7 4.3 %collective-permute-done.8.refs_2_.refs_6_ = f32[4,256,256]{2,1,0:T(8,128)S(1)} collective-permute-done((f32[4,256,256]{2,1,0:T(8,128)S(1)}, f32[4,256,256]{2,1,0:T(8,128)S(1)}, u32[]{:S(2)}, u32[]{:S(2)}) %collective-permute-start.8) | collective-permute-done | bytes 1048608 | tf_op jit(solution)/shard_map/ppermute | solution.py:287
  41.1 5.6 %collective-permute-done.12.refs_3_.refs_7_ = f32[2,256,256]{2,1,0:T(8,128)S(1)} collective-permute-done((f32[2,256,256]{2,1,0:T(8,128)S(1)}, f32[2,256,256]{2,1,0:T(8,128)S(1)}, u32[]{:S(2)}, u32[]{:S(2)}) %collective-permute-start.12) | collective-permute-done | bytes 524320 | tf_op jit(solution)/shard_map/ppermute | solution.py:287
  46.7 0.9 copy-done.6
  47.7 0.9 copy-done.8
  48.6 0.6 pick_for_partner.4
  49.8 1.2 collective-permute-start.11
  51.3 1.0 collective-permute-done.14.refs_9_
  52.3 4.4 %multiply_early.2.sums = f32[8,256,256]{2,1,0:T(8,128)} custom-call(s32[3]{0:T(128)S(1)} %pad_add_fusion.place, s32[32]{0:T(128)S(1)} %copy-done.11, s32[32]{0:T(128)S(1)} %copy-done.12, bf16[32,128,256]{2,1,0:T(8,128)(2,1)} %copy-done, f32[1,256,256]{2,1,0:T(8,128)S(1)} %bitcast.28, f32[1,256,256]{2,1,0:T(8,128)S(1)} %bitcast.46, ...), custom_call_target="tpu_custom_call" | custom-call | tf_op jit(solution)/shard_map/multiply_early/pallas_call | solution.py:173
  56.7 4.3 %collective-permute-done.13 = f32[256,256]{1,0:T(8,128)S(1)} collective-permute-done((f32[256,256]{1,0:T(8,128)S(1)}, f32[256,256]{1,0:T(8,128)S(1)}, u32[]{:S(2)}, u32[]{:S(2)}) %collective-permute-start.13) | collective-permute-done | bytes 262176 | tf_op jit(solution)/shard_map/ppermute | solution.py:287
  61.6 2.3 %collective-permute-start.15 = (f32[3,128,256]{2,1,0:T(8,128)S(1)}, f32[3,128,256]{2,1,0:T(8,128)S(1)}, u32[]{:S(2)}, u32[]{:S(2)}) collective-permute-start(f32[3,128,256]{2,1,0:T(8,128)S(1)} %pick_for_partner.5), channel_id=1, source_target_pairs={{0,1},{1,0},{2,3},{3,2},{4,5},{5,4},{6,7},{7,6},{8,9},{9,8},{10,11... | collective-permute-start | bytes 1179656 | tf_op jit(solution)/shard_map/ppermute | solution.py:279
  63.9 1.3 collective-permute-done.15.other
  65.2 2.1 %multiply_late.2 = f32[8,256,256]{2,1,0:T(8,128)S(1)} custom-call(s32[3]{0:T(128)S(1)} %pad_add_fusion.place, s32[32]{0:T(128)S(1)} %copy-done.11, s32[32]{0:T(128)S(1)} %copy-done.12, bf16[32,128,256]{2,1,0:T(8,128)(2,1)S(1)} %copy-done.1, f32[2,256,256]{2,1,0:T(8,128)S(1)} %collective-permute-done.11.refs_0_.mid, f32[1,256,256]{2,1,0:T(8,128)S(1)} %bitcast.38, ...), custom_call_target="tpu_custom_call" | custom-call | tf_op jit(solution)/shard_map/multiply_late/pallas_call | solution.py:199
  67.4 30.3 %all_to_all.10.terms = f32[8,256,256]{2,1,0:T(8,128)S(1)} all-to-all(f32[8,256,256]{2,1,0:T(8,128)S(1)} %multiply_late.2), channel_id=1, replica_groups=mesh['row'=8,'col'=32] {'row'}, dimensions={0} | all-to-all | bytes 4194304 | tf_op jit(solution)/shard_map/all_to_all | solution.py:322
  98.1 1.9 collective-permute-start.16
  100.0 3.2 %collective-permute-start.18 = (f32[264,256]{1,0:T(8,128)S(1)}, f32[264,256]{1,0:T(8,128)S(1)}, u32[]{:S(2)}, u32[]{:S(2)}) collective-permute-start(f32[264,256]{1,0:T(8,128)S(1)} %first_image.1.image), channel_id=1, source_target_pairs={{0,8},{1,25},{2,10},{3,27},{4,12},{5,29},{6,14},{7,31},{8,16},{9,1... | collective-permute-start | bytes 811016 | tf_op jit(solution)/shard_map/ppermute | solution.py:283
  103.2 1.2 collective-permute-start.17
  104.4 1.2 collective-permute-done.19
  105.6 0.9 collective-permute-start.20
  106.6 6.4 %collective-permute-done.18 = f32[264,256]{1,0:T(8,128)S(1)} collective-permute-done((f32[264,256]{1,0:T(8,128)S(1)}, f32[264,256]{1,0:T(8,128)S(1)}, u32[]{:S(2)}, u32[]{:S(2)}) %collective-permute-start.18) | collective-permute-done | bytes 270368 | tf_op jit(solution)/shard_map/ppermute | solution.py:283
  112.9 2.9 %collective-permute-done.17 = f32[264,256]{1,0:T(8,128)S(1)} collective-permute-done((f32[264,256]{1,0:T(8,128)S(1)}, f32[264,256]{1,0:T(8,128)S(1)}, u32[]{:S(2)}, u32[]{:S(2)}) %collective-permute-start.17) | collective-permute-done | bytes 270368 | tf_op jit(solution)/shard_map/ppermute | solution.py:283
  115.9 2.4 %collective-permute-start.22 = (f32[2,264,256]{2,1,0:T(8,128)S(1)}, f32[2,264,256]{2,1,0:T(8,128)S(1)}, u32[]{:S(2)}, u32[]{:S(2)}) collective-permute-start(f32[2,264,256]{2,1,0:T(8,128)S(1)} %pad_maximum_fusion), channel_id=1, source_target_pairs={{0,1},{1,0},{2,3},{3,2},{4,5},{5,4},{6,7},{7,6},{8,9},{9,8},{10,11... | collective-permute-start | bytes 1622024 | tf_op jit(solution)/shard_map/ppermute | solution.py:279
  118.3 3.2 %collective-permute-start.24 = (f32[264,256]{1,0:T(8,128)S(1)}, f32[264,256]{1,0:T(8,128)S(1)}, u32[]{:S(2)}, u32[]{:S(2)}) collective-permute-start(f32[264,256]{1,0:T(8,128)S(1)} %collective-permute-done.18), channel_id=1, source_target_pairs={{0,8},{1,25},{2,10},{3,27},{4,12},{5,29},{6,14},{7,31},{8,16},{9,1... | collective-permute-start | bytes 811016 | tf_op jit(solution)/shard_map/ppermute | solution.py:283
  122.1 6.3 %collective-permute-done.24 = f32[264,256]{1,0:T(8,128)S(1)} collective-permute-done((f32[264,256]{1,0:T(8,128)S(1)}, f32[264,256]{1,0:T(8,128)S(1)}, u32[]{:S(2)}, u32[]{:S(2)}) %collective-permute-start.24) | collective-permute-done | bytes 270368 | tf_op jit(solution)/shard_map/ppermute | solution.py:283
  128.3 1.0 collective-permute-start.25
  129.4 1.2 collective-permute-done.25
  130.7 5.3 %collective-permute-done.23.refs_2_.refs_6_ = f32[4,264,256]{2,1,0:T(8,128)S(1)} collective-permute-done((f32[4,264,256]{2,1,0:T(8,128)S(1)}, f32[4,264,256]{2,1,0:T(8,128)S(1)}, u32[]{:S(2)}, u32[]{:S(2)}) %collective-permute-start.23) | collective-permute-done | bytes 1081376 | tf_op jit(solution)/shard_map/ppermute | solution.py:287
  136.0 5.8 %collective-permute-done.27.refs_3_.refs_7_ = f32[2,264,256]{2,1,0:T(8,128)S(1)} collective-permute-done((f32[2,264,256]{2,1,0:T(8,128)S(1)}, f32[2,264,256]{2,1,0:T(8,128)S(1)}, u32[]{:S(2)}, u32[]{:S(2)}) %collective-permute-start.27) | collective-permute-done | bytes 540704 | tf_op jit(solution)/shard_map/ppermute | solution.py:287
  142.4 2.1 %collective-permute-start.29 = (f32[9,136,256]{2,1,0:T(8,128)S(1)}, f32[9,136,256]{2,1,0:T(8,128)S(1)}, u32[]{:S(2)}, u32[]{:S(2)}) collective-permute-start(f32[9,136,256]{2,1,0:T(8,128)S(1)} %pick_for_partner.6), channel_id=1, source_target_pairs={{0,1},{1,0},{2,3},{3,2},{4,5},{5,4},{6,7},{7,6},{8,9},{9,8},{10,11... | collective-permute-start | bytes 3760136 | tf_op jit(solution)/shard_map/ppermute | solution.py:279
  145.1 2.1 %collective-permute-done.29.refs_9_ = f32[9,136,256]{2,1,0:T(8,128)S(1)} collective-permute-done((f32[9,136,256]{2,1,0:T(8,128)S(1)}, f32[9,136,256]{2,1,0:T(8,128)S(1)}, u32[]{:S(2)}, u32[]{:S(2)}) %collective-permute-start.29) | collective-permute-done | bytes 1253408 | tf_op jit(solution)/shard_map/ppermute | solution.py:279
  147.2 4.5 %multiply_early.3 = (f32[8,264,256]{2,1,0:T(8,128)}, f32[32,8,256]{2,1,0:T(8,128)S(1)}) custom-call(s32[3]{0:T(128)S(1)} %pad_add_fusion.place, s32[32]{0:T(128)S(1)} %copy-done.11, s32[32]{0:T(128)S(1)} %copy-done.12, bf16[32,128,256]{2,1,0:T(8,128)(2,1)} %copy-done, f32[1,264,256]{2,1,0:T(8,128)S(1)} %bitcast.27, f32[1,264,256]{2,1,0:T(8,128)S(1)} %bitcast.45, ...), custom_call_target="tpu_custom_call" | custom-call | tf_op jit(solution)/shard_map/multiply_early/pallas_call | solution.py:173
  151.7 4.4 %collective-permute-done.28 = f32[264,256]{1,0:T(8,128)S(1)} collective-permute-done((f32[264,256]{1,0:T(8,128)S(1)}, f32[264,256]{1,0:T(8,128)S(1)}, u32[]{:S(2)}, u32[]{:S(2)}) %collective-permute-start.28) | collective-permute-done | bytes 270368 | tf_op jit(solution)/shard_map/ppermute | solution.py:287
  156.7 2.2 %collective-permute-start.30 = (f32[3,136,256]{2,1,0:T(8,128)S(1)}, f32[3,136,256]{2,1,0:T(8,128)S(1)}, u32[]{:S(2)}, u32[]{:S(2)}) collective-permute-start(f32[3,136,256]{2,1,0:T(8,128)S(1)} %pick_for_partner.7), channel_id=1, source_target_pairs={{0,1},{1,0},{2,3},{3,2},{4,5},{5,4},{6,7},{7,6},{8,9},{9,8},{10,11... | collective-permute-start | bytes 1253384 | tf_op jit(solution)/shard_map/ppermute | solution.py:279
  158.9 1.4 collective-permute-done.30.other
  160.3 2.2 %multiply_late.3 = f32[8,264,256]{2,1,0:T(8,128)S(1)} custom-call(s32[3]{0:T(128)S(1)} %pad_add_fusion.place, s32[32]{0:T(128)S(1)} %copy-done.11, s32[32]{0:T(128)S(1)} %copy-done.12, bf16[32,128,256]{2,1,0:T(8,128)(2,1)S(1)} %copy-done.2, f32[2,264,256]{2,1,0:T(8,128)S(1)} %collective-permute-done.26.refs_0_.mid, f32[1,264,256]{2,1,0:T(8,128)S(1)} %bitcast.30, ...), custom_call_target="tpu_custom_call" | custom-call | tf_op jit(solution)/shard_map/multiply_late/pallas_call | solution.py:199
  162.5 29.7 %all_to_all.11.terms = f32[8,264,256]{2,1,0:T(8,128)S(1)} all-to-all(f32[8,264,256]{2,1,0:T(8,128)S(1)} %multiply_late.3), channel_id=1, replica_groups=mesh['row'=8,'col'=32] {'row'}, dimensions={0} | all-to-all | bytes 4325376 | tf_op jit(solution)/shard_map/all_to_all | solution.py:322
  192.2 1.0 finish.1
  (69 shorter events, 6.6 us)
Async XLA Ops:
  0.6 10.1 %collective-permute-start = (f32[256,256]{1,0:T(8,128)}, f32[256,256]{1,0:T(8,128)S(1)}, u32[]{:S(2)}, u32[]{:S(2)}) collective-permute-start(f32[256,256]{1,0:T(8,128)} %vector.3), channel_id=1, source_target_pairs={{0,1},{1,0},{2,3},{3,2},{4,5},{5,4},{6,7},{7,6},{8,9},{9,8},{10,11... | collective-permute-start | bytes 786440 | tf_op jit(solution)/shard_map/ppermute | solution.py:279
  4.0 8.5 %collective-permute-start.3 = (f32[256,256]{1,0:T(8,128)}, f32[256,256]{1,0:T(8,128)S(1)}, u32[]{:S(2)}, u32[]{:S(2)}) collective-permute-start(f32[256,256]{1,0:T(8,128)} %vector.3), channel_id=1, source_target_pairs={{0,2},{1,7},{2,4},{3,1},{4,6},{5,3},{6,0},{7,5},{8,10},{9,15},{10,... | collective-permute-start | bytes 786440 | tf_op jit(solution)/shard_map/ppermute | solution.py:287
  4.7 12.7 %collective-permute-start.2 = (f32[256,256]{1,0:T(8,128)}, f32[256,256]{1,0:T(8,128)S(1)}, u32[]{:S(2)}, u32[]{:S(2)}) collective-permute-start(f32[256,256]{1,0:T(8,128)} %vector.3), channel_id=1, source_target_pairs={{0,8},{1,25},{2,10},{3,27},{4,12},{5,29},{6,14},{7,31},{8,16},{9,1... | collective-permute-start | bytes 786440 | tf_op jit(solution)/shard_map/ppermute | solution.py:283
  10.7 6.7 %copy-start.9 = (f32[256,256]{1,0:T(8,128)}, f32[256,256]{1,0:T(8,128)S(1)}, u32[]{:S(2)}) copy-start(f32[256,256]{1,0:T(8,128)S(1)} %collective-permute-done) | copy-start | bytes 786436
  10.7 11.9 %collective-permute-start.1 = (f32[256,256]{1,0:T(8,128)S(1)}, f32[256,256]{1,0:T(8,128)S(1)}, u32[]{:S(2)}, u32[]{:S(2)}) collective-permute-start(f32[256,256]{1,0:T(8,128)S(1)} %collective-permute-done), channel_id=1, source_target_pairs={{0,8},{1,25},{2,10},{3,27},{4,12},{5,29},{6,14},{7,31},{8,16},{9,1... | collective-permute-start | bytes 786440 | tf_op jit(solution)/shard_map/ppermute | solution.py:283
  11.9 10.8 %collective-permute-start.5 = (f32[256,256]{1,0:T(8,128)S(1)}, f32[256,256]{1,0:T(8,128)S(1)}, u32[]{:S(2)}, u32[]{:S(2)}) collective-permute-start(f32[256,256]{1,0:T(8,128)S(1)} %collective-permute-done), channel_id=1, source_target_pairs={{0,2},{1,7},{2,4},{3,1},{4,6},{5,3},{6,0},{7,5},{8,10},{9,15},{10,... | collective-permute-start | bytes 786440 | tf_op jit(solution)/shard_map/ppermute | solution.py:287
  12.5 10.3 %collective-permute-start.4 = (f32[256,256]{1,0:T(8,128)S(1)}, f32[256,256]{1,0:T(8,128)S(1)}, u32[]{:S(2)}, u32[]{:S(2)}) collective-permute-start(f32[256,256]{1,0:T(8,128)S(1)} %collective-permute-done.3), channel_id=1, source_target_pairs={{0,2},{1,7},{2,4},{3,1},{4,6},{5,3},{6,0},{7,5},{8,10},{9,15},{10,... | collective-permute-start | bytes 786440 | tf_op jit(solution)/shard_map/ppermute | solution.py:287
  12.7 10.0 %collective-permute-start.6 = (s32[32]{0:T(128)}, s32[32]{0:T(128)S(1)}, u32[]{:S(2)}, u32[]{:S(2)}) collective-permute-start(s32[32]{0:T(128)} %rows.7), channel_id=1, source_target_pairs={{0,1},{1,0},{2,3},{3,2},{4,5},{5,4},{6,7},{7,6},{8,9},{9,8},{10,11... | collective-permute-start | bytes 392 | tf_op jit(solution)/shard_map/ppermute | solution.py:279
  14.9 1.6 copy-start.4
  17.4 9.7 %copy-start = (bf16[32,128,256]{2,1,0:T(8,128)(2,1)}, bf16[32,128,256]{2,1,0:T(8,128)(2,1)S(1)}, u32[]{:S(2)}) copy-start(bf16[32,128,256]{2,1,0:T(8,128)(2,1)S(1)} %split_blocks.1.split) | copy-start | bytes 6291460
  22.7 13.3 %copy-start.5 = (f32[256,256]{1,0:T(8,128)}, f32[256,256]{1,0:T(8,128)S(1)}, u32[]{:S(2)}) copy-start(f32[256,256]{1,0:T(8,128)S(1)} %collective-permute-done.5) | copy-start | bytes 786436
  22.8 13.3 %copy-start.7 = (f32[256,256]{1,0:T(8,128)}, f32[256,256]{1,0:T(8,128)S(1)}, u32[]{:S(2)}) copy-start(f32[256,256]{1,0:T(8,128)S(1)} %collective-permute-done.4) | copy-start | bytes 786436
  22.8 4.2 %collective-permute-start.7 = (f32[2,256,256]{2,1,0:T(8,128)S(1)}, f32[2,256,256]{2,1,0:T(8,128)S(1)}, u32[]{:S(2)}, u32[]{:S(2)}) collective-permute-start(f32[2,256,256]{2,1,0:T(8,128)S(1)} %pad_maximum_fusion.2), channel_id=1, source_target_pairs={{0,1},{1,0},{2,3},{3,2},{4,5},{5,4},{6,7},{7,6},{8,9},{9,8},{10,11... | collective-permute-start | bytes 1572872 | tf_op jit(solution)/shard_map/ppermute | solution.py:279
  22.9 9.3 %collective-permute-start.9 = (f32[256,256]{1,0:T(8,128)S(1)}, f32[256,256]{1,0:T(8,128)S(1)}, u32[]{:S(2)}, u32[]{:S(2)}) collective-permute-start(f32[256,256]{1,0:T(8,128)S(1)} %collective-permute-done.2), channel_id=1, source_target_pairs={{0,8},{1,25},{2,10},{3,27},{4,12},{5,29},{6,14},{7,31},{8,16},{9,1... | collective-permute-start | bytes 786440 | tf_op jit(solution)/shard_map/ppermute | solution.py:283
  27.1 14.0 %collective-permute-start.8 = (f32[4,256,256]{2,1,0:T(8,128)S(1)}, f32[4,256,256]{2,1,0:T(8,128)S(1)}, u32[]{:S(2)}, u32[]{:S(2)}) collective-permute-start(f32[4,256,256]{2,1,0:T(8,128)S(1)} %constant_dynamic-update-slice_fusion.refs_2_), channel_id=1, source_target_pairs={{0,2},{1,7},{2,4},{3,1},{4,6},{5,3},{6,0},{7,5},{8,10},{9,15},{10,... | collective-permute-start | bytes 3145736 | tf_op jit(solution)/shard_map/ppermute | solution.py:287
  32.2 3.8 %collective-permute-start.10 = (f32[256,256]{1,0:T(8,128)S(1)}, f32[256,256]{1,0:T(8,128)S(1)}, u32[]{:S(2)}, u32[]{:S(2)}) collective-permute-start(f32[256,256]{1,0:T(8,128)S(1)} %collective-permute-done.9), channel_id=1, source_target_pairs={{0,1},{1,0},{2,3},{3,2},{4,5},{5,4},{6,7},{7,6},{8,9},{9,8},{10,11... | collective-permute-start | bytes 786440 | tf_op jit(solution)/shard_map/ppermute | solution.py:279
  36.0 10.7 %collective-permute-start.12 = (f32[2,256,256]{2,1,0:T(8,128)S(1)}, f32[2,256,256]{2,1,0:T(8,128)S(1)}, u32[]{:S(2)}, u32[]{:S(2)}) collective-permute-start(f32[2,256,256]{2,1,0:T(8,128)S(1)} %pad_maximum_fusion.3.refs_3_), channel_id=1, source_target_pairs={{0,2},{1,7},{2,4},{3,1},{4,6},{5,3},{6,0},{7,5},{8,10},{9,15},{10,... | collective-permute-start | bytes 1572872 | tf_op jit(solution)/shard_map/ppermute | solution.py:287
  46.7 1.0 copy-start.6
  47.7 0.9 copy-start.8
  49.2 3.0 %copy-start.3 = (f32[256,256]{1,0:T(8,128)S(1)}, f32[256,256]{1,0:T(8,128)}, u32[]{:S(2)}) copy-start(f32[256,256]{1,0:T(8,128)} %vector.3) | copy-start | bytes 786436
  49.3 3.0 %copy-start.10 = (f32[256,256]{1,0:T(8,128)S(1)}, f32[256,256]{1,0:T(8,128)}, u32[]{:S(2)}) copy-start(f32[256,256]{1,0:T(8,128)} %copy-done.9) | copy-start | bytes 786436
  49.3 3.0 %copy-start.11 = (s32[32]{0:T(128)S(1)}, s32[32]{0:T(128)}, u32[]{:S(2)}) copy-start(s32[32]{0:T(128)} %rows.7) | copy-start | bytes 388
  49.3 3.0 %copy-start.12 = (s32[32]{0:T(128)S(1)}, s32[32]{0:T(128)}, u32[]{:S(2)}) copy-start(s32[32]{0:T(128)} %cols.7) | copy-start | bytes 388
  49.3 3.0 %collective-permute-start.14 = (f32[9,128,256]{2,1,0:T(8,128)S(1)}, f32[9,128,256]{2,1,0:T(8,128)S(1)}, u32[]{:S(2)}, u32[]{:S(2)}) collective-permute-start(f32[9,128,256]{2,1,0:T(8,128)S(1)} %pick_for_partner.4), channel_id=1, source_target_pairs={{0,1},{1,0},{2,3},{3,2},{4,5},{5,4},{6,7},{7,6},{8,9},{9,8},{10,11... | collective-permute-start | bytes 3538952 | tf_op jit(solution)/shard_map/ppermute | solution.py:279
  49.8 11.2 %collective-permute-start.11 = (f32[2,256,256]{2,1,0:T(8,128)S(1)}, f32[2,256,256]{2,1,0:T(8,128)S(1)}, u32[]{:S(2)}, u32[]{:S(2)}) collective-permute-start(f32[2,256,256]{2,1,0:T(8,128)S(1)} %slice.12), channel_id=1, source_target_pairs={{0,2},{1,7},{2,4},{3,1},{4,6},{5,3},{6,0},{7,5},{8,10},{9,15},{10,... | collective-permute-start | bytes 1572872 | tf_op jit(solution)/shard_map/ppermute | solution.py:287
  51.0 10.0 %collective-permute-start.13 = (f32[256,256]{1,0:T(8,128)S(1)}, f32[256,256]{1,0:T(8,128)S(1)}, u32[]{:S(2)}, u32[]{:S(2)}) collective-permute-start(f32[256,256]{1,0:T(8,128)S(1)} %slice_bitcast_fusion.1), channel_id=1, source_target_pairs={{0,2},{1,7},{2,4},{3,1},{4,6},{5,3},{6,0},{7,5},{8,10},{9,15},{10,... | collective-permute-start | bytes 786440 | tf_op jit(solution)/shard_map/ppermute | solution.py:287
  52.3 13.0 %copy-start.1 = (bf16[32,128,256]{2,1,0:T(8,128)(2,1)S(1)}, bf16[32,128,256]{2,1,0:T(8,128)(2,1)}, u32[]{:S(2)}) copy-start(bf16[32,128,256]{2,1,0:T(8,128)(2,1)} %copy-done) | copy-start | bytes 6291460
  61.6 3.6 %collective-permute-start.15 = (f32[3,128,256]{2,1,0:T(8,128)S(1)}, f32[3,128,256]{2,1,0:T(8,128)S(1)}, u32[]{:S(2)}, u32[]{:S(2)}) collective-permute-start(f32[3,128,256]{2,1,0:T(8,128)S(1)} %pick_for_partner.5), channel_id=1, source_target_pairs={{0,1},{1,0},{2,3},{3,2},{4,5},{5,4},{6,7},{7,6},{8,9},{9,8},{10,11... | collective-permute-start | bytes 1179656 | tf_op jit(solution)/shard_map/ppermute | solution.py:279
  67.4 30.3 %copy-start.13 = (f32[256]{0:T(256)S(1)}, f32[256]{0:T(256)}, u32[]{:S(2)}) copy-start(f32[256]{0:T(256)} %param.10) | copy-start | bytes 3076
  98.1 5.1 %collective-permute-start.16 = (f32[264,256]{1,0:T(8,128)S(1)}, f32[264,256]{1,0:T(8,128)S(1)}, u32[]{:S(2)}, u32[]{:S(2)}) collective-permute-start(f32[264,256]{1,0:T(8,128)S(1)} %first_image.1.image), channel_id=1, source_target_pairs={{0,1},{1,0},{2,3},{3,2},{4,5},{5,4},{6,7},{7,6},{8,9},{9,8},{10,11... | collective-permute-start | bytes 811016 | tf_op jit(solution)/shard_map/ppermute | solution.py:279
  100.0 5.6 %collective-permute-start.19 = (f32[264,256]{1,0:T(8,128)S(1)}, f32[264,256]{1,0:T(8,128)S(1)}, u32[]{:S(2)}, u32[]{:S(2)}) collective-permute-start(f32[264,256]{1,0:T(8,128)S(1)} %first_image.1.image), channel_id=1, source_target_pairs={{0,2},{1,7},{2,4},{3,1},{4,6},{5,3},{6,0},{7,5},{8,10},{9,15},{10,... | collective-permute-start | bytes 811016 | tf_op jit(solution)/shard_map/ppermute | solution.py:287
  100.0 12.9 %collective-permute-start.18 = (f32[264,256]{1,0:T(8,128)S(1)}, f32[264,256]{1,0:T(8,128)S(1)}, u32[]{:S(2)}, u32[]{:S(2)}) collective-permute-start(f32[264,256]{1,0:T(8,128)S(1)} %first_image.1.image), channel_id=1, source_target_pairs={{0,8},{1,25},{2,10},{3,27},{4,12},{5,29},{6,14},{7,31},{8,16},{9,1... | collective-permute-start | bytes 811016 | tf_op jit(solution)/shard_map/ppermute | solution.py:283
  103.2 12.6 %collective-permute-start.17 = (f32[264,256]{1,0:T(8,128)S(1)}, f32[264,256]{1,0:T(8,128)S(1)}, u32[]{:S(2)}, u32[]{:S(2)}) collective-permute-start(f32[264,256]{1,0:T(8,128)S(1)} %collective-permute-done.16), channel_id=1, source_target_pairs={{0,8},{1,25},{2,10},{3,27},{4,12},{5,29},{6,14},{7,31},{8,16},{9,1... | collective-permute-start | bytes 811016 | tf_op jit(solution)/shard_map/ppermute | solution.py:283
  105.6 10.3 %collective-permute-start.20 = (f32[264,256]{1,0:T(8,128)S(1)}, f32[264,256]{1,0:T(8,128)S(1)}, u32[]{:S(2)}, u32[]{:S(2)}) collective-permute-start(f32[264,256]{1,0:T(8,128)S(1)} %collective-permute-done.19), channel_id=1, source_target_pairs={{0,2},{1,7},{2,4},{3,1},{4,6},{5,3},{6,0},{7,5},{8,10},{9,15},{10,... | collective-permute-start | bytes 811016 | tf_op jit(solution)/shard_map/ppermute | solution.py:287
  106.5 9.3 %collective-permute-start.21 = (f32[264,256]{1,0:T(8,128)S(1)}, f32[264,256]{1,0:T(8,128)S(1)}, u32[]{:S(2)}, u32[]{:S(2)}) collective-permute-start(f32[264,256]{1,0:T(8,128)S(1)} %collective-permute-done.16), channel_id=1, source_target_pairs={{0,2},{1,7},{2,4},{3,1},{4,6},{5,3},{6,0},{7,5},{8,10},{9,15},{10,... | collective-permute-start | bytes 811016 | tf_op jit(solution)/shard_map/ppermute | solution.py:287
  115.9 5.7 %collective-permute-start.22 = (f32[2,264,256]{2,1,0:T(8,128)S(1)}, f32[2,264,256]{2,1,0:T(8,128)S(1)}, u32[]{:S(2)}, u32[]{:S(2)}) collective-permute-start(f32[2,264,256]{2,1,0:T(8,128)S(1)} %pad_maximum_fusion), channel_id=1, source_target_pairs={{0,1},{1,0},{2,3},{3,2},{4,5},{5,4},{6,7},{7,6},{8,9},{9,8},{10,11... | collective-permute-start | bytes 1622024 | tf_op jit(solution)/shard_map/ppermute | solution.py:279
  118.3 10.0 %collective-permute-start.24 = (f32[264,256]{1,0:T(8,128)S(1)}, f32[264,256]{1,0:T(8,128)S(1)}, u32[]{:S(2)}, u32[]{:S(2)}) collective-permute-start(f32[264,256]{1,0:T(8,128)S(1)} %collective-permute-done.18), channel_id=1, source_target_pairs={{0,8},{1,25},{2,10},{3,27},{4,12},{5,29},{6,14},{7,31},{8,16},{9,1... | collective-permute-start | bytes 811016 | tf_op jit(solution)/shard_map/ppermute | solution.py:283
  121.6 14.4 %collective-permute-start.23 = (f32[4,264,256]{2,1,0:T(8,128)S(1)}, f32[4,264,256]{2,1,0:T(8,128)S(1)}, u32[]{:S(2)}, u32[]{:S(2)}) collective-permute-start(f32[4,264,256]{2,1,0:T(8,128)S(1)} %constant_dynamic-update-slice_fusion.2.refs_2_), channel_id=1, source_target_pairs={{0,2},{1,7},{2,4},{3,1},{4,6},{5,3},{6,0},{7,5},{8,10},{9,15},{10,... | collective-permute-start | bytes 3244040 | tf_op jit(solution)/shard_map/ppermute | solution.py:287
  128.3 2.2 %collective-permute-start.25 = (f32[264,256]{1,0:T(8,128)S(1)}, f32[264,256]{1,0:T(8,128)S(1)}, u32[]{:S(2)}, u32[]{:S(2)}) collective-permute-start(f32[264,256]{1,0:T(8,128)S(1)} %collective-permute-done.24), channel_id=1, source_target_pairs={{0,1},{1,0},{2,3},{3,2},{4,5},{5,4},{6,7},{7,6},{8,9},{9,8},{10,11... | collective-permute-start | bytes 811016 | tf_op jit(solution)/shard_map/ppermute | solution.py:279
  130.6 11.2 %collective-permute-start.27 = (f32[2,264,256]{2,1,0:T(8,128)S(1)}, f32[2,264,256]{2,1,0:T(8,128)S(1)}, u32[]{:S(2)}, u32[]{:S(2)}) collective-permute-start(f32[2,264,256]{2,1,0:T(8,128)S(1)} %pad_maximum_fusion.1.refs_3_), channel_id=1, source_target_pairs={{0,2},{1,7},{2,4},{3,1},{4,6},{5,3},{6,0},{7,5},{8,10},{9,15},{10,... | collective-permute-start | bytes 1622024 | tf_op jit(solution)/shard_map/ppermute | solution.py:287
  142.4 4.7 %collective-permute-start.29 = (f32[9,136,256]{2,1,0:T(8,128)S(1)}, f32[9,136,256]{2,1,0:T(8,128)S(1)}, u32[]{:S(2)}, u32[]{:S(2)}) collective-permute-start(f32[9,136,256]{2,1,0:T(8,128)S(1)} %pick_for_partner.6), channel_id=1, source_target_pairs={{0,1},{1,0},{2,3},{3,2},{4,5},{5,4},{6,7},{7,6},{8,9},{9,8},{10,11... | collective-permute-start | bytes 3760136 | tf_op jit(solution)/shard_map/ppermute | solution.py:279
  144.6 11.5 %collective-permute-start.26 = (f32[2,264,256]{2,1,0:T(8,128)S(1)}, f32[2,264,256]{2,1,0:T(8,128)S(1)}, u32[]{:S(2)}, u32[]{:S(2)}) collective-permute-start(f32[2,264,256]{2,1,0:T(8,128)S(1)} %slice.14), channel_id=1, source_target_pairs={{0,2},{1,7},{2,4},{3,1},{4,6},{5,3},{6,0},{7,5},{8,10},{9,15},{10,... | collective-permute-start | bytes 1622024 | tf_op jit(solution)/shard_map/ppermute | solution.py:287
  144.8 11.4 %collective-permute-start.28 = (f32[264,256]{1,0:T(8,128)S(1)}, f32[264,256]{1,0:T(8,128)S(1)}, u32[]{:S(2)}, u32[]{:S(2)}) collective-permute-start(f32[264,256]{1,0:T(8,128)S(1)} %slice_bitcast_fusion), channel_id=1, source_target_pairs={{0,2},{1,7},{2,4},{3,1},{4,6},{5,3},{6,0},{7,5},{8,10},{9,15},{10,... | collective-permute-start | bytes 811016 | tf_op jit(solution)/shard_map/ppermute | solution.py:287
  147.2 13.1 %copy-start.2 = (bf16[32,128,256]{2,1,0:T(8,128)(2,1)S(1)}, bf16[32,128,256]{2,1,0:T(8,128)(2,1)}, u32[]{:S(2)}) copy-start(bf16[32,128,256]{2,1,0:T(8,128)(2,1)} %copy-done) | copy-start | bytes 6291460
  156.7 3.6 %collective-permute-start.30 = (f32[3,136,256]{2,1,0:T(8,128)S(1)}, f32[3,136,256]{2,1,0:T(8,128)S(1)}, u32[]{:S(2)}, u32[]{:S(2)}) collective-permute-start(f32[3,136,256]{2,1,0:T(8,128)S(1)} %pick_for_partner.7), channel_id=1, source_target_pairs={{0,1},{1,0},{2,3},{3,2},{4,5},{5,4},{6,7},{7,6},{8,9},{9,8},{10,11... | collective-permute-start | bytes 1253384 | tf_op jit(solution)/shard_map/ppermute | solution.py:279
